TPU v7x, 256 devices: a whole 4x4x8 slice. The times are simulated.
256 devices in a mesh: surf: 32 (over y, z), vol: 8 (over x, core).
Axes of the slice: x: 4, y: 4, z: 8, core: 2. Of those that a mesh axis runs over, the one named last changes fastest.
Arguments:
- centres: float32 [3, 65536], P(None, 'surf'), may hold values from -8 to 40, as said below
- mode_shapes: float32 [16, 65536], P(None, 'surf'), may hold values from -16 to 16
- neighbours: int32 [256, 9], P('surf'), may hold values from -1 to 255, as said below
- volume_nodes: float32 [3, 8388608], P(None, ('surf', 'vol')), may hold values from -8 to 40
- supports: int32 [32768, 9], P(('surf', 'vol')), may hold values from -1 to 255, as said below
Outputs:
- rbf_weights: float32 [16, 65536], P(None, 'surf')
- displacement: float32 [16, 8388608], P(None, ('surf', 'vol'))
Inputs may be any that keep to these rules, and one draw needn't show every extreme that they name: `neighbours`: row b lists block b and every block whose surface cell touches its cell, each once; -1 marks an empty slot. A listed id divided by 8 (rounded down) differs from b divided by 8 by at most one. If c is listed in row b, b is listed in row c. `supports`: row t lists distinct block ids first and -1 after them, at least two ids. A listed id divided by 8 differs from t divided by 1024 (both rounded down) by at most one. Some row lists 9 ids. Tiles of lower index along vol tend to list more ids. `centres`: centres of two blocks that are not listed in each other's rows of neighbours are more than 0.9 apart.
All inputs are finite; a program needn't handle non-finite values.
Results may differ from a plain program's by a relative error of at most 0.012.
Values may be sent and summed in bfloat16 or wider, within the bound.
No kernel may reach another device: no remote copies, remote signals or barrier semaphores. Data moves between devices by JAX's collectives and lax.ppermute only.
A program may use at most 128 MiB of HBM per device.

v0:
```python
import jax
import jax.numpy as jnp
from jax import lax
from jax.sharding import PartitionSpec as P

MODES = 16
BLK = 256
ITERS = 3


support_radius = 0.9
diag_shift = 0.5
highest = lax.Precision.HIGHEST


def extended(shard, sides, width):
    for axis, dim in sides:
        count, length = (lax.axis_size(axis), shard.shape[dim])
        up = [(i, (i + 1) % count) for i in range(count - 1)]
        down = [(j, i) for i, j in up]
        last = lax.slice_in_dim(shard, length - width, length, axis=dim)
        initial = lax.slice_in_dim(shard, 0, width, axis=dim)
        before = lax.ppermute(last, axis, up)
        after = lax.ppermute(initial, axis, down)
        shard = jnp.concatenate([before, shard, after], axis=dim)
    return shard


def wendland(first_pts, second_pts):
    distance = (
        (first_pts[0] - second_pts[0]) ** 2
        + (first_pts[1] - second_pts[1]) ** 2
        + (first_pts[2] - second_pts[2]) ** 2
    )
    scaled = jnp.sqrt(distance) / support_radius
    remain = jnp.maximum(1.0 - scaled, 0.0)
    return remain**4 * (4.0 * scaled + 1.0)


def per_device(centres, mode_shapes, neighbours, volume_nodes, supports):
    blk_dev = neighbours.shape[0]
    slot_count = neighbours.shape[1]
    tile_dev = supports.shape[0]
    rim_width = blk_dev * BLK
    strip_index = lax.axis_index("surf")
    offset_blocks = (strip_index - 1) * blk_dev
    near_centres = extended(centres, (("surf", 1),), rim_width).reshape(3, 3 * blk_dev, BLK)
    own_centres = jnp.transpose(centres.reshape(3, blk_dev, BLK), (1, 0, 2))
    block_places = jnp.clip(neighbours - offset_blocks, 0, 3 * blk_dev - 1)
    block_active = neighbours >= 0

    def build_kernel(inputs):
        own_pts, places, active = inputs
        near_pts = jnp.take(near_centres, places, axis=1)
        return wendland(own_pts[:, None, :, None], near_pts[:, :, None, :]) * active[:, None, None]

    stored_kernels = lax.map(build_kernel, (own_centres, block_places, block_active))

    def squares(vector_field):
        return lax.psum(jnp.sum(vector_field * vector_field, axis=1), "surf")

    solution = jnp.zeros_like(mode_shapes)
    residual = mode_shapes
    direction = mode_shapes
    norm_now = squares(residual)
    for iteration in range(ITERS):
        wide_field = extended(direction, (("surf", 1),), rim_width).reshape(MODES, 3 * blk_dev, BLK)
        values = jnp.take(wide_field, block_places.reshape(-1), axis=1).reshape(
            MODES, blk_dev, slot_count, BLK
        )
        pieces = jnp.einsum("bkij,mbkj->mbi", stored_kernels, values, precision=highest)
        applied = diag_shift * direction + pieces.reshape(MODES, rim_width)
        step_size = norm_now / lax.psum(jnp.sum(direction * applied, axis=1), "surf")
        solution = solution + step_size[:, None] * direction
        residual = residual - step_size[:, None] * applied
        if iteration + 1 < ITERS:
            norm_next = squares(residual)
            direction = residual + (norm_next / norm_now)[:, None] * direction
            norm_now = norm_next
    weights_low = solution.astype(jnp.bfloat16)
    wide_weights = extended(weights_low, (("surf", 1),), rim_width).reshape(MODES, 3 * blk_dev, BLK)

    def contribution(points, block_ids, active):
        places = jnp.clip(block_ids - offset_blocks, 0, 3 * blk_dev - 1)
        sources = jnp.take(near_centres, places, axis=1)
        weights = jnp.take(wide_weights, places, axis=1)
        kernel = (
            wendland(points[:, :, :, None], sources[:, :, None, :]) * active[:, None, None]
        ).astype(jnp.bfloat16)
        return jnp.einsum("gnj,mgj->mgn", kernel, weights, preferred_element_type=jnp.float32)

    tile_pts = volume_nodes.reshape(3, tile_dev, BLK)
    longest = jnp.max(jnp.sum((supports >= 0).astype(jnp.int32), axis=1))

    def add_slot(slot_index, running):
        block_ids = lax.dynamic_index_in_dim(supports, slot_index, 1, keepdims=False)
        return running + contribution(tile_pts, block_ids, block_ids >= 0)

    moved = lax.fori_loop(0, longest, add_slot, jnp.zeros((MODES, tile_dev, BLK), jnp.float32))
    moved = moved.reshape(MODES, tile_dev * BLK)
    power = lax.psum(jnp.sum(moved * moved, axis=1), ("surf", "vol"))
    node_total = moved.shape[1] * lax.axis_size("surf") * lax.axis_size("vol")
    scale = jnp.sqrt(power / node_total + 1e-06)
    return (solution, moved / scale[:, None])


def solution(mesh):
    return jax.shard_map(
        per_device,
        mesh=mesh,
        in_specs=(
            P(None, "surf"),
            P(None, "surf"),
            P("surf", None),
            P(None, ("surf", "vol")),
            P(("surf", "vol"), None),
        ),
        out_specs=(P(None, "surf"), P(None, ("surf", "vol"))),
        check_vma=False,
    )
```

profile of v0, /device:TPU:1, one launch (start us, length us, event | category | flops | bytes accessed | tf_op | source)
XLA Modules:
  0.0 927.7 jit_solution(9666142806893374920)
XLA Ops:
  0.6 4.4 collective-permute-start
  6.3 4.2 collective-permute-start.2
  16.4 39.3 %while.24 = (s32[]{:T(128)}, f32[8,9,256,256]{3,2,1,0:T(8,128)}, f32[8,3,256]{2,1,0:T(4,128)}, s32[8,9]{1,0:T(8,128)S(1)}, f32[3,24,256]{2,0,1:T(4,128)S(1)}, /*...) while((s32[]{:T(128)}, f32[8,9,256,256]{3,2,1,0:T(8,128)}, f32[8,3,256]{2,1,0:T(4,128)}, ...), condition=%wide.region_3.5_spmd, body=%wide.region_2.4_spmd.sunk | while | flops 10035038 | bytes 2622380 | solution.py:57
  27.7 3.4 multiply_dynamic-update-slice_fusion.2
  32.7 3.4 multiply_dynamic-update-slice_fusion.2
  42.5 3.4 multiply_dynamic-update-slice_fusion.2
  52.3 3.3 multiply_dynamic-update-slice_fusion.2
  56.6 18.4 %convolution_bitcast_fusion.2 = f32[8,2,8,256]{3,2,1,0:T(8,128)S(1)} fusion(f32[16,8,9,256]{3,0,2,1:T(8,128)S(1)} %bitcast.148, f32[8,9,256,256]{3,2,1,0:T(8,128)} %get-tuple-element.184), kind=kOutput, calls=%fused_computation.50 | convolution fusion | flops 905969664 | bytes 20185088 | tf_op jit(solution)/shard_map/bkij,mbkj->mbi/dot_general | solution.py:71
  75.2 61.9 %all-reduce = (f32[16]{0:T(128)S(1)}, f32[16]{0:T(128)S(1)}) all-reduce(f32[16]{0:T(128)S(1)} %get-tuple-element.206, f32[16]{0:T(128)S(1)} %get-tuple-element.205), channel_id=1, replica_groups=mesh['surf'=32,'vol'=8] {'surf'}, use_global_device_ids=true, to_apply=%region_1.2 | all-reduce | flops 32 | bytes 256 | tf_op jit(solution)/shard_map/psum | solution.py:60
  137.3 55.7 %psum.51 = f32[16]{0:T(128)S(1)} all-reduce(f32[16]{0:T(128)S(1)} %get-tuple-element.241), channel_id=1, replica_groups=mesh['surf'=32,'vol'=8] {'surf'}, use_global_device_ids=true, to_apply=%region_7.9 | all-reduce | flops 16 | bytes 128 | tf_op jit(solution)/shard_map/psum | solution.py:60
  193.1 3.5 collective-permute-start.4
  198.6 4.1 collective-permute-done.5
  203.6 18.4 %convolution_bitcast_fusion.1 = f32[8,2,8,256]{3,2,1,0:T(8,128)S(1)} fusion(f32[16,8,9,256]{3,0,2,1:T(8,128)S(1)} %bitcast.149, f32[8,9,256,256]{3,2,1,0:T(8,128)} %get-tuple-element.184), kind=kOutput, calls=%fused_computation.49 | convolution fusion | flops 905969664 | bytes 20185088 | tf_op jit(solution)/shard_map/bkij,mbkj->mbi/dot_general | solution.py:71
  222.2 55.7 %psum.52 = f32[16]{0:T(128)S(1)} all-reduce(f32[16]{0:T(128)S(1)} %multiply_reduce_fusion.3), channel_id=1, replica_groups=mesh['surf'=32,'vol'=8] {'surf'}, use_global_device_ids=true, to_apply=%region_9.11 | all-reduce | flops 16 | bytes 128 | tf_op jit(solution)/shard_map/psum | solution.py:73
  278.1 57.4 %psum.53 = f32[16]{0:T(128)S(1)} all-reduce(f32[16]{0:T(128)S(1)} %multiply_reduce_fusion.2), channel_id=1, replica_groups=mesh['surf'=32,'vol'=8] {'surf'}, use_global_device_ids=true, to_apply=%region_11.13 | all-reduce | flops 16 | bytes 128 | tf_op jit(solution)/shard_map/psum | solution.py:60
  339.4 3.9 collective-permute-done.7
  344.3 18.4 %convolution_bitcast_fusion = f32[8,2,8,256]{3,2,1,0:T(8,128)S(1)} fusion(f32[16,8,9,256]{3,0,2,1:T(8,128)S(1)} %bitcast.147, f32[8,9,256,256]{3,2,1,0:T(8,128)} %get-tuple-element.184), kind=kOutput, calls=%fused_computation.48 | convolution fusion | flops 905969664 | bytes 20185088 | tf_op jit(solution)/shard_map/bkij,mbkj->mbi/dot_general | solution.py:71
  362.9 55.9 %psum.54 = f32[16]{0:T(128)S(1)} all-reduce(f32[16]{0:T(128)S(1)} %multiply_reduce_fusion.1), channel_id=1, replica_groups=mesh['surf'=32,'vol'=8] {'surf'}, use_global_device_ids=true, to_apply=%region_13.15 | all-reduce | flops 16 | bytes 128 | tf_op jit(solution)/shard_map/psum | solution.py:73
  429.6 155.5 %while.25 = (s32[]{:T(128)}, f32[16,128,256]{2,0,1:T(8,128)}, s32[]{:T(128)}, s32[128,9]{0,1:T(8,128)S(1)}, s32[]{:T(128)}, /*index=5*/bf16[16,24,256]{2,0,1:T(8...) while((s32[]{:T(128)}, f32[16,128,256]{2,0,1:T(8,128)}, ...), condition=%wide.region_17.19_spmd, body=%wide.region_16.18_spmd.sunk | while | flops 420579584 | bytes 14950423 | solution.py:99
  434.0 34.5 %bitcast_add_fusion.2 = f32[16,128,256]{2,0,1:T(8,128)} fusion(f32[16,128,256]{2,0,1:T(8,128)} %get-tuple-element.424, f32[128]{0:T(128)S(1)} %get-tuple-element.371, f32[128,256]{1,0:T(8,128)S(1)} %get-tuple-element.376, f32[128,256]{1,0:T(8,128)S(1)} %sub.382, f32[128,256]{1,0:T(8,128)S(1)} %get-tuple-element.378, f32[128,256]{1,0:T(8,128)S(1)} %sub.383, ...), kind=kOutput, calls=%fused_computation.24.clone.3 | convolution fusion | flops 419954688 | bytes 6029824 | tf_op jit(solution)/shard_map/while/body/gnj,mgj->mgn/dot_general | solution.py:90
  472.7 34.5 %bitcast_add_fusion.2 = f32[16,128,256]{2,0,1:T(8,128)} fusion(f32[16,128,256]{2,0,1:T(8,128)} %get-tuple-element.424, f32[128]{0:T(128)S(1)} %get-tuple-element.371, f32[128,256]{1,0:T(8,128)S(1)} %get-tuple-element.376, f32[128,256]{1,0:T(8,128)S(1)} %sub.382, f32[128,256]{1,0:T(8,128)S(1)} %get-tuple-element.378, f32[128,256]{1,0:T(8,128)S(1)} %sub.383, ...), kind=kOutput, calls=%fused_computation.24.clone.3 | convolution fusion | flops 419954688 | bytes 6029824 | tf_op jit(solution)/shard_map/while/body/gnj,mgj->mgn/dot_general | solution.py:90
  511.4 34.5 %bitcast_add_fusion.2 = f32[16,128,256]{2,0,1:T(8,128)} fusion(f32[16,128,256]{2,0,1:T(8,128)} %get-tuple-element.424, f32[128]{0:T(128)S(1)} %get-tuple-element.371, f32[128,256]{1,0:T(8,128)S(1)} %get-tuple-element.376, f32[128,256]{1,0:T(8,128)S(1)} %sub.382, f32[128,256]{1,0:T(8,128)S(1)} %get-tuple-element.378, f32[128,256]{1,0:T(8,128)S(1)} %sub.383, ...), kind=kOutput, calls=%fused_computation.24.clone.3 | convolution fusion | flops 419954688 | bytes 6029824 | tf_op jit(solution)/shard_map/while/body/gnj,mgj->mgn/dot_general | solution.py:90
  550.0 34.5 %bitcast_add_fusion.2 = f32[16,128,256]{2,0,1:T(8,128)} fusion(f32[16,128,256]{2,0,1:T(8,128)} %get-tuple-element.424, f32[128]{0:T(128)S(1)} %get-tuple-element.371, f32[128,256]{1,0:T(8,128)S(1)} %get-tuple-element.376, f32[128,256]{1,0:T(8,128)S(1)} %sub.382, f32[128,256]{1,0:T(8,128)S(1)} %get-tuple-element.378, f32[128,256]{1,0:T(8,128)S(1)} %sub.383, ...), kind=kOutput, calls=%fused_computation.24.clone.3 | convolution fusion | flops 419954688 | bytes 6029824 | tf_op jit(solution)/shard_map/while/body/gnj,mgj->mgn/dot_general | solution.py:90
  587.5 338.6 %psum.55 = f32[16]{0:T(128)S(1)} all-reduce(f32[16]{0:T(128)S(1)} %multiply_reduce_fusion), channel_id=1, replica_groups=mesh['surf'=32,'vol'=8] {'surf','vol'}, use_global_device_ids=true, to_apply=%region_19.21 | all-reduce | flops 16 | bytes 128 | tf_op jit(solution)/shard_map/psum | solution.py:101
  (204 shorter events, 70.4 us)
Async XLA Ops:
  0.6 55.1 %collective-permute-start = (f32[16,2048]{1,0:T(8,128)}, f32[16,2048]{1,0:T(8,128)S(1)}, u32[]{:S(2)}, u32[]{:S(2)}) collective-permute-start(f32[16,2048]{1,0:T(8,128)} %param.12), channel_id=1, source_target_pairs={{0,8},{8,16},{16,24},{24,32},{32,40},{40,48},{48,56},{56,64},{64,7... | collective-permute-start | bytes 393224 | tf_op jit(solution)/shard_map/ppermute | solution.py:23
  5.0 50.7 %collective-permute-start.1 = (f32[16,2048]{1,0:T(8,128)}, f32[16,2048]{1,0:T(8,128)S(1)}, u32[]{:S(2)}, u32[]{:S(2)}) collective-permute-start(f32[16,2048]{1,0:T(8,128)} %param.12), channel_id=1, source_target_pairs={{8,0},{16,8},{24,16},{32,24},{40,32},{48,40},{56,48},{64,56},{72,6... | collective-permute-start | bytes 393224 | tf_op jit(solution)/shard_map/ppermute | solution.py:24
  6.3 7.0 collective-permute-start.2
  10.5 5.1 collective-permute-start.3
  16.3 39.3 %copy-start.2 = (f32[16,2048]{1,0:T(8,128)S(1)}, f32[16,2048]{1,0:T(8,128)}, u32[]{:S(2)}) copy-start(f32[16,2048]{1,0:T(8,128)} %param.12) | copy-start | bytes 393220
  193.1 5.4 collective-permute-start.4
  196.6 6.1 collective-permute-start.5
  335.6 3.8 collective-permute-start.6
  337.5 5.9 collective-permute-start.7
  344.3 79.7 %copy-start.3 = (s32[128,9]{0,1:T(8,128)S(1)}, s32[128,9]{0,1:T(8,128)}, u32[]{:S(2)}) copy-start(s32[128,9]{0,1:T(8,128)} %param.15) | copy-start | bytes 13828
  362.7 66.9 %copy-start.1 = (f32[3,32768]{1,0:T(4,128)S(1)}, f32[3,32768]{1,0:T(4,128)}, u32[]{:S(2)}) copy-start(f32[3,32768]{1,0:T(4,128)} %param.14) | copy-start | bytes 1179652
  419.5 5.2 collective-permute-start.8
  422.7 5.3 collective-permute-start.9
  585.2 2.2 copy-start
where the time goes:
time: 929 us; the launch traced here: 928 us
  blocking collectives  625 us (67%)
  matrix products  193 us (21%)
  other arithmetic  38.3 us (4%)
  local copies, waits for them, and re-layouts  27.3 us (3%)
  starting transfers between devices  23.8 us (3%)
  waiting for transfers between devices  14.7 us (2%)
    psum x1, blocking collectives, per_device(): power = lax.psum(jnp.sum(moved * moved, axis=1), ('surf', 'vol'))  339 us
    psum x3, blocking collectives, squares(): return lax.psum(jnp.sum(vector_field * vector_field, axis=1), 'surf')  175 us
    dot_general x4, matrix products, contribution(): jnp.einsum('gnj,mgj->mgn', kernel, weights, preferred_element_type=jnp.fl...  138 us
    psum x2, blocking collectives, per_device(): lax.psum(jnp.sum(direction * applied, axis=1), 'surf')  112 us
    dot_general x3, matrix products, per_device(): jnp.einsum('bkij,mbkj->mbi', stored_kernels, values, precision=highest)  55.3 us
    dynamic_update_slice x8, other arithmetic, per_device(): lax.map(build_kernel, (own_centres, block_places, block_active))  26.7 us
  transfers between devices with their start and end apart: 10, of which 6 were waited for; matrix products, arithmetic and copies ran while one was open for 5% of the time, Pallas kernels for 0%

commit v1 on v0

v1 whole, which is shorter than its diff:
```python
import functools

import jax
import jax.numpy as jnp
from jax import lax
from jax.experimental import pallas as pl
from jax.experimental.pallas import tpu as pltpu
from jax.sharding import PartitionSpec as P

MODES = 16
BLK = 256
RADIUS = 0.9
SHIFT = 0.5
DEPTH = 48
KRYLOV = 3
LANES = 128
f32 = jnp.float32
bf16 = jnp.bfloat16


def whole(memory):
    return pl.BlockSpec(memory_space=memory)


def split3(x):
    first = x.astype(bf16).astype(f32)
    rest = x - first
    second = rest.astype(bf16).astype(f32)
    return first, second, rest - second


def augmented(points, is_node):
    count = points.shape[1]
    row = lax.broadcasted_iota(jnp.int32, (8, count), 0)
    square = jnp.sum(points * points, axis=0, keepdims=True)
    one = jnp.ones_like(square)
    if is_node:
        coords, low, high = points, square, one
    else:
        coords, low, high = -2.0 * points, one, square
    zeros = jnp.zeros((5, count), f32)
    padded = jnp.concatenate([coords, zeros], axis=0)
    return jnp.where(row == 3, low, jnp.where(row == 4, high, padded))


def node_kernel(steps, centres_ref, nodes_ref, out_ref):
    step = pl.program_id(0)
    origin = centres_ref[:, 0:1]

    def fill(points):
        a, b, c = split3(augmented((points - origin) * (1.0 / RADIUS), True))
        rows = jnp.concatenate([a, b, a, b, c, a], axis=0)
        for t in range(out_ref.shape[0]):
            out_ref[t] = jnp.transpose(rows[:, t * BLK : (t + 1) * BLK]).astype(bf16)

    @pl.when(step < steps - 1)
    def _():
        fill(nodes_ref[...])

    @pl.when(step == steps - 1)
    def _():
        fill(centres_ref[...])


def prepare_nodes(centres, nodes):
    width = centres.shape[1]
    per_step = width // BLK
    node_steps = nodes.shape[1] // width
    steps = node_steps + 1
    return pl.pallas_call(
        functools.partial(node_kernel, steps),
        grid=(steps,),
        in_specs=[
            pl.BlockSpec((3, width), lambda i: (0, 0)),
            pl.BlockSpec((3, width), lambda i: (0, jnp.minimum(i, node_steps - 1))),
        ],
        out_specs=pl.BlockSpec((per_step, BLK, DEPTH), lambda i: (i, 0, 0)),
        out_shape=jax.ShapeDtypeStruct((steps * per_step, BLK, DEPTH), bf16),
        name="prepare_nodes",
    )(centres, nodes)


def centre_kernel(before_ref, own_ref, after_ref, out_ref):
    per = own_ref.shape[1] // BLK
    origin = own_ref[:, 0:1]
    for k, ref in enumerate((before_ref, own_ref, after_ref)):
        points = (ref[0:3, :] - origin[0:3]) * (1.0 / RADIUS)
        a, b, c = split3(augmented(points, False))
        rows = jnp.concatenate([a, a, b, b, a, c], axis=0)
        for t in range(per):
            out_ref[k * per + t] = rows[:, t * BLK : (t + 1) * BLK].astype(bf16)


def prepare_centres(before, own, after):
    per = own.shape[1] // BLK
    return pl.pallas_call(
        centre_kernel,
        in_specs=[whole(pltpu.VMEM)] * 3,
        out_specs=whole(pltpu.VMEM),
        out_shape=jax.ShapeDtypeStruct((3 * per, DEPTH, BLK), bf16),
        name="prepare_centres",
    )(before, own, after)


def phi(square):
    bounded = jnp.maximum(square, 1e-12)
    scaled = bounded * lax.rsqrt(bounded)
    remain = jnp.maximum(1.0 - scaled, 0.0)
    squared = remain * remain
    return (squared * squared * (scaled + 0.25)).astype(bf16)


def accumulate(
    unroll, together, tiles, group_count, places, members, left_ref, right_ref, weight_ref, total
):
    def clear(t, carry):
        total[t] = jnp.zeros((BLK, LANES), f32)
        return carry

    lax.fori_loop(0, tiles + 1, clear, 0)

    def step(g, carry):
        for h in range(unroll):
            group = g * unroll + h
            place = places[group]
            ids = [members[group * together + j] for j in range(together)]
            left = jnp.concatenate([left_ref[jnp.minimum(t, tiles - 1)] for t in ids], axis=0)
            square = jnp.dot(left, right_ref[place], preferred_element_type=f32)
            image = jnp.dot(phi(square), weight_ref[place], preferred_element_type=f32)
            for j, t in enumerate(ids):
                total[t] += image[j * BLK : (j + 1) * BLK]
        return carry

    lax.fori_loop(0, group_count, step, 0)


def fill_weights(weight_ref, fields, per):
    width = 2 * MODES * len(fields[0])
    for k, refs in enumerate(fields):
        stack = jnp.concatenate([r[...].astype(f32) for r in refs], axis=0) * 4.0
        high = stack.astype(bf16).astype(f32)
        low = stack - high
        rows = jnp.concatenate(
            [high, low, jnp.zeros((LANES - width, stack.shape[1]), f32)], axis=0
        )
        for t in range(per):
            weight_ref[k * per + t] = jnp.transpose(rows[:, t * BLK : (t + 1) * BLK]).astype(bf16)


def operator_kernel(
    unroll, together, tiles, count_ref, place_ref, member_ref, left_ref, right_ref,
    before_ref, own_ref, after_ref, out_ref, weight_ref, total,
):
    fill_weights(weight_ref, ((before_ref,), (own_ref,), (after_ref,)), tiles)
    accumulate(
        unroll, together, tiles, count_ref[0], place_ref, member_ref, left_ref, right_ref,
        weight_ref, total,
    )
    for t in range(tiles):
        image = jnp.transpose(total[t])
        sl = slice(t * BLK, (t + 1) * BLK)
        out_ref[:, sl] = image[0:MODES] + image[MODES : 2 * MODES] + SHIFT * own_ref[:, sl]


def apply_operator(unroll, together, lists, left, right, before, own, after):
    tiles = own.shape[1] // BLK
    last = left.shape[0] // tiles - 1
    vmem, smem = whole(pltpu.VMEM), whole(pltpu.SMEM)
    return pl.pallas_call(
        functools.partial(operator_kernel, unroll, together, tiles),
        grid=(1,),
        in_specs=[smem] * 3
        + [pl.BlockSpec((tiles, BLK, DEPTH), lambda i: (last, 0, 0))]
        + [vmem] * 4,
        out_specs=vmem,
        out_shape=jax.ShapeDtypeStruct(own.shape, f32),
        scratch_shapes=[
            pltpu.VMEM((3 * tiles, BLK, LANES), bf16),
            pltpu.VMEM((tiles + 1, BLK, LANES), f32),
        ],
        compiler_params=pltpu.CompilerParams(vmem_limit_bytes=40 * 2**20),
        name="operator",
    )(*lists, left, right, before, own, after)


def row_of(columns):
    mode = lax.broadcasted_iota(jnp.int32, (MODES, BLK), 0)
    lane = lax.broadcasted_iota(jnp.int32, (MODES, BLK), 1)
    spread = jnp.zeros((MODES, BLK), f32)
    for q, column in enumerate(columns):
        spread = jnp.where(lane == q * MODES + mode, column, spread)
    return jnp.sum(spread, axis=0, keepdims=True)


def columns_of(row, count):
    mode = lax.broadcasted_iota(jnp.int32, (MODES, BLK), 0)
    lane = lax.broadcasted_iota(jnp.int32, (MODES, BLK), 1)
    return [
        jnp.sum(jnp.where(lane == q * MODES + mode, row, 0.0), axis=1, keepdims=True)
        for q in range(count)
    ]


PAIRS = ((0, 0), (0, 1), (1, 1), (1, 2), (2, 2), (0, 2))


def volume_kernel(
    unroll, together, tiles, own_tiles, share, count_ref, place_ref, member_ref, left_ref, right_ref,
    *refs,
):
    fields = (refs[0:3], refs[3:6], refs[6:9])
    out_ref, sums_ref, weight_ref, total = refs[9:]
    fill_weights(weight_ref, fields, own_tiles)
    accumulate(
        unroll, together, tiles, count_ref[0], place_ref, member_ref, left_ref, right_ref,
        weight_ref, total,
    )
    wide = KRYLOV * MODES

    def finish(g, gram):
        for h in range(4):
            t = g * 4 + h
            image = jnp.transpose(total[t])
            image = image[0:wide] + image[wide : 2 * wide]
            out_ref[:, pl.ds(pl.multiple_of(t * BLK, BLK), BLK)] = image
            parts = [image[k * MODES : (k + 1) * MODES] for k in range(KRYLOV)]
            gram = tuple(s + parts[i] * parts[j] for s, (i, j) in zip(gram, PAIRS))
        return gram

    node_tiles = tiles - own_tiles
    gram = lax.fori_loop(
        0, node_tiles // 4, finish, tuple(jnp.zeros((MODES, BLK), f32) for _ in PAIRS)
    )
    columns = [jnp.sum(s, axis=1, keepdims=True) for s in gram]
    own = [r[...] for r in fields[1]]
    moments = [own[0] * own[0], own[0] * own[1], own[1] * own[1], own[1] * own[2], own[2] * own[2]]
    columns += [share * jnp.sum(s, axis=1, keepdims=True) for s in moments]
    last = jnp.zeros((MODES, BLK), f32)
    for b in range(own_tiles):
        image = jnp.transpose(total[node_tiles + b])
        piece = own[2][:, b * BLK : (b + 1) * BLK]
        low = 2 * MODES
        image = image[low : low + MODES] + image[wide + low : wide + low + MODES]
        last = last + piece * (image + SHIFT * piece)
    columns.append(share * jnp.sum(last, axis=1, keepdims=True))
    sums_ref[...] = jnp.broadcast_to(row_of(columns), sums_ref.shape)


def volume_images(unroll, together, lists, left, right, fields, devices, share):
    own_tiles = fields[1][0].shape[1] // BLK
    tiles = left.shape[0]
    nodes = (tiles - own_tiles) * BLK
    vmem, smem = whole(pltpu.VMEM), whole(pltpu.SMEM)
    return pl.pallas_call(
        functools.partial(volume_kernel, unroll, together, tiles, own_tiles, share),
        in_specs=[smem] * 3 + [vmem] * 11,
        out_specs=(vmem, vmem),
        out_shape=(
            jax.ShapeDtypeStruct((KRYLOV * MODES, nodes), f32),
            jax.ShapeDtypeStruct((devices, BLK), f32),
        ),
        scratch_shapes=[
            pltpu.VMEM((3 * own_tiles, BLK, LANES), bf16),
            pltpu.VMEM((tiles + 1, BLK, LANES), f32),
        ],
        compiler_params=pltpu.CompilerParams(vmem_limit_bytes=58 * 2**20),
        name="volume",
    )(*lists, left, right, *[f for side in fields for f in side])


def coefficients(row, total_nodes):
    columns = columns_of(row, 2 * len(PAIRS))
    gram, mu = columns[:6], columns[6:]
    zero = jnp.zeros_like(mu[0])
    one = jnp.ones_like(mu[0])

    def pairing(a, b, extra):
        out = zero
        for i, x in enumerate(a):
            for j, y in enumerate(b):
                out = out + x * y * mu[i + j + extra]
        return out

    residual, direction = [one], [one]
    answer = [zero, zero, zero]
    norm = mu[0]
    for iteration in range(KRYLOV):
        size = norm / pairing(direction, direction, 1)
        for i, x in enumerate(direction):
            answer[i] = answer[i] + size * x
        if iteration + 1 < KRYLOV:
            grown = residual + [zero]
            for i, x in enumerate(direction):
                grown[i + 1] = grown[i + 1] - size * x
            residual = grown
            later = pairing(residual, residual, 0)
            ratio = later / norm
            longer = direction + [zero]
            direction = [r + ratio * d for r, d in zip(residual, longer)]
            norm = later
    power = zero
    for s, (i, j) in zip(gram, PAIRS):
        power = power + (1.0 if i == j else 2.0) * s * answer[i] * answer[j]
    scale = jnp.sqrt(jnp.maximum(power, 0.0) / total_nodes + 1e-06)
    return answer, [a / scale for a in answer]


def combine_kernel(total_nodes, sums_ref, v0_ref, v1_ref, v2_ref, image_ref, weights_ref, out_ref, coef):
    @pl.when(pl.program_id(0) == 0)
    def _():
        row = jnp.sum(sums_ref[...], axis=0, keepdims=True)
        answer, scaled = coefficients(row, total_nodes)
        weights_ref[...] = answer[0] * v0_ref[...] + answer[1] * v1_ref[...] + answer[2] * v2_ref[...]
        for k, column in enumerate(scaled):
            coef[k] = jnp.broadcast_to(column, (MODES, LANES))

    c = [coef[k][:, 0:1] for k in range(KRYLOV)]
    out_ref[...] = (
        c[0] * image_ref[0:MODES]
        + c[1] * image_ref[MODES : 2 * MODES]
        + c[2] * image_ref[2 * MODES : 3 * MODES]
    )


def combine(sums, vectors, images, total_nodes):
    nodes = images.shape[1]
    width = 8192 if nodes % 8192 == 0 else nodes
    fixed = lambda i: (0, 0)
    moving = lambda i: (0, i)
    small = pl.BlockSpec(vectors[0].shape, fixed)
    return pl.pallas_call(
        functools.partial(combine_kernel, total_nodes),
        grid=(nodes // width,),
        in_specs=[pl.BlockSpec(sums.shape, fixed), small, small, small]
        + [pl.BlockSpec((KRYLOV * MODES, width), moving)],
        out_specs=(small, pl.BlockSpec((MODES, width), moving)),
        out_shape=(
            jax.ShapeDtypeStruct(vectors[0].shape, f32),
            jax.ShapeDtypeStruct((MODES, nodes), f32),
        ),
        scratch_shapes=[pltpu.VMEM((KRYLOV, MODES, LANES), f32)],
        name="combine",
    )(sums, *vectors, images)


def work_list(places, together, unroll, kinds):
    rows, slots = places.shape
    limit = -(-(rows * slots + kinds * (together - 1)) // together)
    limit = -(-limit // unroll) * unroll
    kind = jnp.arange(kinds, dtype=jnp.int32)
    present = jnp.any(places[:, :, None] == kind, axis=1).astype(f32)
    lower = (jnp.arange(rows)[:, None] >= jnp.arange(rows)[None, :]).astype(f32)
    reach = jnp.dot(lower, present, preferred_element_type=f32)
    groups = jnp.ceil(reach[-1] / together)
    before = (jnp.arange(kinds)[:, None] < jnp.arange(kinds)[None, :]).astype(f32)
    start = jnp.sum(before * groups[:, None], axis=0)
    end = start + groups
    index = jnp.arange(limit, dtype=jnp.int32).astype(f32)
    chosen = (index[:, None] >= start[None, :]) & (index[:, None] < end[None, :])
    place = jnp.sum(jnp.where(chosen, kind[None, :], 0), axis=1)
    first = together * (index - jnp.sum(jnp.where(chosen, start[None, :], 0.0), axis=1))
    reached = jnp.dot(chosen.astype(f32), reach.T, preferred_element_type=f32)
    rank = first[:, None] + jnp.arange(together).astype(f32)[None, :]
    member = jnp.sum((reached[:, None, :] <= rank[:, :, None]).astype(jnp.int32), axis=2)
    count = jnp.ceil(jnp.sum(groups) / unroll).astype(jnp.int32).reshape(1)
    return count, place.astype(jnp.int32), member.reshape(-1)


def halves(shard, axis):
    count = lax.axis_size(axis)
    up = [(i, i + 1) for i in range(count - 1)]
    down = [(i + 1, i) for i in range(count - 1)]
    return lax.ppermute(shard, axis, up), lax.ppermute(shard, axis, down)


def per_device(centres, mode_shapes, neighbours, volume_nodes, supports):
    blk_dev = neighbours.shape[0]
    kinds = 3 * blk_dev
    offset = (lax.axis_index("surf") - 1) * blk_dev
    devices = lax.axis_size("surf") * lax.axis_size("vol")
    share = 1.0 / lax.axis_size("vol")
    total_nodes = volume_nodes.shape[1] * devices

    packed = jnp.concatenate([centres, jnp.zeros((5, centres.shape[1]), f32), mode_shapes], axis=0)
    before, after = halves(packed, "surf")

    def place_of(ids):
        return jnp.where(ids >= 0, jnp.clip(ids - offset, 0, kinds - 1), -1)

    own_places = place_of(neighbours)
    left = prepare_nodes(centres, volume_nodes)
    own_list = work_list(own_places, 3, 4, kinds)
    whole_list = work_list(jnp.concatenate([place_of(supports), own_places]), 4, 4, kinds)

    right = prepare_centres(before, packed, after)
    v0 = mode_shapes
    v0_before, v0_after = before[8:], after[8:]
    v1 = apply_operator(4, 3, own_list, left, right, v0_before, v0, v0_after)
    v1_before, v1_after = halves(v1, "surf")
    v2 = apply_operator(4, 3, own_list, left, right, v1_before, v1, v1_after)
    v2_before, v2_after = halves(v2, "surf")
    fields = (
        (v0_before, v1_before, v2_before),
        (v0, v1, v2),
        (v0_after, v1_after, v2_after),
    )
    images, sums = volume_images(4, 4, whole_list, left, right, fields, devices, share)
    sums = lax.all_to_all(sums, ("surf", "vol"), 0, 0, tiled=True)
    return combine(sums, (v0, v1, v2), images, total_nodes)


def solution(mesh):
    return jax.shard_map(
        per_device,
        mesh=mesh,
        in_specs=(
            P(None, "surf"),
            P(None, "surf"),
            P("surf", None),
            P(None, ("surf", "vol")),
            P(("surf", "vol"), None),
        ),
        out_specs=(P(None, "surf"), P(None, ("surf", "vol"))),
        check_vma=False,
    )
```

time: 929 us -> 253 us (0.27)
  blocking collectives: 625 us -> 112 us
  matrix products: 193 us -> 0.69 us
  Pallas kernels: 0 us -> 96.8 us
  other arithmetic: 38.3 us -> 4.81 us
  local copies, waits for them, and re-layouts: 27.3 us -> 10 us
  waiting for transfers between devices: 14.7 us -> 1.86 us
    psum x6 -> x0, blocking collectives: 625 us -> none  [the longest x1 339 us: per_device(): power = lax.psum(jnp.sum(moved * moved, axis=1), ('surf', 'vol'))]
    dot_general x7 -> x4, matrix products: 193 us -> 0.69 us  [the longest x2 0.43 us: work_list(): reached = jnp.dot(chosen.astype(f32), reach.T, preferred_element_type=f32)]
    all_to_all x0 -> x1, blocking collectives: none -> 112 us  [per_device(): sums = lax.all_to_all(sums, ('surf', 'vol'), 0, 0, tiled=True)]
    pallas_call x0 -> x6, Pallas kernels: none -> 96.8 us  [the longest x1 63.8 us: volume_images(): pl.pallas_call(functools.partial(volume_kernel, unroll, together, tiles,...]
    dynamic_update_slice x8 -> x0, other arithmetic: 26.7 us -> none  [per_device(): lax.map(build_kernel, (own_centres, block_places, block_active))]
    ppermute x10 -> x6, waiting for transfers between devices: 14.7 us -> 1.86 us  [halves(): return (lax.ppermute(shard, axis, up), lax.ppermute(shard, axis, down))]
    gather x19 -> x0, local copies, waits for them, and re-layouts: 12.7 us -> none  [the longest x8 4.61 us: build_kernel(): near_pts = jnp.take(near_centres, places, axis=1)]
    slice x24 -> x2, local copies, waits for them, and re-layouts: 11.8 us -> 0.02 us  [per_device(): v0_before, v0_after = (before[8:], after[8:])]
  transfers between devices with their start and end apart: 10 -> 6, of which waited for: 6 -> 2; matrix products, arithmetic and copies ran while one was open for 5% -> 3% of each run, Pallas kernels for 0% -> 5%
where the time goes in v1:
time: 253 us; the launch traced here: 252 us
  blocking collectives  112 us (44%)
  Pallas kernels  96.8 us (38%)
  starting transfers between devices  22.9 us (9%)
  local copies, waits for them, and re-layouts  10 us (4%)
  other arithmetic  4.81 us (2%)
    all_to_all x1, blocking collectives, per_device(): sums = lax.all_to_all(sums, ('surf', 'vol'), 0, 0, tiled=True)  112 us
    pallas_call x1, Pallas kernels, volume_images(): pl.pallas_call(functools.partial(volume_kernel, unroll, together, tiles,...  63.8 us
    ppermute x6, starting transfers between devices, halves(): return (lax.ppermute(shard, axis, up), lax.ppermute(shard, axis, down))  22.9 us
    pallas_call x2, Pallas kernels, apply_operator(): pl.pallas_call(functools.partial(operator_kernel, unroll, together, tiles...  13.7 us
    pallas_call x1, Pallas kernels, prepare_nodes(): pl.pallas_call(functools.partial(node_kernel, steps), grid=(steps,), in_s...  11.7 us
    unnamed x30, local copies, waits for them, and re-layouts  7.52 us
    pallas_call x1, Pallas kernels, combine(): pl.pallas_call(functools.partial(combine_kernel, total_nodes), grid=(node...  5.41 us
  transfers between devices with their start and end apart: 6, of which 2 were waited for; matrix products, arithmetic and copies ran while one was open for 3% of the time, Pallas kernels for 5%

profile of v1, /device:TPU:1, one launch (start us, length us, event | category | flops | bytes accessed | tf_op | source)
XLA Modules:
  0.0 251.7 jit_solution(9617588390649442634)
XLA Ops:
  0.7 1.0 pad_maximum_fusion.own_ref
  1.7 1.3 collective-permute-start.1
  3.0 5.0 %collective-permute-start = (f32[24,2048]{1,0:T(8,128)S(1)}, f32[24,2048]{1,0:T(8,128)S(1)}, u32[]{:S(2)}, u32[]{:S(2)}) collective-permute-start(f32[24,2048]{1,0:T(8,128)S(1)} %pad_maximum_fusion.own_ref), channel_id=1, source_target_pairs={{0,8},{8,16},{16,24},{24,32},{32,40},{40,48},{48,56},{56,64},{64,7... | collective-permute-start | bytes 589832 | tf_op jit(solution)/shard_map/ppermute | solution.py:373
  8.1 0.8 copy.29
  10.2 0.7 clamp_select_fusion.1
  11.4 0.7 add_reduce_fusion
  13.5 11.7 %prepare_nodes.1.left_ref = bf16[136,256,48]{2,1,0:T(8,128)(2,1)} custom-call(f32[3,2048]{1,0:T(4,128)} %centres_ref.1, f32[3,32768]{1,0:T(4,128)} %nodes_ref.1), custom_call_target="tpu_custom_call" | custom-call | tf_op jit(solution)/shard_map/prepare_nodes/pallas_call | solution.py:70
  26.0 2.2 prepare_centres.1.right_ref
  28.2 3.5 %copy-done = bf16[136,256,48]{2,1,0:T(8,128)(2,1)S(1)} copy-done((bf16[136,256,48]{2,1,0:T(8,128)(2,1)S(1)}, bf16[136,256,48]{2,1,0:T(8,128)(2,1)}, u32[]{:S(2)}) %copy-start) | copy-done | bytes 3342360
  31.7 1.1 copy-done.1
  32.8 6.9 %operator.2.own_ref.refs_4_.v1_ref = f32[16,2048]{1,0:T(8,128)S(1)} custom-call(s32[1]{0:T(128)} %bitcast.2.count_ref, s32[40]{0:T(128)S(1)} %select_reduce_fusion.3.place_ref, s32[120]{0:T(128)S(1)} %reshape.129.member_ref, bf16[136,256,48]{2,1,0:T(8,128)(2,1)S(1)} %copy-done, bf16[24,48,256]{2,1,0:T(8,128)(2,1)S(1)} %copy-done.1, ...), custom_call_target="tpu_custom_call" | custom-call | tf_op jit(solution)/shard_map/operator/pallas_call | solution.py:169
  39.7 1.3 collective-permute-start.3
  41.0 6.9 %collective-permute-start.2 = (f32[16,2048]{1,0:T(8,128)S(1)}, f32[16,2048]{1,0:T(8,128)S(1)}, u32[]{:S(2)}, u32[]{:S(2)}) collective-permute-start(f32[16,2048]{1,0:T(8,128)S(1)} %operator.2.own_ref.refs_4_.v1_ref), channel_id=1, source_target_pairs={{0,8},{8,16},{16,24},{24,32},{32,40},{40,48},{48,56},{56,64},{64,7... | collective-permute-start | bytes 393224 | tf_op jit(solution)/shard_map/ppermute | solution.py:373
  48.0 0.8 collective-permute-done.3.after_ref.refs_7_
  48.7 1.1 collective-permute-done.2.before_ref.refs_1_
  49.8 6.9 %operator.3.refs_5_.v2_ref = f32[16,2048]{1,0:T(8,128)S(1)} custom-call(s32[1]{0:T(128)} %bitcast.2.count_ref, s32[40]{0:T(128)S(1)} %select_reduce_fusion.3.place_ref, s32[120]{0:T(128)S(1)} %reshape.129.member_ref, bf16[136,256,48]{2,1,0:T(8,128)(2,1)S(1)} %copy-done, bf16[24,48,256]{2,1,0:T(8,128)(2,1)S(1)} %copy-done.1, ...), custom_call_target="tpu_custom_call" | custom-call | tf_op jit(solution)/shard_map/operator/pallas_call | solution.py:169
  56.7 1.3 collective-permute-start.5
  58.0 7.1 %collective-permute-start.4 = (f32[16,2048]{1,0:T(8,128)S(1)}, f32[16,2048]{1,0:T(8,128)S(1)}, u32[]{:S(2)}, u32[]{:S(2)}) collective-permute-start(f32[16,2048]{1,0:T(8,128)S(1)} %operator.3.refs_5_.v2_ref), channel_id=1, source_target_pairs={{0,8},{8,16},{16,24},{24,32},{32,40},{40,48},{48,56},{56,64},{64,7... | collective-permute-start | bytes 393224 | tf_op jit(solution)/shard_map/ppermute | solution.py:373
  66.0 0.7 reshape.127.member_ref
  68.2 63.8 %volume.1 = (f32[48,32768]{1,0:T(8,128)}, f32[256,256]{1,0:T(8,128)}) custom-call(s32[1]{0:T(128)} %bitcast.count_ref, s32[324]{0:T(512)} %select_reduce_fusion.1.place_ref, s32[1296]{0:T(1024)} %reshape.127.member_ref, bf16[136,256,48]{2,1,0:T(8,128)(2,1)} %prepare_nodes.1.left_ref, bf16[24,48,256]{2,1,0:T(8,128)(2,1)} %prepare_centres.1.right_ref, ...), custom_call_target="tpu_custom_call" | custom-call | tf_op jit(solution)/shard_map/volume/pallas_call | solution.py:254
  132.0 1.2 copy.34
  133.2 112.4 %all_to_all.11 = f32[256,1,256]{2,1,0:T(1,128)S(1)} all-to-all(f32[256,1,256]{2,1,0:T(1,128)S(1)} %copy.34), channel_id=1, replica_groups=mesh['surf'=32,'vol'=8] {'surf','vol'}, dimensions={0} | all-to-all | bytes 524288 | tf_op jit(solution)/shard_map/all_to_all | solution.py:408
  245.6 0.7 copy.37
  246.3 5.4 %combine.1 = (f32[16,2048]{1,0:T(8,128)}, f32[16,32768]{1,0:T(8,128)}) custom-call(f32[256,256]{1,0:T(8,128)} %bitcast.19, f32[16,2048]{1,0:T(8,128)} %v0_ref.1, f32[16,2048]{1,0:T(8,128)} %copy-done.2, f32[16,2048]{1,0:T(8,128)} %copy-done.4, f32[48,32768]{1,0:T(8,128)} %get-tuple-element.5.image_ref), custom_call_target="tpu_custom_call" | custom-call | tf_op jit(solution)/shard_map/combine/pallas_call | solution.py:331
  (65 shorter events, 5.1 us)
Async XLA Ops:
  0.6 27.6 %copy-start.3 = (f32[16,2048]{1,0:T(8,128)S(1)}, f32[16,2048]{1,0:T(8,128)}, u32[]{:S(2)}) copy-start(f32[16,2048]{1,0:T(8,128)} %v0_ref.1) | copy-start | bytes 393220
  1.7 23.5 %copy-start.9 = (f32[24,2048]{1,0:T(8,128)}, f32[24,2048]{1,0:T(8,128)S(1)}, u32[]{:S(2)}) copy-start(f32[24,2048]{1,0:T(8,128)S(1)} %pad_maximum_fusion.own_ref) | copy-start | bytes 589828
  1.7 23.4 %collective-permute-start.1 = (f32[24,2048]{1,0:T(8,128)S(1)}, f32[24,2048]{1,0:T(8,128)S(1)}, u32[]{:S(2)}, u32[]{:S(2)}) collective-permute-start(f32[24,2048]{1,0:T(8,128)S(1)} %pad_maximum_fusion.own_ref), channel_id=1, source_target_pairs={{8,0},{16,8},{24,16},{32,24},{40,32},{48,40},{56,48},{64,56},{72,6... | collective-permute-start | bytes 589832 | tf_op jit(solution)/shard_map/ppermute | solution.py:373
  3.0 22.2 %collective-permute-start = (f32[24,2048]{1,0:T(8,128)S(1)}, f32[24,2048]{1,0:T(8,128)S(1)}, u32[]{:S(2)}, u32[]{:S(2)}) collective-permute-start(f32[24,2048]{1,0:T(8,128)S(1)} %pad_maximum_fusion.own_ref), channel_id=1, source_target_pairs={{0,8},{8,16},{16,24},{24,32},{32,40},{40,48},{48,56},{56,64},{64,7... | collective-permute-start | bytes 589832 | tf_op jit(solution)/shard_map/ppermute | solution.py:373
  25.2 0.7 copy-start.10
  25.2 31.5 %copy-start.5 = (f32[16,2048]{1,0:T(8,128)}, f32[16,2048]{1,0:T(8,128)S(1)}, u32[]{:S(2)}) copy-start(f32[16,2048]{1,0:T(8,128)S(1)} %slice.18.after_ref.refs_6_) | copy-start | bytes 393220
  25.2 0.8 copy-start.11
  26.0 30.7 %copy-start.6 = (f32[16,2048]{1,0:T(8,128)}, f32[16,2048]{1,0:T(8,128)S(1)}, u32[]{:S(2)}) copy-start(f32[16,2048]{1,0:T(8,128)S(1)} %slice.17.before_ref.refs_0_) | copy-start | bytes 393220
  28.2 3.5 %copy-start = (bf16[136,256,48]{2,1,0:T(8,128)(2,1)S(1)}, bf16[136,256,48]{2,1,0:T(8,128)(2,1)}, u32[]{:S(2)}) copy-start(bf16[136,256,48]{2,1,0:T(8,128)(2,1)} %prepare_nodes.1.left_ref) | copy-start | bytes 10027012
  31.7 1.1 copy-start.1
  39.7 27.8 %copy-start.2 = (f32[16,2048]{1,0:T(8,128)}, f32[16,2048]{1,0:T(8,128)S(1)}, u32[]{:S(2)}) copy-start(f32[16,2048]{1,0:T(8,128)S(1)} %operator.2.own_ref.refs_4_.v1_ref) | copy-start | bytes 393220
  39.7 9.0 %collective-permute-start.3 = (f32[16,2048]{1,0:T(8,128)S(1)}, f32[16,2048]{1,0:T(8,128)S(1)}, u32[]{:S(2)}, u32[]{:S(2)}) collective-permute-start(f32[16,2048]{1,0:T(8,128)S(1)} %operator.2.own_ref.refs_4_.v1_ref), channel_id=1, source_target_pairs={{8,0},{16,8},{24,16},{32,24},{40,32},{48,40},{56,48},{64,56},{72,6... | collective-permute-start | bytes 393224 | tf_op jit(solution)/shard_map/ppermute | solution.py:373
  41.0 8.8 %collective-permute-start.2 = (f32[16,2048]{1,0:T(8,128)S(1)}, f32[16,2048]{1,0:T(8,128)S(1)}, u32[]{:S(2)}, u32[]{:S(2)}) collective-permute-start(f32[16,2048]{1,0:T(8,128)S(1)} %operator.2.own_ref.refs_4_.v1_ref), channel_id=1, source_target_pairs={{0,8},{8,16},{16,24},{24,32},{32,40},{40,48},{48,56},{56,64},{64,7... | collective-permute-start | bytes 393224 | tf_op jit(solution)/shard_map/ppermute | solution.py:373
  48.7 18.8 %copy-start.7 = (f32[16,2048]{1,0:T(8,128)}, f32[16,2048]{1,0:T(8,128)S(1)}, u32[]{:S(2)}) copy-start(f32[16,2048]{1,0:T(8,128)S(1)} %collective-permute-done.3.after_ref.refs_7_) | copy-start | bytes 393220
  49.8 17.7 %copy-start.8 = (f32[16,2048]{1,0:T(8,128)}, f32[16,2048]{1,0:T(8,128)S(1)}, u32[]{:S(2)}) copy-start(f32[16,2048]{1,0:T(8,128)S(1)} %collective-permute-done.2.before_ref.refs_1_) | copy-start | bytes 393220
  56.7 10.8 %copy-start.4 = (f32[16,2048]{1,0:T(8,128)}, f32[16,2048]{1,0:T(8,128)S(1)}, u32[]{:S(2)}) copy-start(f32[16,2048]{1,0:T(8,128)S(1)} %operator.3.refs_5_.v2_ref) | copy-start | bytes 393220
  56.7 10.7 %collective-permute-start.5 = (f32[16,2048]{1,0:T(8,128)S(1)}, f32[16,2048]{1,0:T(8,128)S(1)}, u32[]{:S(2)}, u32[]{:S(2)}) collective-permute-start(f32[16,2048]{1,0:T(8,128)S(1)} %operator.3.refs_5_.v2_ref), channel_id=1, source_target_pairs={{8,0},{16,8},{24,16},{32,24},{40,32},{48,40},{56,48},{64,56},{72,6... | collective-permute-start | bytes 393224 | tf_op jit(solution)/shard_map/ppermute | solution.py:373
  58.0 9.5 %collective-permute-start.4 = (f32[16,2048]{1,0:T(8,128)S(1)}, f32[16,2048]{1,0:T(8,128)S(1)}, u32[]{:S(2)}, u32[]{:S(2)}) collective-permute-start(f32[16,2048]{1,0:T(8,128)S(1)} %operator.3.refs_5_.v2_ref), channel_id=1, source_target_pairs={{0,8},{8,16},{16,24},{24,32},{32,40},{40,48},{48,56},{56,64},{64,7... | collective-permute-start | bytes 393224 | tf_op jit(solution)/shard_map/ppermute | solution.py:373
  67.5 0.6 copy-start.12
  67.5 0.7 copy-start.13

commit v2 on v1

--- a/solution.py
+++ b/solution.py
@@ -43,39 +43,26 @@
     return jnp.where(row == 3, low, jnp.where(row == 4, high, padded))
 
 
-def node_kernel(steps, centres_ref, nodes_ref, out_ref):
-    step = pl.program_id(0)
-    origin = centres_ref[:, 0:1]
-
-    def fill(points):
-        a, b, c = split3(augmented((points - origin) * (1.0 / RADIUS), True))
-        rows = jnp.concatenate([a, b, a, b, c, a], axis=0)
-        for t in range(out_ref.shape[0]):
-            out_ref[t] = jnp.transpose(rows[:, t * BLK : (t + 1) * BLK]).astype(bf16)
-
-    @pl.when(step < steps - 1)
-    def _():
-        fill(nodes_ref[...])
-
-    @pl.when(step == steps - 1)
-    def _():
-        fill(centres_ref[...])
+def node_kernel(centres_ref, nodes_ref, out_ref):
+    points = (nodes_ref[...] - centres_ref[:, 0:1]) * (1.0 / RADIUS)
+    a, b, c = split3(augmented(points, True))
+    rows = jnp.concatenate([a, b, a, b, c, a], axis=0)
+    for t in range(out_ref.shape[0]):
+        out_ref[t] = rows[:, t * BLK : (t + 1) * BLK].astype(bf16)
 
 
 def prepare_nodes(centres, nodes):
-    width = centres.shape[1]
-    per_step = width // BLK
-    node_steps = nodes.shape[1] // width
-    steps = node_steps + 1
-    return pl.pallas_call(
-        functools.partial(node_kernel, steps),
-        grid=(steps,),
+    tiles = nodes.shape[1] // BLK
+    step = 32 if tiles % 32 == 0 else tiles
+    return pl.pallas_call(
+        node_kernel,
+        grid=(tiles // step,),
         in_specs=[
-            pl.BlockSpec((3, width), lambda i: (0, 0)),
-            pl.BlockSpec((3, width), lambda i: (0, jnp.minimum(i, node_steps - 1))),
+            pl.BlockSpec((3, BLK), lambda i: (0, 0)),
+            pl.BlockSpec((3, step * BLK), lambda i: (0, i)),
         ],
-        out_specs=pl.BlockSpec((per_step, BLK, DEPTH), lambda i: (i, 0, 0)),
-        out_shape=jax.ShapeDtypeStruct((steps * per_step, BLK, DEPTH), bf16),
+        out_specs=pl.BlockSpec((step, DEPTH, BLK), lambda i: (i, 0, 0)),
+        out_shape=jax.ShapeDtypeStruct((tiles, DEPTH, BLK), bf16),
         name="prepare_nodes",
     )(centres, nodes)
 
@@ -102,30 +89,37 @@
     )(before, own, after)
 
 
+def pl_reciprocal(x):
+    return pltpu.reciprocal(x, approx=True)
+
+
 def phi(square):
-    bounded = jnp.maximum(square, 1e-12)
-    scaled = bounded * lax.rsqrt(bounded)
+    scaled = pl_reciprocal(lax.rsqrt(jnp.maximum(square, 1e-12)))
     remain = jnp.maximum(1.0 - scaled, 0.0)
     squared = remain * remain
     return (squared * squared * (scaled + 0.25)).astype(bf16)
 
 
+def clear(tiles, total):
+    def one(t, carry):
+        total[t] = jnp.zeros((BLK, LANES), f32)
+        return carry
+
+    lax.fori_loop(0, tiles + 1, one, 0)
+
+
 def accumulate(
     unroll, together, tiles, group_count, places, members, left_ref, right_ref, weight_ref, total
 ):
-    def clear(t, carry):
-        total[t] = jnp.zeros((BLK, LANES), f32)
-        return carry
-
-    lax.fori_loop(0, tiles + 1, clear, 0)
-
     def step(g, carry):
         for h in range(unroll):
             group = g * unroll + h
             place = places[group]
             ids = [members[group * together + j] for j in range(together)]
-            left = jnp.concatenate([left_ref[jnp.minimum(t, tiles - 1)] for t in ids], axis=0)
-            square = jnp.dot(left, right_ref[place], preferred_element_type=f32)
+            left = jnp.concatenate([left_ref[jnp.minimum(t, tiles - 1)] for t in ids], axis=1)
+            square = lax.dot_general(
+                left, right_ref[place], (((0,), (0,)), ((), ())), preferred_element_type=f32
+            )
             image = jnp.dot(phi(square), weight_ref[place], preferred_element_type=f32)
             for j, t in enumerate(ids):
                 total[t] += image[j * BLK : (j + 1) * BLK]
@@ -152,6 +146,7 @@
     before_ref, own_ref, after_ref, out_ref, weight_ref, total,
 ):
     fill_weights(weight_ref, ((before_ref,), (own_ref,), (after_ref,)), tiles)
+    clear(tiles, total)
     accumulate(
         unroll, together, tiles, count_ref[0], place_ref, member_ref, left_ref, right_ref,
         weight_ref, total,
@@ -164,14 +159,10 @@
 
 def apply_operator(unroll, together, lists, left, right, before, own, after):
     tiles = own.shape[1] // BLK
-    last = left.shape[0] // tiles - 1
     vmem, smem = whole(pltpu.VMEM), whole(pltpu.SMEM)
     return pl.pallas_call(
         functools.partial(operator_kernel, unroll, together, tiles),
-        grid=(1,),
-        in_specs=[smem] * 3
-        + [pl.BlockSpec((tiles, BLK, DEPTH), lambda i: (last, 0, 0))]
-        + [vmem] * 4,
+        in_specs=[smem] * 3 + [vmem] * 5,
         out_specs=vmem,
         out_shape=jax.ShapeDtypeStruct(own.shape, f32),
         scratch_shapes=[
@@ -205,67 +196,102 @@
 
 
 def volume_kernel(
-    unroll, together, tiles, own_tiles, share, count_ref, place_ref, member_ref, left_ref, right_ref,
-    *refs,
+    unroll, together, sizes, share, count_ref, place_ref, member_ref, turn_ref, right_ref, *refs
 ):
-    fields = (refs[0:3], refs[3:6], refs[6:9])
-    out_ref, sums_ref, weight_ref, total = refs[9:]
-    fill_weights(weight_ref, fields, own_tiles)
+    lefts, fields = refs[0:3], (refs[3:6], refs[6:9], refs[9:12])
+    out_ref, guest_ref, sums_ref, weight_ref, total, left_ref, image_ref, sems, sent = refs[12:]
+    own, guests, checks = sizes
+    tiles = own + guests + checks
+    turn = turn_ref[0]
+    spans = (
+        (lefts[0], left_ref.at[pl.ds(0, own)]),
+        (lefts[1], left_ref.at[pl.ds(own, guests)]),
+        (lefts[2].at[pl.ds(turn * checks, checks)], left_ref.at[pl.ds(own + guests, checks)]),
+    )
+    copies = [pltpu.make_async_copy(a, b, sems.at[i]) for i, (a, b) in enumerate(spans)]
+    for copy in copies:
+        copy.start()
+    per = fields[1][0].shape[1] // BLK
+    fill_weights(weight_ref, fields, per)
+    clear(tiles, total)
+    for copy in copies:
+        copy.wait()
     accumulate(
         unroll, together, tiles, count_ref[0], place_ref, member_ref, left_ref, right_ref,
         weight_ref, total,
     )
     wide = KRYLOV * MODES
-
-    def finish(g, gram):
-        for h in range(4):
-            t = g * 4 + h
+    zeros = tuple(jnp.zeros((MODES, BLK), f32) for _ in PAIRS)
+
+    def finish(first, ref, sem, steps, g, gram):
+        for h in range(steps):
+            t = first + g * steps + h
             image = jnp.transpose(total[t])
             image = image[0:wide] + image[wide : 2 * wide]
-            out_ref[:, pl.ds(pl.multiple_of(t * BLK, BLK), BLK)] = image
+            image_ref[:, pl.ds(pl.multiple_of(t * BLK, BLK), BLK)] = image
             parts = [image[k * MODES : (k + 1) * MODES] for k in range(KRYLOV)]
             gram = tuple(s + parts[i] * parts[j] for s, (i, j) in zip(gram, PAIRS))
+        width = steps * BLK
+        start = pl.multiple_of(first * BLK + g * width, BLK)
+        pltpu.make_async_copy(
+            image_ref.at[:, pl.ds(start, width)],
+            ref.at[:, pl.ds(pl.multiple_of(g * width, BLK), width)],
+            sem,
+        ).start()
         return gram
 
-    node_tiles = tiles - own_tiles
-    gram = lax.fori_loop(
-        0, node_tiles // 4, finish, tuple(jnp.zeros((MODES, BLK), f32) for _ in PAIRS)
-    )
+    def steps_of(count):
+        return next(n for n in (4, 5, 3, 2, 1) if count % n == 0)
+
+    n = steps_of(guests)
+    gram = lax.fori_loop(0, guests // n, functools.partial(finish, own, guest_ref, sent.at[1], n), zeros)
+    n = steps_of(own)
+    gram = lax.fori_loop(0, own // n, functools.partial(finish, 0, out_ref, sent.at[0], n), gram)
     columns = [jnp.sum(s, axis=1, keepdims=True) for s in gram]
-    own = [r[...] for r in fields[1]]
-    moments = [own[0] * own[0], own[0] * own[1], own[1] * own[1], own[1] * own[2], own[2] * own[2]]
+    v = [r[...] for r in fields[1]]
+    moments = [v[0] * v[0], v[0] * v[1], v[1] * v[1], v[1] * v[2], v[2] * v[2]]
     columns += [share * jnp.sum(s, axis=1, keepdims=True) for s in moments]
     last = jnp.zeros((MODES, BLK), f32)
-    for b in range(own_tiles):
-        image = jnp.transpose(total[node_tiles + b])
-        piece = own[2][:, b * BLK : (b + 1) * BLK]
-        low = 2 * MODES
+    low = 2 * MODES
+    for b in range(checks):
+        image = jnp.transpose(total[own + guests + b])
+        start = pl.multiple_of((turn * checks + b) * BLK, BLK)
+        piece = fields[1][2][:, pl.ds(start, BLK)]
         image = image[low : low + MODES] + image[wide + low : wide + low + MODES]
         last = last + piece * (image + SHIFT * piece)
-    columns.append(share * jnp.sum(last, axis=1, keepdims=True))
-    sums_ref[...] = jnp.broadcast_to(row_of(columns), sums_ref.shape)
-
-
-def volume_images(unroll, together, lists, left, right, fields, devices, share):
-    own_tiles = fields[1][0].shape[1] // BLK
-    tiles = left.shape[0]
-    nodes = (tiles - own_tiles) * BLK
-    vmem, smem = whole(pltpu.VMEM), whole(pltpu.SMEM)
-    return pl.pallas_call(
-        functools.partial(volume_kernel, unroll, together, tiles, own_tiles, share),
-        in_specs=[smem] * 3 + [vmem] * 11,
-        out_specs=(vmem, vmem),
+    columns.append(jnp.sum(last, axis=1, keepdims=True))
+    row = row_of(columns)
+    pair = jnp.concatenate([row[:, 0:LANES], row[:, LANES : 2 * LANES]], axis=0)
+    sums_ref[...] = jnp.broadcast_to(pair[None], sums_ref.shape)
+    pltpu.make_async_copy(image_ref.at[:, pl.ds(0, own * BLK)], out_ref, sent.at[0]).wait()
+    pltpu.make_async_copy(image_ref.at[:, pl.ds(own * BLK, guests * BLK)], guest_ref, sent.at[1]).wait()
+
+
+def volume_images(unroll, together, lists, turn, right, lefts, checks, fields, devices, share):
+    per = fields[1][0].shape[1] // BLK
+    own, guests = lefts[0].shape[0], lefts[1].shape[0]
+    tiles = own + guests + checks
+    vmem, smem, far = whole(pltpu.VMEM), whole(pltpu.SMEM), whole(pl.ANY)
+    return pl.pallas_call(
+        functools.partial(volume_kernel, unroll, together, (own, guests, checks), share),
+        in_specs=[smem] * 4 + [vmem] + [far] * 3 + [vmem] * 9,
+        out_specs=(far, far, vmem),
         out_shape=(
-            jax.ShapeDtypeStruct((KRYLOV * MODES, nodes), f32),
-            jax.ShapeDtypeStruct((devices, BLK), f32),
+            jax.ShapeDtypeStruct((KRYLOV * MODES, own * BLK), f32),
+            jax.ShapeDtypeStruct((KRYLOV * MODES, guests * BLK), f32),
+            jax.ShapeDtypeStruct((devices, 2, LANES), f32),
         ),
         scratch_shapes=[
-            pltpu.VMEM((3 * own_tiles, BLK, LANES), bf16),
+            pltpu.VMEM((3 * per, BLK, LANES), bf16),
             pltpu.VMEM((tiles + 1, BLK, LANES), f32),
+            pltpu.VMEM((tiles, DEPTH, BLK), bf16),
+            pltpu.VMEM((KRYLOV * MODES, (own + guests) * BLK), f32),
+            pltpu.SemaphoreType.DMA((3,)),
+            pltpu.SemaphoreType.DMA((2,)),
         ],
         compiler_params=pltpu.CompilerParams(vmem_limit_bytes=58 * 2**20),
         name="volume",
-    )(*lists, left, right, *[f for side in fields for f in side])
+    )(*lists, turn, right, *lefts, *[f for side in fields for f in side])
 
 
 def coefficients(row, total_nodes):
@@ -305,42 +331,90 @@
     return answer, [a / scale for a in answer]
 
 
-def combine_kernel(total_nodes, sums_ref, v0_ref, v1_ref, v2_ref, image_ref, weights_ref, out_ref, coef):
-    @pl.when(pl.program_id(0) == 0)
-    def _():
-        row = jnp.sum(sums_ref[...], axis=0, keepdims=True)
-        answer, scaled = coefficients(row, total_nodes)
-        weights_ref[...] = answer[0] * v0_ref[...] + answer[1] * v1_ref[...] + answer[2] * v2_ref[...]
-        for k, column in enumerate(scaled):
-            coef[k] = jnp.broadcast_to(column, (MODES, LANES))
-
-    c = [coef[k][:, 0:1] for k in range(KRYLOV)]
-    out_ref[...] = (
+def settle_kernel(total_nodes, sums_ref, v0_ref, v1_ref, v2_ref, guest_ref, weights_ref, coef_ref, out_ref):
+    pair = jnp.sum(sums_ref[...], axis=0)
+    row = jnp.concatenate([pair[0:1], pair[1:2]], axis=1)
+    answer, scaled = coefficients(row, total_nodes)
+    weights_ref[...] = answer[0] * v0_ref[...] + answer[1] * v1_ref[...] + answer[2] * v2_ref[...]
+    for k, column in enumerate(scaled):
+        coef_ref[k] = jnp.broadcast_to(column, (MODES, LANES))
+    out_ref[...] = blend(scaled, guest_ref).astype(bf16)
+
+
+def blend(c, image_ref):
+    return (
         c[0] * image_ref[0:MODES]
         + c[1] * image_ref[MODES : 2 * MODES]
         + c[2] * image_ref[2 * MODES : 3 * MODES]
     )
 
 
-def combine(sums, vectors, images, total_nodes):
+def settle(sums, vectors, guests, total_nodes):
+    vmem = whole(pltpu.VMEM)
+    return pl.pallas_call(
+        functools.partial(settle_kernel, total_nodes),
+        in_specs=[vmem] * 5,
+        out_specs=(vmem,) * 3,
+        out_shape=(
+            jax.ShapeDtypeStruct(vectors[0].shape, f32),
+            jax.ShapeDtypeStruct((KRYLOV, MODES, LANES), f32),
+            jax.ShapeDtypeStruct((MODES, guests.shape[1]), bf16),
+        ),
+        name="settle",
+    )(sums, *vectors, guests)
+
+
+def combine_kernel(coef_ref, image_ref, out_ref):
+    out_ref[...] = blend([coef_ref[k][:, 0:1] for k in range(KRYLOV)], image_ref)
+
+
+def combine(coef, images):
     nodes = images.shape[1]
     width = 8192 if nodes % 8192 == 0 else nodes
-    fixed = lambda i: (0, 0)
-    moving = lambda i: (0, i)
-    small = pl.BlockSpec(vectors[0].shape, fixed)
-    return pl.pallas_call(
-        functools.partial(combine_kernel, total_nodes),
+    return pl.pallas_call(
+        combine_kernel,
         grid=(nodes // width,),
-        in_specs=[pl.BlockSpec(sums.shape, fixed), small, small, small]
-        + [pl.BlockSpec((KRYLOV * MODES, width), moving)],
-        out_specs=(small, pl.BlockSpec((MODES, width), moving)),
-        out_shape=(
-            jax.ShapeDtypeStruct(vectors[0].shape, f32),
-            jax.ShapeDtypeStruct((MODES, nodes), f32),
-        ),
-        scratch_shapes=[pltpu.VMEM((KRYLOV, MODES, LANES), f32)],
+        in_specs=[
+            pl.BlockSpec(coef.shape, lambda i: (0, 0, 0)),
+            pl.BlockSpec((KRYLOV * MODES, width), lambda i: (0, i)),
+        ],
+        out_specs=pl.BlockSpec((MODES, width), lambda i: (0, i)),
+        out_shape=jax.ShapeDtypeStruct((MODES, nodes), f32),
         name="combine",
-    )(sums, *vectors, images)
+    )(coef, images)
+
+
+def insert_kernel(kept, turn_ref, *refs):
+    parts, out_ref, wide, sems = refs[1:-3], refs[-3], refs[-2], refs[-1]
+
+    @pl.when(turn_ref[0] == 0)
+    def _():
+        width = parts[0].shape[1]
+        copies = []
+        for k, part in enumerate(parts):
+            wide[k] = part[...].astype(f32)
+            target = out_ref.at[:, pl.ds((kept + k * width // BLK) * BLK, width)]
+            copy = pltpu.make_async_copy(wide.at[k], target, sems.at[k])
+            copy.start()
+            copies.append(copy)
+        for copy in copies:
+            copy.wait()
+
+
+def insert(turn, main, parts, kept):
+    vmem, far = whole(pltpu.VMEM), whole(pl.ANY)
+    return pl.pallas_call(
+        functools.partial(insert_kernel, kept),
+        in_specs=[whole(pltpu.SMEM), far] + [vmem] * len(parts),
+        out_specs=far,
+        out_shape=jax.ShapeDtypeStruct(main.shape, f32),
+        input_output_aliases={1: 0},
+        scratch_shapes=[
+            pltpu.VMEM((len(parts),) + parts[0].shape, f32),
+            pltpu.SemaphoreType.DMA((len(parts),)),
+        ],
+        name="insert",
+    )(turn, main, *parts)
 
 
 def work_list(places, together, unroll, kinds):
@@ -366,47 +440,86 @@
     return count, place.astype(jnp.int32), member.reshape(-1)
 
 
-def halves(shard, axis):
+def neighbour_pairs(axis):
     count = lax.axis_size(axis)
-    up = [(i, i + 1) for i in range(count - 1)]
-    down = [(i + 1, i) for i in range(count - 1)]
-    return lax.ppermute(shard, axis, up), lax.ppermute(shard, axis, down)
+    return [(i, i + 1) for i in range(count - 1)], [(i + 1, i) for i in range(count - 1)]
+
+
+MOVED_SHARE = 20 / 128
+
+
+def helper_turns(count):
+    return (1, 2, count - 2) if count >= 6 else (1,)
 
 
 def per_device(centres, mode_shapes, neighbours, volume_nodes, supports):
     blk_dev = neighbours.shape[0]
+    tile_dev, slots = supports.shape
     kinds = 3 * blk_dev
     offset = (lax.axis_index("surf") - 1) * blk_dev
+    helpers = helper_turns(lax.axis_size("vol"))
+    turn = lax.axis_index("vol")
+    turns = turn.astype(jnp.int32).reshape(1)
     devices = lax.axis_size("surf") * lax.axis_size("vol")
     share = 1.0 / lax.axis_size("vol")
+    checks = blk_dev // lax.axis_size("vol")
     total_nodes = volume_nodes.shape[1] * devices
+    moved = int(tile_dev * MOVED_SHARE)
+    kept = tile_dev - len(helpers) * moved
 
     packed = jnp.concatenate([centres, jnp.zeros((5, centres.shape[1]), f32), mode_shapes], axis=0)
-    before, after = halves(packed, "surf")
+    up, down = neighbour_pairs("surf")
+    before = lax.ppermute(packed, "surf", up)
 
     def place_of(ids):
         return jnp.where(ids >= 0, jnp.clip(ids - offset, 0, kinds - 1), -1)
 
     own_places = place_of(neighbours)
+    own_list = work_list(own_places, 3, 4, kinds)
+    own_left = prepare_nodes(centres, centres)
+    again, own_left = lax.optimization_barrier((packed, own_left))
+    after = lax.ppermute(again, "surf", down)
     left = prepare_nodes(centres, volume_nodes)
-    own_list = work_list(own_places, 3, 4, kinds)
-    whole_list = work_list(jnp.concatenate([place_of(supports), own_places]), 4, 4, kinds)
 
     right = prepare_centres(before, packed, after)
+    ids = jnp.pad(supports[kept:].astype(f32), ((0, 0), (0, BLK - slots))).reshape(1, -1)
+    parcel = jnp.concatenate([volume_nodes[:, kept * BLK :], ids], axis=0)
+    parcel, right = lax.optimization_barrier((parcel, right))
+    width = moved * BLK
+    got = jnp.zeros((4, width), f32)
+    helping = False
+    for k, helper in enumerate(helpers):
+        piece = parcel[:, k * width : (k + 1) * width]
+        got = got + lax.ppermute(piece, "vol", [(0, helper)])
+        helping = helping | (turn == helper)
+    guest_ids = got[3].reshape(moved, BLK)[:, :slots].astype(jnp.int32)
+    guest_places = jnp.where(helping, place_of(guest_ids), -1)
+    kept_here = (turn > 0) | (jnp.arange(tile_dev) < kept)
+    tile_places = jnp.where(kept_here[:, None], place_of(supports), -1)
+    check_places = lax.dynamic_slice_in_dim(own_places, turn * checks, checks, axis=0)
+    places = jnp.concatenate([tile_places, guest_places, check_places], axis=0)
+    whole_list = work_list(places, 4, 4, kinds)
+    guest_left = prepare_nodes(centres, got[:3])
+
     v0 = mode_shapes
     v0_before, v0_after = before[8:], after[8:]
-    v1 = apply_operator(4, 3, own_list, left, right, v0_before, v0, v0_after)
-    v1_before, v1_after = halves(v1, "surf")
-    v2 = apply_operator(4, 3, own_list, left, right, v1_before, v1, v1_after)
-    v2_before, v2_after = halves(v2, "surf")
+    v1 = apply_operator(4, 3, own_list, own_left, right, v0_before, v0, v0_after)
+    v1_before, v1_after = lax.ppermute(v1, "surf", up), lax.ppermute(v1, "surf", down)
+    v2 = apply_operator(4, 3, own_list, own_left, right, v1_before, v1, v1_after)
+    v2_before, v2_after = lax.ppermute(v2, "surf", up), lax.ppermute(v2, "surf", down)
     fields = (
         (v0_before, v1_before, v2_before),
         (v0, v1, v2),
         (v0_after, v1_after, v2_after),
     )
-    images, sums = volume_images(4, 4, whole_list, left, right, fields, devices, share)
+    lefts = (left, guest_left, own_left)
+    images, guests, sums = volume_images(
+        4, 4, whole_list, turns, right, lefts, checks, fields, devices, share
+    )
     sums = lax.all_to_all(sums, ("surf", "vol"), 0, 0, tiled=True)
-    return combine(sums, (v0, v1, v2), images, total_nodes)
+    weights, coef, away = settle(sums, (v0, v1, v2), guests, total_nodes)
+    parts = [lax.ppermute(away, "vol", [(helper, 0)]) for helper in helpers]
+    return weights, insert(turns, combine(coef, images), parts, kept)
 
 
 def solution(mesh):

time: 253 us -> 192 us (0.76)
  blocking collectives: 112 us -> 43 us
  starting transfers between devices: 22.9 us -> 29.8 us
  Pallas kernels: 96.8 us -> 102 us
    all_to_all x1, blocking collectives: 112 us -> 43 us  [per_device(): sums = lax.all_to_all(sums, ('surf', 'vol'), 0, 0, tiled=True)]
    ppermute x6 -> x12, starting transfers between devices: 22.9 us -> 29.8 us  [the longest x1 7.48 us: per_device(): lax.ppermute(v1, 'surf', up)]
    pallas_call x3 -> x7, Pallas kernels: 80.9 us -> 86.4 us  [the longest x1 69.8 us: volume_images(): pl.pallas_call(functools.partial(volume_kernel, unroll, together, (own, g...]
    unnamed x30 -> x45, local copies, waits for them, and re-layouts: 7.52 us -> 5.51 us
  transfers between devices with their start and end apart: 6 -> 12, of which waited for: 2 -> 0; matrix products, arithmetic and copies ran while one was open for 3% -> 4% of each run, Pallas kernels for 5% -> 10%
where the time goes in v2:
time: 192 us; the launch traced here: 191 us
  Pallas kernels  102 us (53%)
  blocking collectives  43 us (22%)
  starting transfers between devices  29.8 us (16%)
  local copies, waits for them, and re-layouts  8.8 us (5%)
  other arithmetic  4.52 us (2%)
  between operations  2.42 us (1%)
    pallas_call x1, Pallas kernels, volume_images(): pl.pallas_call(functools.partial(volume_kernel, unroll, together, (own, g...  69.8 us
    all_to_all x1, blocking collectives, per_device(): sums = lax.all_to_all(sums, ('surf', 'vol'), 0, 0, tiled=True)  43 us
    pallas_call x2, Pallas kernels, apply_operator(): pl.pallas_call(functools.partial(operator_kernel, unroll, together, tiles...  13.6 us
    pallas_call x3, Pallas kernels, prepare_nodes(): pl.pallas_call(node_kernel, grid=(tiles // step,), in_specs=[pl.BlockSpec...  7.84 us
    ppermute x1, starting transfers between devices, per_device(): lax.ppermute(v1, 'surf', up)  7.48 us
    ppermute x1, starting transfers between devices, per_device(): lax.ppermute(v2, 'surf', up)  6.97 us
    unnamed x45, local copies, waits for them, and re-layouts  5.51 us
    pallas_call x1, Pallas kernels, combine(): pl.pallas_call(combine_kernel, grid=(nodes // width,), in_specs=[pl.Block...  5.05 us
  transfers between devices with their start and end apart: 12, of which 0 were waited for; matrix products, arithmetic and copies ran while one was open for 4% of the time, Pallas kernels for 10%

profile of v2, /device:TPU:1, one launch (start us, length us, event | category | flops | bytes accessed | tf_op | source)
XLA Modules:
  0.0 191.5 jit_solution(3147168284879461706)
XLA Ops:
  0.7 1.0 pad_maximum_fusion.1.own_ref
  1.8 4.4 %collective-permute-start = (f32[24,2048]{1,0:T(8,128)S(1)}, f32[24,2048]{1,0:T(8,128)S(1)}, u32[]{:S(2)}, u32[]{:S(2)}) collective-permute-start(f32[24,2048]{1,0:T(8,128)S(1)} %pad_maximum_fusion.1.own_ref), channel_id=1, source_target_pairs={{0,8},{8,16},{16,24},{24,32},{32,40},{40,48},{48,56},{56,64},{64,7... | collective-permute-start | bytes 589832 | tf_op jit(solution)/shard_map/ppermute | solution.py:472
  6.2 1.6 prepare_nodes.3.left_ref.refs_2_
  7.8 1.3 collective-permute-start.1
  11.2 4.3 %prepare_nodes.4.refs_0_ = bf16[128,48,256]{2,1,0:T(8,128)(2,1)} custom-call(f32[3,2048]{1,0:T(4,128)} %centres_ref.5, f32[3,32768]{1,0:T(4,128)} %nodes_ref.3), custom_call_target="tpu_custom_call" | custom-call | tf_op jit(solution)/shard_map/prepare_nodes/pallas_call | solution.py:57
  18.4 2.1 %prepare_centres.1.right_ref = bf16[24,48,256]{2,1,0:T(8,128)(2,1)} custom-call(f32[24,2048]{1,0:T(8,128)} %copy-done.11, f32[24,2048]{1,0:T(8,128)} %copy-done.10, f32[24,2048]{1,0:T(8,128)} %copy-done.12), custom_call_target="tpu_custom_call" | custom-call | tf_op jit(solution)/shard_map/prepare_centres/pallas_call | solution.py:83
  20.6 0.8 collective-permute-start.3
  22.0 1.3 collective-permute-start.2
  23.3 0.9 slice.53.after_ref.refs_9_
  24.3 1.0 slice.52.before_ref.refs_3_
  25.3 1.1 copy-done
  26.4 6.8 %operator.2.own_ref.refs_7_.v1_ref = f32[16,2048]{1,0:T(8,128)S(1)} custom-call(s32[1]{0:T(128)} %bitcast.3.count_ref, s32[40]{0:T(128)S(1)} %select_reduce_fusion.3.place_ref, s32[120]{0:T(128)S(1)} %reshape.140.member_ref, bf16[8,48,256]{2,1,0:T(8,128)(2,1)S(1)} %copy-done.2, bf16[24,48,256]{2,1,0:T(8,128)(2,1)S(1)} %copy-done, ...), custom_call_target="tpu_custom_call" | custom-call | tf_op jit(solution)/shard_map/operator/pallas_call | solution.py:163
  33.2 1.3 collective-permute-start.6
  34.5 7.5 %collective-permute-start.5 = (f32[16,2048]{1,0:T(8,128)S(1)}, f32[16,2048]{1,0:T(8,128)S(1)}, u32[]{:S(2)}, u32[]{:S(2)}) collective-permute-start(f32[16,2048]{1,0:T(8,128)S(1)} %operator.2.own_ref.refs_7_.v1_ref), channel_id=1, source_target_pairs={{0,8},{8,16},{16,24},{24,32},{32,40},{40,48},{48,56},{56,64},{64,7... | collective-permute-start | bytes 393224 | tf_op jit(solution)/shard_map/ppermute | solution.py:507
  44.0 6.8 %operator.3.refs_8_.v2_ref = f32[16,2048]{1,0:T(8,128)S(1)} custom-call(s32[1]{0:T(128)} %bitcast.3.count_ref, s32[40]{0:T(128)S(1)} %select_reduce_fusion.3.place_ref, s32[120]{0:T(128)S(1)} %reshape.140.member_ref, bf16[8,48,256]{2,1,0:T(8,128)(2,1)S(1)} %copy-done.2, bf16[24,48,256]{2,1,0:T(8,128)(2,1)S(1)} %copy-done.1, ...), custom_call_target="tpu_custom_call" | custom-call | tf_op jit(solution)/shard_map/operator/pallas_call | solution.py:163
  50.8 1.3 collective-permute-start.8
  52.1 7.0 %collective-permute-start.7 = (f32[16,2048]{1,0:T(8,128)S(1)}, f32[16,2048]{1,0:T(8,128)S(1)}, u32[]{:S(2)}, u32[]{:S(2)}) collective-permute-start(f32[16,2048]{1,0:T(8,128)S(1)} %operator.3.refs_8_.v2_ref), channel_id=1, source_target_pairs={{0,8},{8,16},{16,24},{24,32},{32,40},{40,48},{48,56},{56,64},{64,7... | collective-permute-start | bytes 393224 | tf_op jit(solution)/shard_map/ppermute | solution.py:509
  60.9 1.9 prepare_nodes.5.refs_1_
  64.0 69.8 %volume.1 = (f32[48,32768]{1,0:T(8,128)}, f32[48,5120]{1,0:T(8,128)}, f32[256,2,128]{2,1,0:T(2,128)}) custom-call(s32[1]{0:T(128)} %bitcast.count_ref, s32[356]{0:T(512)} %select_reduce_fusion.1.place_ref, s32[1424]{0:T(1024)} %reshape.137.member_ref, s32[1]{0:T(128)} %bitcast.2.turn_ref, bf16[24,48,256]{2,1,0:T(8,128)(2,1)} %prepare_centres.1.right_ref, ...), custom_call_target="tpu_custom_call" | custom-call | tf_op jit(solution)/shard_map/volume/pallas_call | solution.py:275
  133.8 43.0 %all_to_all.5.sums_ref = f32[256,2,128]{2,1,0:T(2,128)} all-to-all(f32[256,2,128]{2,1,0:T(2,128)} %get-tuple-element.16), channel_id=1, replica_groups=mesh['surf'=32,'vol'=8] {'surf','vol'}, dimensions={0} | all-to-all | bytes 524288 | tf_op jit(solution)/shard_map/all_to_all | solution.py:519
  176.9 2.7 %settle.1 = (f32[16,2048]{1,0:T(8,128)}, f32[3,16,128]{2,1,0:T(8,128)}, bf16[16,5120]{1,0:T(8,128)(2,1)}) custom-call(f32[256,2,128]{2,1,0:T(2,128)} %all_to_all.5.sums_ref, f32[16,2048]{1,0:T(8,128)} %v0_ref.1, f32[16,2048]{1,0:T(8,128)} %copy-done.4, f32[16,2048]{1,0:T(8,128)} %copy-done.5, f32[48,5120]{1,0:T(8,128)} %get-tuple-element.17.guest_ref), custom_call_target="tpu_custom_call" | custom-call | tf_op jit(solution)/shard_map/settle/pallas_call | solution.py:354
  180.9 3.0 %collective-permute-start.9 = (bf16[16,5120]{1,0:T(8,128)(2,1)}, bf16[16,5120]{1,0:T(8,128)(2,1)S(1)}, u32[]{:S(2)}, u32[]{:S(2)}) collective-permute-start(bf16[16,5120]{1,0:T(8,128)(2,1)} %get-tuple-element.21), channel_id=1, source_target_pairs={{1,0},{9,8},{17,16},{25,24},{33,32},{41,40},{49,48},{57,56},{65,64... | collective-permute-start | bytes 491528 | tf_op jit(solution)/shard_map/ppermute | solution.py:521
  183.9 5.1 %combine.1.refs_0_ = f32[16,32768]{1,0:T(8,128)} custom-call(f32[3,16,128]{2,1,0:T(8,128)} %get-tuple-element.19.coef_ref, f32[48,32768]{1,0:T(8,128)} %get-tuple-element.20.image_ref), custom_call_target="tpu_custom_call" | custom-call | tf_op jit(solution)/shard_map/combine/pallas_call | solution.py:374
  190.4 1.1 insert.1
  (107 shorter events, 12.1 us)
Async XLA Ops:
  0.6 16.2 %slice-start = ((f32[3,32768]{1,0:T(4,128)}), f32[3,15360]{1,0:T(4,128)S(1)}, s32[]{:S(2)}) async-start(f32[3,32768]{1,0:T(4,128)} %nodes_ref.3), calls=%async_computation.1 | async-start | bytes 491520 | tf_op jit(solution)/shard_map/slice | solution.py:486
  0.6 15.6 %copy-start.19 = (s32[128,9]{0,1:T(8,128)S(1)}, s32[128,9]{0,1:T(8,128)}, u32[]{:S(2)}) copy-start(s32[128,9]{0,1:T(8,128)} %param.9) | copy-start | bytes 13828
  1.8 15.3 %copy-start.10 = (f32[24,2048]{1,0:T(8,128)}, f32[24,2048]{1,0:T(8,128)S(1)}, u32[]{:S(2)}) copy-start(f32[24,2048]{1,0:T(8,128)S(1)} %pad_maximum_fusion.1.own_ref) | copy-start | bytes 589828
  1.8 15.3 %collective-permute-start = (f32[24,2048]{1,0:T(8,128)S(1)}, f32[24,2048]{1,0:T(8,128)S(1)}, u32[]{:S(2)}, u32[]{:S(2)}) collective-permute-start(f32[24,2048]{1,0:T(8,128)S(1)} %pad_maximum_fusion.1.own_ref), channel_id=1, source_target_pairs={{0,8},{8,16},{16,24},{24,32},{32,40},{40,48},{48,56},{56,64},{64,7... | collective-permute-start | bytes 589832 | tf_op jit(solution)/shard_map/ppermute | solution.py:472
  7.8 9.2 %collective-permute-start.1 = (f32[24,2048]{1,0:T(8,128)S(1)}, f32[24,2048]{1,0:T(8,128)S(1)}, u32[]{:S(2)}, u32[]{:S(2)}) collective-permute-start(f32[24,2048]{1,0:T(8,128)S(1)} %pad_maximum_fusion.1.own_ref), channel_id=1, source_target_pairs={{8,0},{16,8},{24,16},{32,24},{40,32},{48,40},{56,48},{64,56},{72,6... | collective-permute-start | bytes 589832 | tf_op jit(solution)/shard_map/ppermute | solution.py:481
  11.2 14.1 %copy-start.2 = (bf16[8,48,256]{2,1,0:T(8,128)(2,1)S(1)}, bf16[8,48,256]{2,1,0:T(8,128)(2,1)}, u32[]{:S(2)}) copy-start(bf16[8,48,256]{2,1,0:T(8,128)(2,1)} %prepare_nodes.3.left_ref.refs_2_) | copy-start | bytes 589828
  11.2 14.1 %copy-start.3 = (f32[16,2048]{1,0:T(8,128)S(1)}, f32[16,2048]{1,0:T(8,128)}, u32[]{:S(2)}) copy-start(f32[16,2048]{1,0:T(8,128)} %v0_ref.1) | copy-start | bytes 393220
  20.5 23.4 %copy-start.1 = (bf16[24,48,256]{2,1,0:T(8,128)(2,1)S(1)}, bf16[24,48,256]{2,1,0:T(8,128)(2,1)}, u32[]{:S(2)}) copy-start(bf16[24,48,256]{2,1,0:T(8,128)(2,1)} %prepare_centres.1.right_ref) | copy-start | bytes 1769476
  20.6 21.4 %collective-permute-start.3 = (f32[4,5120]{1,0:T(4,128)S(1)}, f32[4,5120]{1,0:T(4,128)S(1)}, u32[]{:S(2)}, u32[]{:S(2)}) collective-permute-start(f32[4,5120]{1,0:T(4,128)S(1)} %get-tuple-element.24), channel_id=1, source_target_pairs={{0,2},{8,10},{16,18},{24,26},{32,34},{40,42},{48,50},{56,58},{64,6... | collective-permute-start | bytes 245768 | tf_op jit(solution)/shard_map/ppermute | solution.py:493
  21.4 20.6 %collective-permute-start.4 = (f32[4,5120]{1,0:T(4,128)S(1)}, f32[4,5120]{1,0:T(4,128)S(1)}, u32[]{:S(2)}, u32[]{:S(2)}) collective-permute-start(f32[4,5120]{1,0:T(4,128)S(1)} %get-tuple-element.25), channel_id=1, source_target_pairs={{0,6},{8,14},{16,22},{24,30},{32,38},{40,46},{48,54},{56,62},{64,7... | collective-permute-start | bytes 245768 | tf_op jit(solution)/shard_map/ppermute | solution.py:493
  22.0 19.9 %collective-permute-start.2 = (f32[4,5120]{1,0:T(4,128)S(1)}, f32[4,5120]{1,0:T(4,128)S(1)}, u32[]{:S(2)}, u32[]{:S(2)}) collective-permute-start(f32[4,5120]{1,0:T(4,128)S(1)} %get-tuple-element.26), channel_id=1, source_target_pairs={{0,1},{8,9},{16,17},{24,25},{32,33},{40,41},{48,49},{56,57},{64,65... | collective-permute-start | bytes 245768 | tf_op jit(solution)/shard_map/ppermute | solution.py:493
  24.3 39.1 %copy-start.6 = (f32[16,2048]{1,0:T(8,128)}, f32[16,2048]{1,0:T(8,128)S(1)}, u32[]{:S(2)}) copy-start(f32[16,2048]{1,0:T(8,128)S(1)} %slice.53.after_ref.refs_9_) | copy-start | bytes 393220
  25.2 38.1 %copy-start.7 = (f32[16,2048]{1,0:T(8,128)}, f32[16,2048]{1,0:T(8,128)S(1)}, u32[]{:S(2)}) copy-start(f32[16,2048]{1,0:T(8,128)S(1)} %slice.52.before_ref.refs_3_) | copy-start | bytes 393220
  33.1 30.2 %copy-start.4 = (f32[16,2048]{1,0:T(8,128)}, f32[16,2048]{1,0:T(8,128)S(1)}, u32[]{:S(2)}) copy-start(f32[16,2048]{1,0:T(8,128)S(1)} %operator.2.own_ref.refs_7_.v1_ref) | copy-start | bytes 393220
  33.2 10.8 %collective-permute-start.6 = (f32[16,2048]{1,0:T(8,128)S(1)}, f32[16,2048]{1,0:T(8,128)S(1)}, u32[]{:S(2)}, u32[]{:S(2)}) collective-permute-start(f32[16,2048]{1,0:T(8,128)S(1)} %operator.2.own_ref.refs_7_.v1_ref), channel_id=1, source_target_pairs={{8,0},{16,8},{24,16},{32,24},{40,32},{48,40},{56,48},{64,56},{72,6... | collective-permute-start | bytes 393224 | tf_op jit(solution)/shard_map/ppermute | solution.py:507
  34.5 9.5 %collective-permute-start.5 = (f32[16,2048]{1,0:T(8,128)S(1)}, f32[16,2048]{1,0:T(8,128)S(1)}, u32[]{:S(2)}, u32[]{:S(2)}) collective-permute-start(f32[16,2048]{1,0:T(8,128)S(1)} %operator.2.own_ref.refs_7_.v1_ref), channel_id=1, source_target_pairs={{0,8},{8,16},{16,24},{24,32},{32,40},{40,48},{48,56},{56,64},{64,7... | collective-permute-start | bytes 393224 | tf_op jit(solution)/shard_map/ppermute | solution.py:507
  42.0 18.8 %copy-start.13 = (f32[4,5120]{1,0:T(4,128)}, f32[4,5120]{1,0:T(4,128)S(1)}, u32[]{:S(2)}) copy-start(f32[4,5120]{1,0:T(4,128)S(1)} %add_add_fusion) | copy-start | bytes 245764
  44.0 19.4 %copy-start.8 = (f32[16,2048]{1,0:T(8,128)}, f32[16,2048]{1,0:T(8,128)S(1)}, u32[]{:S(2)}) copy-start(f32[16,2048]{1,0:T(8,128)S(1)} %collective-permute-done.6.after_ref.refs_10_) | copy-start | bytes 393220
  44.0 19.4 %copy-start.9 = (f32[16,2048]{1,0:T(8,128)}, f32[16,2048]{1,0:T(8,128)S(1)}, u32[]{:S(2)}) copy-start(f32[16,2048]{1,0:T(8,128)S(1)} %collective-permute-done.5.before_ref.refs_4_) | copy-start | bytes 393220
  50.8 12.6 %collective-permute-start.8 = (f32[16,2048]{1,0:T(8,128)S(1)}, f32[16,2048]{1,0:T(8,128)S(1)}, u32[]{:S(2)}, u32[]{:S(2)}) collective-permute-start(f32[16,2048]{1,0:T(8,128)S(1)} %operator.3.refs_8_.v2_ref), channel_id=1, source_target_pairs={{8,0},{16,8},{24,16},{32,24},{40,32},{48,40},{56,48},{64,56},{72,6... | collective-permute-start | bytes 393224 | tf_op jit(solution)/shard_map/ppermute | solution.py:509
  52.1 11.3 %collective-permute-start.7 = (f32[16,2048]{1,0:T(8,128)S(1)}, f32[16,2048]{1,0:T(8,128)S(1)}, u32[]{:S(2)}, u32[]{:S(2)}) collective-permute-start(f32[16,2048]{1,0:T(8,128)S(1)} %operator.3.refs_8_.v2_ref), channel_id=1, source_target_pairs={{0,8},{8,16},{16,24},{24,32},{32,40},{40,48},{48,56},{56,64},{64,7... | collective-permute-start | bytes 393224 | tf_op jit(solution)/shard_map/ppermute | solution.py:509
  179.6 9.4 %collective-permute-start.11 = (bf16[16,5120]{1,0:T(8,128)(2,1)}, bf16[16,5120]{1,0:T(8,128)(2,1)S(1)}, u32[]{:S(2)}, u32[]{:S(2)}) collective-permute-start(bf16[16,5120]{1,0:T(8,128)(2,1)} %get-tuple-element.21), channel_id=1, source_target_pairs={{6,0},{14,8},{22,16},{30,24},{38,32},{46,40},{54,48},{62,56},{70,6... | collective-permute-start | bytes 491528 | tf_op jit(solution)/shard_map/ppermute | solution.py:521
  180.2 8.8 %collective-permute-start.10 = (bf16[16,5120]{1,0:T(8,128)(2,1)}, bf16[16,5120]{1,0:T(8,128)(2,1)S(1)}, u32[]{:S(2)}, u32[]{:S(2)}) collective-permute-start(bf16[16,5120]{1,0:T(8,128)(2,1)} %get-tuple-element.21), channel_id=1, source_target_pairs={{2,0},{10,8},{18,16},{26,24},{34,32},{42,40},{50,48},{58,56},{66,6... | collective-permute-start | bytes 491528 | tf_op jit(solution)/shard_map/ppermute | solution.py:521
  180.9 8.1 %collective-permute-start.9 = (bf16[16,5120]{1,0:T(8,128)(2,1)}, bf16[16,5120]{1,0:T(8,128)(2,1)S(1)}, u32[]{:S(2)}, u32[]{:S(2)}) collective-permute-start(bf16[16,5120]{1,0:T(8,128)(2,1)} %get-tuple-element.21), channel_id=1, source_target_pairs={{1,0},{9,8},{17,16},{25,24},{33,32},{41,40},{49,48},{57,56},{65,64... | collective-permute-start | bytes 491528 | tf_op jit(solution)/shard_map/ppermute | solution.py:521
  (9 other events, 18.4 us)

commit v3 on v2

--- a/solution.py
+++ b/solution.py
@@ -128,10 +128,14 @@
     lax.fori_loop(0, group_count, step, 0)
 
 
+def modes_of(ref):
+    return ref[ref.shape[0] - MODES :, :]
+
+
 def fill_weights(weight_ref, fields, per):
     width = 2 * MODES * len(fields[0])
     for k, refs in enumerate(fields):
-        stack = jnp.concatenate([r[...].astype(f32) for r in refs], axis=0) * 4.0
+        stack = jnp.concatenate([modes_of(r).astype(f32) for r in refs], axis=0) * 4.0
         high = stack.astype(bf16).astype(f32)
         low = stack - high
         rows = jnp.concatenate(
@@ -241,7 +245,7 @@
         return gram
 
     def steps_of(count):
-        return next(n for n in (4, 5, 3, 2, 1) if count % n == 0)
+        return next(n for n in (8, 4, 5, 3, 2, 1) if count % n == 0)
 
     n = steps_of(guests)
     gram = lax.fori_loop(0, guests // n, functools.partial(finish, own, guest_ref, sent.at[1], n), zeros)
@@ -445,11 +449,11 @@
     return [(i, i + 1) for i in range(count - 1)], [(i + 1, i) for i in range(count - 1)]
 
 
-MOVED_SHARE = 20 / 128
+MOVED_SHARE = 1 / 8
 
 
 def helper_turns(count):
-    return (1, 2, count - 2) if count >= 6 else (1,)
+    return (1, 2, count - 2, count - 1) if count >= 6 else (1,)
 
 
 def per_device(centres, mode_shapes, neighbours, volume_nodes, supports):
@@ -475,16 +479,22 @@
         return jnp.where(ids >= 0, jnp.clip(ids - offset, 0, kinds - 1), -1)
 
     own_places = place_of(neighbours)
-    own_list = work_list(own_places, 3, 4, kinds)
+    own_list = work_list(own_places, 3, 8, kinds)
     own_left = prepare_nodes(centres, centres)
     again, own_left = lax.optimization_barrier((packed, own_left))
     after = lax.ppermute(again, "surf", down)
     left = prepare_nodes(centres, volume_nodes)
 
     right = prepare_centres(before, packed, after)
+    v0 = mode_shapes
+    v1 = apply_operator(8, 3, own_list, own_left, right, before, v0, after)
+    v1_low = v1.astype(bf16)
+    v1_before = lax.ppermute(v1_low, "surf", up)
+    v1_after = lax.ppermute(v1_low, "surf", down)
+
     ids = jnp.pad(supports[kept:].astype(f32), ((0, 0), (0, BLK - slots))).reshape(1, -1)
     parcel = jnp.concatenate([volume_nodes[:, kept * BLK :], ids], axis=0)
-    parcel, right = lax.optimization_barrier((parcel, right))
+    parcel, v1_before = lax.optimization_barrier((parcel, v1_before))
     width = moved * BLK
     got = jnp.zeros((4, width), f32)
     helping = False
@@ -498,23 +508,21 @@
     tile_places = jnp.where(kept_here[:, None], place_of(supports), -1)
     check_places = lax.dynamic_slice_in_dim(own_places, turn * checks, checks, axis=0)
     places = jnp.concatenate([tile_places, guest_places, check_places], axis=0)
-    whole_list = work_list(places, 4, 4, kinds)
+    whole_list = work_list(places, 2, 10, kinds)
     guest_left = prepare_nodes(centres, got[:3])
 
-    v0 = mode_shapes
-    v0_before, v0_after = before[8:], after[8:]
-    v1 = apply_operator(4, 3, own_list, own_left, right, v0_before, v0, v0_after)
-    v1_before, v1_after = lax.ppermute(v1, "surf", up), lax.ppermute(v1, "surf", down)
-    v2 = apply_operator(4, 3, own_list, own_left, right, v1_before, v1, v1_after)
-    v2_before, v2_after = lax.ppermute(v2, "surf", up), lax.ppermute(v2, "surf", down)
+    v2 = apply_operator(8, 3, own_list, own_left, right, v1_before, v1, v1_after)
+    v2_low = v2.astype(bf16)
+    v2_before = lax.ppermute(v2_low, "surf", up)
+    v2_after = lax.ppermute(v2_low, "surf", down)
     fields = (
-        (v0_before, v1_before, v2_before),
+        (before, v1_before, v2_before),
         (v0, v1, v2),
-        (v0_after, v1_after, v2_after),
+        (after, v1_after, v2_after),
     )
     lefts = (left, guest_left, own_left)
     images, guests, sums = volume_images(
-        4, 4, whole_list, turns, right, lefts, checks, fields, devices, share
+        10, 2, whole_list, turns, right, lefts, checks, fields, devices, share
     )
     sums = lax.all_to_all(sums, ("surf", "vol"), 0, 0, tiled=True)
     weights, coef, away = settle(sums, (v0, v1, v2), guests, total_nodes)

time: 192 us -> 183 us (0.953)
  Pallas kernels: 102 us -> 92.6 us
  blocking collectives: 43 us -> 38.8 us
    pallas_call x1, Pallas kernels: 69.8 us -> 61.7 us  [volume_images(): pl.pallas_call(functools.partial(volume_kernel, unroll, together, (own, g...]
    all_to_all x1, blocking collectives: 43 us -> 38.8 us  [per_device(): sums = lax.all_to_all(sums, ('surf', 'vol'), 0, 0, tiled=True)]
    unnamed x45 -> x47, local copies, waits for them, and re-layouts: 5.51 us -> 8.33 us
    ppermute x3 -> x4, starting transfers between devices: 4.36 us -> 5.75 us  [per_device(): parts = [lax.ppermute(away, 'vol', [(helper, 0)]) for helper in helpers]]
  transfers between devices with their start and end apart: 12 -> 14, of which waited for: 0 -> 1; matrix products, arithmetic and copies ran while one was open for 4% -> 4% of each run, Pallas kernels for 10% -> 10%
where the time goes in v3:
time: 183 us; the launch traced here: 182 us
  Pallas kernels  92.6 us (51%)
  blocking collectives  38.8 us (21%)
  starting transfers between devices  31.6 us (17%)
  local copies, waits for them, and re-layouts  9.85 us (5%)
  other arithmetic  4.79 us (3%)
  between operations  2.68 us (1%)
    pallas_call x1, Pallas kernels, volume_images(): pl.pallas_call(functools.partial(volume_kernel, unroll, together, (own, g...  61.7 us
    all_to_all x1, blocking collectives, per_device(): sums = lax.all_to_all(sums, ('surf', 'vol'), 0, 0, tiled=True)  38.8 us
    pallas_call x2, Pallas kernels, apply_operator(): pl.pallas_call(functools.partial(operator_kernel, unroll, together, tiles...  12.3 us
    unnamed x47, local copies, waits for them, and re-layouts  8.33 us
    ppermute x1, starting transfers between devices, per_device(): v2_before = lax.ppermute(v2_low, 'surf', up)  7.75 us
    pallas_call x3, Pallas kernels, prepare_nodes(): pl.pallas_call(node_kernel, grid=(tiles // step,), in_specs=[pl.BlockSpec...  7.74 us
    ppermute x1, starting transfers between devices, per_device(): v1_before = lax.ppermute(v1_low, 'surf', up)  6.54 us
    ppermute x4, starting transfers between devices, per_device(): parts = [lax.ppermute(away, 'vol', [(helper, 0)]) for helper in helpers]  5.75 us
  transfers between devices with their start and end apart: 14, of which 1 were waited for; matrix products, arithmetic and copies ran while one was open for 4% of the time, Pallas kernels for 10%

profile of v3, /device:TPU:1, one launch (start us, length us, event | category | flops | bytes accessed | tf_op | source)
XLA Modules:
  0.0 181.6 jit_solution(15213195802196777258)
XLA Ops:
  0.7 1.0 pad_maximum_fusion.1.own_ref
  1.7 4.4 %collective-permute-start = (f32[24,2048]{1,0:T(8,128)S(1)}, f32[24,2048]{1,0:T(8,128)S(1)}, u32[]{:S(2)}, u32[]{:S(2)}) collective-permute-start(f32[24,2048]{1,0:T(8,128)S(1)} %pad_maximum_fusion.1.own_ref), channel_id=1, source_target_pairs={{0,8},{8,16},{16,24},{24,32},{32,40},{40,48},{48,56},{56,64},{64,7... | collective-permute-start | bytes 589832 | tf_op jit(solution)/shard_map/ppermute | solution.py:476
  6.1 1.6 prepare_nodes.3.left_ref.refs_2_
  7.8 1.3 collective-permute-start.1
  11.2 4.3 %prepare_nodes.4.refs_0_ = bf16[128,48,256]{2,1,0:T(8,128)(2,1)} custom-call(f32[3,2048]{1,0:T(4,128)} %centres_ref.5, f32[3,32768]{1,0:T(4,128)} %nodes_ref.3), custom_call_target="tpu_custom_call" | custom-call | tf_op jit(solution)/shard_map/prepare_nodes/pallas_call | solution.py:57
  18.4 2.1 %prepare_centres.1.right_ref = bf16[24,48,256]{2,1,0:T(8,128)(2,1)} custom-call(f32[24,2048]{1,0:T(8,128)} %copy-done.6, f32[24,2048]{1,0:T(8,128)} %copy-done.12, f32[24,2048]{1,0:T(8,128)} %copy-done.8), custom_call_target="tpu_custom_call" | custom-call | tf_op jit(solution)/shard_map/prepare_centres/pallas_call | solution.py:83
  20.5 1.1 copy-done
  21.6 0.9 copy-done.7
  22.5 0.9 copy-done.9
  23.4 6.2 %operator.2.own_ref.refs_7_.v1_ref = f32[16,2048]{1,0:T(8,128)S(1)} custom-call(s32[1]{0:T(128)} %bitcast.count_ref, s32[40]{0:T(128)S(1)} %select_reduce_fusion.4.place_ref, s32[120]{0:T(128)S(1)} %reshape.137.member_ref, bf16[8,48,256]{2,1,0:T(8,128)(2,1)S(1)} %copy-done.3, bf16[24,48,256]{2,1,0:T(8,128)(2,1)S(1)} %copy-done, f32[24,2048]{1,0:T(8,128)S(1)} %copy-done.7, ...), custom_call_target="tpu_custom_call" | custom-call | tf_op jit(solution)/shard_map/operator/pallas_call | solution.py:167
  29.6 6.5 %collective-permute-start.2 = (bf16[16,2048]{1,0:T(8,128)(2,1)S(1)}, bf16[16,2048]{1,0:T(8,128)(2,1)S(1)}, u32[]{:S(2)}, u32[]{:S(2)}) collective-permute-start(bf16[16,2048]{1,0:T(8,128)(2,1)S(1)} %convert_element_type.81), channel_id=1, source_target_pairs={{0,8},{8,16},{16,24},{24,32},{32,40},{40,48},{48,56},{56,64},{64,7... | collective-permute-start | bytes 196616 | tf_op jit(solution)/shard_map/ppermute | solution.py:492
  36.2 1.3 collective-permute-start.7
  39.5 1.3 collective-permute-start.3
  41.4 1.1 copy-done.1
  42.4 6.2 %operator.3.refs_8_.v2_ref = f32[16,2048]{1,0:T(8,128)S(1)} custom-call(s32[1]{0:T(128)} %bitcast.count_ref, s32[40]{0:T(128)S(1)} %select_reduce_fusion.4.place_ref, s32[120]{0:T(128)S(1)} %reshape.137.member_ref, bf16[8,48,256]{2,1,0:T(8,128)(2,1)S(1)} %copy-done.3, bf16[24,48,256]{2,1,0:T(8,128)(2,1)S(1)} %copy-done.1, ...), custom_call_target="tpu_custom_call" | custom-call | tf_op jit(solution)/shard_map/operator/pallas_call | solution.py:167
  48.6 1.3 collective-permute-start.9
  49.9 7.7 %collective-permute-start.8 = (bf16[16,2048]{1,0:T(8,128)(2,1)S(1)}, bf16[16,2048]{1,0:T(8,128)(2,1)S(1)}, u32[]{:S(2)}, u32[]{:S(2)}) collective-permute-start(bf16[16,2048]{1,0:T(8,128)(2,1)S(1)} %convert_element_type.87), channel_id=1, source_target_pairs={{0,8},{8,16},{16,24},{24,32},{32,40},{40,48},{48,56},{56,64},{64,7... | collective-permute-start | bytes 196616 | tf_op jit(solution)/shard_map/ppermute | solution.py:516
  60.3 1.8 prepare_nodes.5.refs_1_
  65.0 61.7 %volume.1 = (f32[48,32768]{1,0:T(8,128)}, f32[48,4096]{1,0:T(8,128)}, f32[256,2,128]{2,1,0:T(2,128)}) custom-call(s32[1]{0:T(128)} %bitcast.4.count_ref, s32[670]{0:T(1024)} %select_reduce_fusion.1.place_ref, s32[1340]{0:T(1024)} %reshape.139.member_ref, s32[1]{0:T(128)} %bitcast.6.turn_ref, bf16[24,48,256]{2,1,0:T(8,128)(2,1)} %prepare_centres.1.right_ref, ...), custom_call_target="tpu_custom_call" | custom-call | tf_op jit(solution)/shard_map/volume/pallas_call | solution.py:279
  126.7 38.8 %all_to_all.5.sums_ref = f32[256,2,128]{2,1,0:T(2,128)} all-to-all(f32[256,2,128]{2,1,0:T(2,128)} %get-tuple-element.16), channel_id=1, replica_groups=mesh['surf'=32,'vol'=8] {'surf','vol'}, dimensions={0} | all-to-all | bytes 524288 | tf_op jit(solution)/shard_map/all_to_all | solution.py:527
  165.5 2.6 %settle.1 = (f32[16,2048]{1,0:T(8,128)}, f32[3,16,128]{2,1,0:T(8,128)}, bf16[16,4096]{1,0:T(8,128)(2,1)}) custom-call(f32[256,2,128]{2,1,0:T(2,128)} %all_to_all.5.sums_ref, f32[16,2048]{1,0:T(8,128)} %v0_ref.1, f32[16,2048]{1,0:T(8,128)} %copy-done.2, f32[16,2048]{1,0:T(8,128)} %copy-done.5, f32[48,4096]{1,0:T(8,128)} %get-tuple-element.17.guest_ref), custom_call_target="tpu_custom_call" | custom-call | tf_op jit(solution)/shard_map/settle/pallas_call | solution.py:358
  170.1 3.8 %collective-permute-start.10 = (bf16[16,4096]{1,0:T(8,128)(2,1)}, bf16[16,4096]{1,0:T(8,128)(2,1)S(1)}, u32[]{:S(2)}, u32[]{:S(2)}) collective-permute-start(bf16[16,4096]{1,0:T(8,128)(2,1)} %get-tuple-element.21), channel_id=1, source_target_pairs={{1,0},{9,8},{17,16},{25,24},{33,32},{41,40},{49,48},{57,56},{65,64... | collective-permute-start | bytes 393224 | tf_op jit(solution)/shard_map/ppermute | solution.py:529
  173.8 5.1 %combine.1.refs_0_ = f32[16,32768]{1,0:T(8,128)} custom-call(f32[3,16,128]{2,1,0:T(8,128)} %get-tuple-element.19.coef_ref, f32[48,32768]{1,0:T(8,128)} %get-tuple-element.20.image_ref), custom_call_target="tpu_custom_call" | custom-call | tf_op jit(solution)/shard_map/combine/pallas_call | solution.py:378
  180.3 1.1 insert.1
  (113 shorter events, 14.9 us)
Async XLA Ops:
  0.6 16.2 %slice-start = ((f32[3,32768]{1,0:T(4,128)}), f32[3,16384]{1,0:T(4,128)S(1)}, s32[]{:S(2)}) async-start(f32[3,32768]{1,0:T(4,128)} %nodes_ref.3), calls=%async_computation.1 | async-start | bytes 524288 | tf_op jit(solution)/shard_map/slice | solution.py:496
  0.6 15.6 %copy-start.20 = (s32[128,9]{0,1:T(8,128)S(1)}, s32[128,9]{0,1:T(8,128)}, u32[]{:S(2)}) copy-start(s32[128,9]{0,1:T(8,128)} %param.9) | copy-start | bytes 13828
  1.7 15.3 %copy-start.12 = (f32[24,2048]{1,0:T(8,128)}, f32[24,2048]{1,0:T(8,128)S(1)}, u32[]{:S(2)}) copy-start(f32[24,2048]{1,0:T(8,128)S(1)} %pad_maximum_fusion.1.own_ref) | copy-start | bytes 589828
  1.7 15.3 %collective-permute-start = (f32[24,2048]{1,0:T(8,128)S(1)}, f32[24,2048]{1,0:T(8,128)S(1)}, u32[]{:S(2)}, u32[]{:S(2)}) collective-permute-start(f32[24,2048]{1,0:T(8,128)S(1)} %pad_maximum_fusion.1.own_ref), channel_id=1, source_target_pairs={{0,8},{8,16},{16,24},{24,32},{32,40},{40,48},{48,56},{56,64},{64,7... | collective-permute-start | bytes 589832 | tf_op jit(solution)/shard_map/ppermute | solution.py:476
  7.8 9.2 %collective-permute-start.1 = (f32[24,2048]{1,0:T(8,128)S(1)}, f32[24,2048]{1,0:T(8,128)S(1)}, u32[]{:S(2)}, u32[]{:S(2)}) collective-permute-start(f32[24,2048]{1,0:T(8,128)S(1)} %pad_maximum_fusion.1.own_ref), channel_id=1, source_target_pairs={{8,0},{16,8},{24,16},{32,24},{40,32},{48,40},{56,48},{64,56},{72,6... | collective-permute-start | bytes 589832 | tf_op jit(solution)/shard_map/ppermute | solution.py:485
  11.2 9.3 %copy-start.3 = (bf16[8,48,256]{2,1,0:T(8,128)(2,1)S(1)}, bf16[8,48,256]{2,1,0:T(8,128)(2,1)}, u32[]{:S(2)}) copy-start(bf16[8,48,256]{2,1,0:T(8,128)(2,1)} %prepare_nodes.3.left_ref.refs_2_) | copy-start | bytes 589828
  11.2 9.3 %copy-start.4 = (f32[16,2048]{1,0:T(8,128)S(1)}, f32[16,2048]{1,0:T(8,128)}, u32[]{:S(2)}) copy-start(f32[16,2048]{1,0:T(8,128)} %v0_ref.1) | copy-start | bytes 393220
  29.6 34.8 %copy-start.2 = (f32[16,2048]{1,0:T(8,128)}, f32[16,2048]{1,0:T(8,128)S(1)}, u32[]{:S(2)}) copy-start(f32[16,2048]{1,0:T(8,128)S(1)} %operator.2.own_ref.refs_7_.v1_ref) | copy-start | bytes 393220
  29.6 7.9 %collective-permute-start.2 = (bf16[16,2048]{1,0:T(8,128)(2,1)S(1)}, bf16[16,2048]{1,0:T(8,128)(2,1)S(1)}, u32[]{:S(2)}, u32[]{:S(2)}) collective-permute-start(bf16[16,2048]{1,0:T(8,128)(2,1)S(1)} %convert_element_type.81), channel_id=1, source_target_pairs={{0,8},{8,16},{16,24},{24,32},{32,40},{40,48},{48,56},{56,64},{64,7... | collective-permute-start | bytes 196616 | tf_op jit(solution)/shard_map/ppermute | solution.py:492
  36.2 5.2 %collective-permute-start.7 = (bf16[16,2048]{1,0:T(8,128)(2,1)S(1)}, bf16[16,2048]{1,0:T(8,128)(2,1)S(1)}, u32[]{:S(2)}, u32[]{:S(2)}) collective-permute-start(bf16[16,2048]{1,0:T(8,128)(2,1)S(1)} %convert_element_type.81), channel_id=1, source_target_pairs={{8,0},{16,8},{24,16},{32,24},{40,32},{48,40},{56,48},{64,56},{72,6... | collective-permute-start | bytes 196616 | tf_op jit(solution)/shard_map/ppermute | solution.py:493
  37.5 26.9 %copy-start.10 = (bf16[16,2048]{1,0:T(8,128)(2,1)}, bf16[16,2048]{1,0:T(8,128)(2,1)S(1)}, u32[]{:S(2)}) copy-start(bf16[16,2048]{1,0:T(8,128)(2,1)S(1)} %collective-permute-done.2.before_ref.refs_4_) | copy-start | bytes 196612
  37.5 12.4 %collective-permute-start.4 = (f32[4,4096]{1,0:T(4,128)S(1)}, f32[4,4096]{1,0:T(4,128)S(1)}, u32[]{:S(2)}, u32[]{:S(2)}) collective-permute-start(f32[4,4096]{1,0:T(4,128)S(1)} %get-tuple-element.24), channel_id=1, source_target_pairs={{0,2},{8,10},{16,18},{24,26},{32,34},{40,42},{48,50},{56,58},{64,6... | collective-permute-start | bytes 196616 | tf_op jit(solution)/shard_map/ppermute | solution.py:503
  38.2 19.5 %collective-permute-start.6 = (f32[4,4096]{1,0:T(4,128)S(1)}, f32[4,4096]{1,0:T(4,128)S(1)}, u32[]{:S(2)}, u32[]{:S(2)}) collective-permute-start(f32[4,4096]{1,0:T(4,128)S(1)} %get-tuple-element.25), channel_id=1, source_target_pairs={{0,7},{8,15},{16,23},{24,31},{32,39},{40,47},{48,55},{56,63},{64,7... | collective-permute-start | bytes 196616 | tf_op jit(solution)/shard_map/ppermute | solution.py:503
  38.9 18.8 %collective-permute-start.5 = (f32[4,4096]{1,0:T(4,128)S(1)}, f32[4,4096]{1,0:T(4,128)S(1)}, u32[]{:S(2)}, u32[]{:S(2)}) collective-permute-start(f32[4,4096]{1,0:T(4,128)S(1)} %get-tuple-element.26), channel_id=1, source_target_pairs={{0,6},{8,14},{16,22},{24,30},{32,38},{40,46},{48,54},{56,62},{64,7... | collective-permute-start | bytes 196616 | tf_op jit(solution)/shard_map/ppermute | solution.py:503
  39.5 18.2 %collective-permute-start.3 = (f32[4,4096]{1,0:T(4,128)S(1)}, f32[4,4096]{1,0:T(4,128)S(1)}, u32[]{:S(2)}, u32[]{:S(2)}) collective-permute-start(f32[4,4096]{1,0:T(4,128)S(1)} %get-tuple-element.27), channel_id=1, source_target_pairs={{0,1},{8,9},{16,17},{24,25},{32,33},{40,41},{48,49},{56,57},{64,65... | collective-permute-start | bytes 196616 | tf_op jit(solution)/shard_map/ppermute | solution.py:503
  42.4 22.0 %copy-start.11 = (bf16[16,2048]{1,0:T(8,128)(2,1)}, bf16[16,2048]{1,0:T(8,128)(2,1)S(1)}, u32[]{:S(2)}) copy-start(bf16[16,2048]{1,0:T(8,128)(2,1)S(1)} %collective-permute-done.7.after_ref.refs_10_) | copy-start | bytes 196612
  48.6 15.8 %copy-start.5 = (f32[16,2048]{1,0:T(8,128)}, f32[16,2048]{1,0:T(8,128)S(1)}, u32[]{:S(2)}) copy-start(f32[16,2048]{1,0:T(8,128)S(1)} %operator.3.refs_8_.v2_ref) | copy-start | bytes 393220
  48.6 15.7 %collective-permute-start.9 = (bf16[16,2048]{1,0:T(8,128)(2,1)S(1)}, bf16[16,2048]{1,0:T(8,128)(2,1)S(1)}, u32[]{:S(2)}, u32[]{:S(2)}) collective-permute-start(bf16[16,2048]{1,0:T(8,128)(2,1)S(1)} %convert_element_type.87), channel_id=1, source_target_pairs={{8,0},{16,8},{24,16},{32,24},{40,32},{48,40},{56,48},{64,56},{72,6... | collective-permute-start | bytes 196616 | tf_op jit(solution)/shard_map/ppermute | solution.py:517
  49.9 14.4 %collective-permute-start.8 = (bf16[16,2048]{1,0:T(8,128)(2,1)S(1)}, bf16[16,2048]{1,0:T(8,128)(2,1)S(1)}, u32[]{:S(2)}, u32[]{:S(2)}) collective-permute-start(bf16[16,2048]{1,0:T(8,128)(2,1)S(1)} %convert_element_type.87), channel_id=1, source_target_pairs={{0,8},{8,16},{16,24},{24,32},{32,40},{40,48},{48,56},{56,64},{64,7... | collective-permute-start | bytes 196616 | tf_op jit(solution)/shard_map/ppermute | solution.py:516
  57.8 2.6 %copy-start.13 = (f32[4,4096]{1,0:T(4,128)}, f32[4,4096]{1,0:T(4,128)S(1)}, u32[]{:S(2)}) copy-start(f32[4,4096]{1,0:T(4,128)S(1)} %add_add_fusion) | copy-start | bytes 196612
  168.1 10.8 %collective-permute-start.13 = (bf16[16,4096]{1,0:T(8,128)(2,1)}, bf16[16,4096]{1,0:T(8,128)(2,1)S(1)}, u32[]{:S(2)}, u32[]{:S(2)}) collective-permute-start(bf16[16,4096]{1,0:T(8,128)(2,1)} %get-tuple-element.21), channel_id=1, source_target_pairs={{7,0},{15,8},{23,16},{31,24},{39,32},{47,40},{55,48},{63,56},{71,6... | collective-permute-start | bytes 393224 | tf_op jit(solution)/shard_map/ppermute | solution.py:529
  168.7 10.2 %collective-permute-start.12 = (bf16[16,4096]{1,0:T(8,128)(2,1)}, bf16[16,4096]{1,0:T(8,128)(2,1)S(1)}, u32[]{:S(2)}, u32[]{:S(2)}) collective-permute-start(bf16[16,4096]{1,0:T(8,128)(2,1)} %get-tuple-element.21), channel_id=1, source_target_pairs={{6,0},{14,8},{22,16},{30,24},{38,32},{46,40},{54,48},{62,56},{70,6... | collective-permute-start | bytes 393224 | tf_op jit(solution)/shard_map/ppermute | solution.py:529
  169.4 9.5 %collective-permute-start.11 = (bf16[16,4096]{1,0:T(8,128)(2,1)}, bf16[16,4096]{1,0:T(8,128)(2,1)S(1)}, u32[]{:S(2)}, u32[]{:S(2)}) collective-permute-start(bf16[16,4096]{1,0:T(8,128)(2,1)} %get-tuple-element.21), channel_id=1, source_target_pairs={{2,0},{10,8},{18,16},{26,24},{34,32},{42,40},{50,48},{58,56},{66,6... | collective-permute-start | bytes 393224 | tf_op jit(solution)/shard_map/ppermute | solution.py:529
  170.1 8.9 %collective-permute-start.10 = (bf16[16,4096]{1,0:T(8,128)(2,1)}, bf16[16,4096]{1,0:T(8,128)(2,1)S(1)}, u32[]{:S(2)}, u32[]{:S(2)}) collective-permute-start(bf16[16,4096]{1,0:T(8,128)(2,1)} %get-tuple-element.21), channel_id=1, source_target_pairs={{1,0},{9,8},{17,16},{25,24},{33,32},{41,40},{49,48},{57,56},{65,64... | collective-permute-start | bytes 393224 | tf_op jit(solution)/shard_map/ppermute | solution.py:529
  (12 other events, 9.3 us)

commit v4 on v3

--- a/solution.py
+++ b/solution.py
@@ -67,26 +67,15 @@
     )(centres, nodes)
 
 
-def centre_kernel(before_ref, own_ref, after_ref, out_ref):
+def fill_centres(out_ref, before_ref, own_ref, after_ref):
     per = own_ref.shape[1] // BLK
-    origin = own_ref[:, 0:1]
+    origin = own_ref[0:3, 0:1]
     for k, ref in enumerate((before_ref, own_ref, after_ref)):
-        points = (ref[0:3, :] - origin[0:3]) * (1.0 / RADIUS)
+        points = (ref[0:3, :] - origin) * (1.0 / RADIUS)
         a, b, c = split3(augmented(points, False))
         rows = jnp.concatenate([a, a, b, b, a, c], axis=0)
         for t in range(per):
             out_ref[k * per + t] = rows[:, t * BLK : (t + 1) * BLK].astype(bf16)
-
-
-def prepare_centres(before, own, after):
-    per = own.shape[1] // BLK
-    return pl.pallas_call(
-        centre_kernel,
-        in_specs=[whole(pltpu.VMEM)] * 3,
-        out_specs=whole(pltpu.VMEM),
-        out_shape=jax.ShapeDtypeStruct((3 * per, DEPTH, BLK), bf16),
-        name="prepare_centres",
-    )(before, own, after)
 
 
 def pl_reciprocal(x):
@@ -145,37 +134,43 @@
             weight_ref[k * per + t] = jnp.transpose(rows[:, t * BLK : (t + 1) * BLK]).astype(bf16)
 
 
-def operator_kernel(
-    unroll, together, tiles, count_ref, place_ref, member_ref, left_ref, right_ref,
-    before_ref, own_ref, after_ref, out_ref, weight_ref, total,
-):
+def operator_kernel(unroll, together, tiles, first, count_ref, place_ref, member_ref, left_ref, *refs):
+    if first:
+        before_ref, own_ref, after_ref, out_ref, right_ref, weight_ref, total = refs
+        fill_centres(right_ref, before_ref, own_ref, after_ref)
+    else:
+        right_ref, before_ref, own_ref, after_ref, out_ref, weight_ref, total = refs
     fill_weights(weight_ref, ((before_ref,), (own_ref,), (after_ref,)), tiles)
     clear(tiles, total)
     accumulate(
         unroll, together, tiles, count_ref[0], place_ref, member_ref, left_ref, right_ref,
         weight_ref, total,
     )
+    own = modes_of(own_ref)
     for t in range(tiles):
         image = jnp.transpose(total[t])
         sl = slice(t * BLK, (t + 1) * BLK)
-        out_ref[:, sl] = image[0:MODES] + image[MODES : 2 * MODES] + SHIFT * own_ref[:, sl]
+        out_ref[:, sl] = image[0:MODES] + image[MODES : 2 * MODES] + SHIFT * own[:, sl]
 
 
 def apply_operator(unroll, together, lists, left, right, before, own, after):
     tiles = own.shape[1] // BLK
     vmem, smem = whole(pltpu.VMEM), whole(pltpu.SMEM)
+    first = right is None
+    image = jax.ShapeDtypeStruct((MODES, own.shape[1]), f32)
+    factors = jax.ShapeDtypeStruct((3 * tiles, DEPTH, BLK), bf16)
     return pl.pallas_call(
-        functools.partial(operator_kernel, unroll, together, tiles),
-        in_specs=[smem] * 3 + [vmem] * 5,
-        out_specs=vmem,
-        out_shape=jax.ShapeDtypeStruct(own.shape, f32),
+        functools.partial(operator_kernel, unroll, together, tiles, first),
+        in_specs=[smem] * 3 + [vmem] * (4 if first else 5),
+        out_specs=(vmem, vmem) if first else vmem,
+        out_shape=(image, factors) if first else image,
         scratch_shapes=[
             pltpu.VMEM((3 * tiles, BLK, LANES), bf16),
             pltpu.VMEM((tiles + 1, BLK, LANES), f32),
         ],
         compiler_params=pltpu.CompilerParams(vmem_limit_bytes=40 * 2**20),
         name="operator",
-    )(*lists, left, right, before, own, after)
+    )(*lists, left, *(() if first else (right,)), before, own, after)
 
 
 def row_of(columns):
@@ -368,57 +363,38 @@
     )(sums, *vectors, guests)
 
 
-def combine_kernel(coef_ref, image_ref, out_ref):
-    out_ref[...] = blend([coef_ref[k][:, 0:1] for k in range(KRYLOV)], image_ref)
-
-
-def combine(coef, images):
+def combine_kernel(kept, turn_ref, coef_ref, image_ref, *refs):
+    parts, out_ref = refs[:-1], refs[-1]
+    step = pl.program_id(0)
+    elsewhere = (turn_ref[0] == 0) & (step >= kept)
+
+    @pl.when(jnp.logical_not(elsewhere))
+    def _():
+        out_ref[...] = blend([coef_ref[k][:, 0:1] for k in range(KRYLOV)], image_ref)
+
+    for k, part in enumerate(parts):
+
+        @pl.when(elsewhere & (step == kept + k))
+        def _(part=part):
+            out_ref[...] = part[...].astype(f32)
+
+
+def combine(turn, coef, images, parts, kept):
     nodes = images.shape[1]
-    width = 8192 if nodes % 8192 == 0 else nodes
+    width = parts[0].shape[1]
     return pl.pallas_call(
-        combine_kernel,
+        functools.partial(combine_kernel, kept // width),
         grid=(nodes // width,),
         in_specs=[
+            whole(pltpu.SMEM),
             pl.BlockSpec(coef.shape, lambda i: (0, 0, 0)),
             pl.BlockSpec((KRYLOV * MODES, width), lambda i: (0, i)),
-        ],
+        ]
+        + [pl.BlockSpec(part.shape, lambda i: (0, 0)) for part in parts],
         out_specs=pl.BlockSpec((MODES, width), lambda i: (0, i)),
         out_shape=jax.ShapeDtypeStruct((MODES, nodes), f32),
         name="combine",
-    )(coef, images)
-
-
-def insert_kernel(kept, turn_ref, *refs):
-    parts, out_ref, wide, sems = refs[1:-3], refs[-3], refs[-2], refs[-1]
-
-    @pl.when(turn_ref[0] == 0)
-    def _():
-        width = parts[0].shape[1]
-        copies = []
-        for k, part in enumerate(parts):
-            wide[k] = part[...].astype(f32)
-            target = out_ref.at[:, pl.ds((kept + k * width // BLK) * BLK, width)]
-            copy = pltpu.make_async_copy(wide.at[k], target, sems.at[k])
-            copy.start()
-            copies.append(copy)
-        for copy in copies:
-            copy.wait()
-
-
-def insert(turn, main, parts, kept):
-    vmem, far = whole(pltpu.VMEM), whole(pl.ANY)
-    return pl.pallas_call(
-        functools.partial(insert_kernel, kept),
-        in_specs=[whole(pltpu.SMEM), far] + [vmem] * len(parts),
-        out_specs=far,
-        out_shape=jax.ShapeDtypeStruct(main.shape, f32),
-        input_output_aliases={1: 0},
-        scratch_shapes=[
-            pltpu.VMEM((len(parts),) + parts[0].shape, f32),
-            pltpu.SemaphoreType.DMA((len(parts),)),
-        ],
-        name="insert",
-    )(turn, main, *parts)
+    )(turn, coef, images, *parts)
 
 
 def work_list(places, together, unroll, kinds):
@@ -481,16 +457,17 @@
     own_places = place_of(neighbours)
     own_list = work_list(own_places, 3, 8, kinds)
     own_left = prepare_nodes(centres, centres)
-    again, own_left = lax.optimization_barrier((packed, own_left))
+    again, own_left, own_list = lax.optimization_barrier((packed, own_left, own_list))
     after = lax.ppermute(again, "surf", down)
-    left = prepare_nodes(centres, volume_nodes)
-
-    right = prepare_centres(before, packed, after)
+
     v0 = mode_shapes
-    v1 = apply_operator(8, 3, own_list, own_left, right, before, v0, after)
+    v1, right = apply_operator(8, 3, own_list, own_left, None, before, packed, after)
     v1_low = v1.astype(bf16)
     v1_before = lax.ppermute(v1_low, "surf", up)
-    v1_after = lax.ppermute(v1_low, "surf", down)
+    later_nodes, again = lax.optimization_barrier((volume_nodes, v1_low))
+    left = prepare_nodes(centres, later_nodes)
+    again, left = lax.optimization_barrier((again, left))
+    v1_after = lax.ppermute(again, "surf", down)
 
     ids = jnp.pad(supports[kept:].astype(f32), ((0, 0), (0, BLK - slots))).reshape(1, -1)
     parcel = jnp.concatenate([volume_nodes[:, kept * BLK :], ids], axis=0)
@@ -502,6 +479,14 @@
         piece = parcel[:, k * width : (k + 1) * width]
         got = got + lax.ppermute(piece, "vol", [(0, helper)])
         helping = helping | (turn == helper)
+    v2 = apply_operator(8, 3, own_list, own_left, right, v1_before, v1, v1_after)
+    v2_low = v2.astype(bf16)
+    v2_before = lax.ppermute(v2_low, "surf", up)
+    got, again = lax.optimization_barrier((got, v2_low))
+    guest_left = prepare_nodes(centres, got[:3])
+    again, guest_left = lax.optimization_barrier((again, guest_left))
+    v2_after = lax.ppermute(again, "surf", down)
+
     guest_ids = got[3].reshape(moved, BLK)[:, :slots].astype(jnp.int32)
     guest_places = jnp.where(helping, place_of(guest_ids), -1)
     kept_here = (turn > 0) | (jnp.arange(tile_dev) < kept)
@@ -509,12 +494,6 @@
     check_places = lax.dynamic_slice_in_dim(own_places, turn * checks, checks, axis=0)
     places = jnp.concatenate([tile_places, guest_places, check_places], axis=0)
     whole_list = work_list(places, 2, 10, kinds)
-    guest_left = prepare_nodes(centres, got[:3])
-
-    v2 = apply_operator(8, 3, own_list, own_left, right, v1_before, v1, v1_after)
-    v2_low = v2.astype(bf16)
-    v2_before = lax.ppermute(v2_low, "surf", up)
-    v2_after = lax.ppermute(v2_low, "surf", down)
     fields = (
         (before, v1_before, v2_before),
         (v0, v1, v2),
@@ -527,7 +506,7 @@
     sums = lax.all_to_all(sums, ("surf", "vol"), 0, 0, tiled=True)
     weights, coef, away = settle(sums, (v0, v1, v2), guests, total_nodes)
     parts = [lax.ppermute(away, "vol", [(helper, 0)]) for helper in helpers]
-    return weights, insert(turns, combine(coef, images), parts, kept)
+    return weights, combine(turns, coef, images, parts, kept * BLK)
 
 
 def solution(mesh):

time: 183 us -> 185 us (1.011)
  waiting for transfers between devices: 0.56 us -> 8.21 us
  local copies, waits for them, and re-layouts: 9.85 us -> 5.87 us
    unnamed x47 -> x37, local copies, waits for them, and re-layouts: 8.33 us -> 3.33 us
    ppermute x1, waiting for transfers between devices: 0.01 us -> 3.46 us  [per_device(): after = lax.ppermute(again, 'surf', down)]
    ppermute x2, waiting for transfers between devices: 0.53 us -> 3.61 us  [the longest x1 1.84 us: per_device(): v1_after = lax.ppermute(again, 'surf', down)]
    pallas_call x3 -> x1, Pallas kernels: 8.32 us -> 7.13 us  [combine(): pl.pallas_call(functools.partial(combine_kernel, kept // width), grid=(no...]
  transfers between devices with their start and end apart: 14 -> 14, of which waited for: 1 -> 4; matrix products, arithmetic and copies ran while one was open for 4% -> 5% of each run, Pallas kernels for 10% -> 8%
where the time goes in v4:
time: 185 us; the launch traced here: 184 us
  Pallas kernels  91.6 us (50%)
  blocking collectives  38.8 us (21%)
  starting transfers between devices  29.8 us (16%)
  waiting for transfers between devices  8.21 us (4%)
  other arithmetic  6.18 us (3%)
  local copies, waits for them, and re-layouts  5.87 us (3%)
  between operations  2.46 us (1%)
    pallas_call x1, Pallas kernels, volume_images(): pl.pallas_call(functools.partial(volume_kernel, unroll, together, (own, g...  61.7 us
    all_to_all x1, blocking collectives, per_device(): sums = lax.all_to_all(sums, ('surf', 'vol'), 0, 0, tiled=True)  38.8 us
    pallas_call x2, Pallas kernels, apply_operator(): pl.pallas_call(functools.partial(operator_kernel, unroll, together, tiles...  12.5 us
    pallas_call x3, Pallas kernels, prepare_nodes(): pl.pallas_call(node_kernel, grid=(tiles // step,), in_specs=[pl.BlockSpec...  7.69 us
    pallas_call x1, Pallas kernels, combine(): pl.pallas_call(functools.partial(combine_kernel, kept // width), grid=(no...  7.13 us
    ppermute x1, starting transfers between devices, per_device(): v2_before = lax.ppermute(v2_low, 'surf', up)  6.63 us
    ppermute x1, starting transfers between devices, per_device(): v1_before = lax.ppermute(v1_low, 'surf', up)  5.93 us
    ppermute x4, starting transfers between devices, per_device(): parts = [lax.ppermute(away, 'vol', [(helper, 0)]) for helper in helpers]  5.75 us
  transfers between devices with their start and end apart: 14, of which 4 were waited for; matrix products, arithmetic and copies ran while one was open for 5% of the time, Pallas kernels for 8%

profile of v4, /device:TPU:1, one launch (start us, length us, event | category | flops | bytes accessed | tf_op | source)
XLA Modules:
  0.0 183.7 jit_solution(3722025809767011043)
XLA Ops:
  0.7 1.0 pad_maximum_fusion.1.refs_1_
  1.7 4.4 %collective-permute-start = (f32[24,2048]{1,0:T(8,128)S(1)}, f32[24,2048]{1,0:T(8,128)S(1)}, u32[]{:S(2)}, u32[]{:S(2)}) collective-permute-start(f32[24,2048]{1,0:T(8,128)S(1)} %pad_maximum_fusion.1.refs_1_), channel_id=1, source_target_pairs={{0,8},{8,16},{16,24},{24,32},{32,40},{40,48},{48,56},{56,64},{64,7... | collective-permute-start | bytes 589832 | tf_op jit(solution)/shard_map/ppermute | solution.py:452
  8.2 1.6 prepare_nodes.3.left_ref.refs_2_
  10.8 1.3 collective-permute-start.1
  13.2 1.0 slice.33
  15.1 3.5 %collective-permute-done.1.refs_2_.refs_9_ = f32[24,2048]{1,0:T(8,128)S(1)} collective-permute-done((f32[24,2048]{1,0:T(8,128)S(1)}, f32[24,2048]{1,0:T(8,128)S(1)}, u32[]{:S(2)}, u32[]{:S(2)}) %collective-permute-start.1) | collective-permute-done | bytes 196640 | tf_op jit(solution)/shard_map/ppermute | solution.py:461
  18.5 1.0 copy-done
  19.5 6.3 %operator.2 = (f32[16,2048]{1,0:T(8,128)S(1)}, bf16[24,48,256]{2,1,0:T(8,128)(2,1)S(1)}) custom-call(s32[1]{0:T(128)} %bitcast.count_ref, s32[40]{0:T(128)S(1)} %select_reduce_fusion.4.place_ref, s32[120]{0:T(128)S(1)} %reshape.137.member_ref, bf16[8,48,256]{2,1,0:T(8,128)(2,1)S(1)} %copy-done, f32[24,2048]{1,0:T(8,128)S(1)} %collective-permute-done.refs_0_.refs_3_, ...), custom_call_target="tpu_custom_call" | custom-call | tf_op jit(solution)/shard_map/operator/pallas_call | solution.py:162
  25.9 5.9 %collective-permute-start.2 = (bf16[16,2048]{1,0:T(8,128)(2,1)S(1)}, bf16[16,2048]{1,0:T(8,128)(2,1)S(1)}, u32[]{:S(2)}, u32[]{:S(2)}) collective-permute-start(bf16[16,2048]{1,0:T(8,128)(2,1)S(1)} %convert_element_type.81), channel_id=1, source_target_pairs={{0,8},{8,16},{16,24},{24,32},{32,40},{40,48},{48,56},{56,64},{64,7... | collective-permute-start | bytes 196616 | tf_op jit(solution)/shard_map/ppermute | solution.py:466
  31.8 4.3 %prepare_nodes.4.refs_0_ = bf16[128,48,256]{2,1,0:T(8,128)(2,1)} custom-call(f32[3,2048]{1,0:T(4,128)} %centres_ref.5, f32[3,32768]{1,0:T(4,128)} %nodes_ref.2), custom_call_target="tpu_custom_call" | custom-call | tf_op jit(solution)/shard_map/prepare_nodes/pallas_call | solution.py:57
  36.1 1.3 collective-permute-start.7
  39.4 1.3 collective-permute-start.3
  40.8 1.8 %collective-permute-done.7.refs_3_.refs_10_ = bf16[16,2048]{1,0:T(8,128)(2,1)S(1)} collective-permute-done((bf16[16,2048]{1,0:T(8,128)(2,1)S(1)}, bf16[16,2048]{1,0:T(8,128)(2,1)S(1)}, u32[]{:S(2)}, u32[]{:S(2)}) %collective-permute-start.7) | collective-permute-done | bytes 65568 | tf_op jit(solution)/shard_map/ppermute | solution.py:470
  42.6 6.2 %operator.3.refs_8_.v2_ref = f32[16,2048]{1,0:T(8,128)S(1)} custom-call(s32[1]{0:T(128)} %bitcast.count_ref, s32[40]{0:T(128)S(1)} %select_reduce_fusion.4.place_ref, s32[120]{0:T(128)S(1)} %reshape.137.member_ref, bf16[8,48,256]{2,1,0:T(8,128)(2,1)S(1)} %copy-done.1, bf16[24,48,256]{2,1,0:T(8,128)(2,1)S(1)} %get-tuple-element.32.refs_0_.right_ref, ...), custom_call_target="tpu_custom_call" | custom-call | tf_op jit(solution)/shard_map/operator/pallas_call | solution.py:162
  48.8 6.6 %collective-permute-start.8 = (bf16[16,2048]{1,0:T(8,128)(2,1)S(1)}, bf16[16,2048]{1,0:T(8,128)(2,1)S(1)}, u32[]{:S(2)}, u32[]{:S(2)}) collective-permute-start(bf16[16,2048]{1,0:T(8,128)(2,1)S(1)} %convert_element_type.82), channel_id=1, source_target_pairs={{0,8},{8,16},{16,24},{24,32},{32,40},{40,48},{48,56},{56,64},{64,7... | collective-permute-start | bytes 196616 | tf_op jit(solution)/shard_map/ppermute | solution.py:484
  58.1 1.8 prepare_nodes.5.refs_1_
  59.9 1.3 collective-permute-start.9
  63.4 1.8 collective-permute-done.9.refs_11_
  65.8 61.7 %volume.1 = (f32[48,32768]{1,0:T(8,128)}, f32[48,4096]{1,0:T(8,128)}, f32[256,2,128]{2,1,0:T(2,128)}) custom-call(s32[1]{0:T(128)} %bitcast.4.count_ref, s32[670]{0:T(1024)} %select_reduce_fusion.1.place_ref, s32[1340]{0:T(1024)} %reshape.139.member_ref, s32[1]{0:T(128)} %bitcast.6.turn_ref, bf16[24,48,256]{2,1,0:T(8,128)(2,1)} %copy-done.2, ...), custom_call_target="tpu_custom_call" | custom-call | tf_op jit(solution)/shard_map/volume/pallas_call | solution.py:274
  127.5 38.8 %all_to_all.5.sums_ref = f32[256,2,128]{2,1,0:T(2,128)} all-to-all(f32[256,2,128]{2,1,0:T(2,128)} %get-tuple-element.42), channel_id=1, replica_groups=mesh['surf'=32,'vol'=8] {'surf','vol'}, dimensions={0} | all-to-all | bytes 524288 | tf_op jit(solution)/shard_map/all_to_all | solution.py:506
  166.3 2.6 %settle.1 = (f32[16,2048]{1,0:T(8,128)}, f32[3,16,128]{2,1,0:T(8,128)}, bf16[16,4096]{1,0:T(8,128)(2,1)}) custom-call(f32[256,2,128]{2,1,0:T(2,128)} %all_to_all.5.sums_ref, f32[16,2048]{1,0:T(8,128)} %v0_ref.1, f32[16,2048]{1,0:T(8,128)} %copy-done.3, f32[16,2048]{1,0:T(8,128)} %copy-done.4, f32[48,4096]{1,0:T(8,128)} %get-tuple-element.43.guest_ref), custom_call_target="tpu_custom_call" | custom-call | tf_op jit(solution)/shard_map/settle/pallas_call | solution.py:353
  170.9 3.8 %collective-permute-start.10 = (bf16[16,4096]{1,0:T(8,128)(2,1)}, bf16[16,4096]{1,0:T(8,128)(2,1)S(1)}, u32[]{:S(2)}, u32[]{:S(2)}) collective-permute-start(bf16[16,4096]{1,0:T(8,128)(2,1)} %get-tuple-element.47), channel_id=1, source_target_pairs={{1,0},{9,8},{17,16},{25,24},{33,32},{41,40},{49,48},{57,56},{65,64... | collective-permute-start | bytes 393224 | tf_op jit(solution)/shard_map/ppermute | solution.py:508
  174.8 1.1 collective-permute-done.10.refs_0_
  176.5 7.1 %combine.1 = f32[16,32768]{1,0:T(8,128)} custom-call(s32[1]{0:T(128)} %bitcast.6.turn_ref, f32[3,16,128]{2,1,0:T(8,128)} %get-tuple-element.45.coef_ref, f32[48,32768]{1,0:T(8,128)} %get-tuple-element.46.image_ref, bf16[16,4096]{1,0:T(8,128)(2,1)} %copy-done.13, bf16[16,4096]{1,0:T(8,128)(2,1)} %copy-done.12, bf16[16,4096]{1,0:T(8,128)(2,1)} %copy-done.11, ...), custom_call_target="tpu_custom_call" | custom-call | tf_op jit(solution)/shard_map/combine/pallas_call | solution.py:385
  (100 shorter events, 13.8 us)
Async XLA Ops:
  1.7 16.8 %collective-permute-start = (f32[24,2048]{1,0:T(8,128)S(1)}, f32[24,2048]{1,0:T(8,128)S(1)}, u32[]{:S(2)}, u32[]{:S(2)}) collective-permute-start(f32[24,2048]{1,0:T(8,128)S(1)} %pad_maximum_fusion.1.refs_1_), channel_id=1, source_target_pairs={{0,8},{8,16},{16,24},{24,32},{32,40},{40,48},{48,56},{56,64},{64,7... | collective-permute-start | bytes 589832 | tf_op jit(solution)/shard_map/ppermute | solution.py:452
  10.8 7.7 %collective-permute-start.1 = (f32[24,2048]{1,0:T(8,128)S(1)}, f32[24,2048]{1,0:T(8,128)S(1)}, u32[]{:S(2)}, u32[]{:S(2)}) collective-permute-start(f32[24,2048]{1,0:T(8,128)S(1)} %pad_maximum_fusion.1.refs_1_), channel_id=1, source_target_pairs={{8,0},{16,8},{24,16},{32,24},{40,32},{48,40},{56,48},{64,56},{72,6... | collective-permute-start | bytes 589832 | tf_op jit(solution)/shard_map/ppermute | solution.py:461
  13.2 29.4 %copy-start.1 = (bf16[8,48,256]{2,1,0:T(8,128)(2,1)S(1)}, bf16[8,48,256]{2,1,0:T(8,128)(2,1)}, u32[]{:S(2)}) copy-start(bf16[8,48,256]{2,1,0:T(8,128)(2,1)} %prepare_nodes.3.left_ref.refs_2_) | copy-start | bytes 589828
  18.5 30.3 %copy-start.6 = (f32[24,2048]{1,0:T(8,128)}, f32[24,2048]{1,0:T(8,128)S(1)}, u32[]{:S(2)}) copy-start(f32[24,2048]{1,0:T(8,128)S(1)} %collective-permute-done.1.refs_2_.refs_9_) | copy-start | bytes 589828
  19.5 29.3 %copy-start.5 = (f32[24,2048]{1,0:T(8,128)}, f32[24,2048]{1,0:T(8,128)S(1)}, u32[]{:S(2)}) copy-start(f32[24,2048]{1,0:T(8,128)S(1)} %collective-permute-done.refs_0_.refs_3_) | copy-start | bytes 589828
  25.8 30.0 %copy-start.2 = (bf16[24,48,256]{2,1,0:T(8,128)(2,1)}, bf16[24,48,256]{2,1,0:T(8,128)(2,1)S(1)}, u32[]{:S(2)}) copy-start(bf16[24,48,256]{2,1,0:T(8,128)(2,1)S(1)} %get-tuple-element.32.refs_0_.right_ref) | copy-start | bytes 1769476
  25.8 30.0 %copy-start.3 = (f32[16,2048]{1,0:T(8,128)}, f32[16,2048]{1,0:T(8,128)S(1)}, u32[]{:S(2)}) copy-start(f32[16,2048]{1,0:T(8,128)S(1)} %get-tuple-element.30.refs_2_.refs_7_.v1_ref) | copy-start | bytes 393220
  25.9 11.5 %collective-permute-start.2 = (bf16[16,2048]{1,0:T(8,128)(2,1)S(1)}, bf16[16,2048]{1,0:T(8,128)(2,1)S(1)}, u32[]{:S(2)}, u32[]{:S(2)}) collective-permute-start(bf16[16,2048]{1,0:T(8,128)(2,1)S(1)} %convert_element_type.81), channel_id=1, source_target_pairs={{0,8},{8,16},{16,24},{24,32},{32,40},{40,48},{48,56},{56,64},{64,7... | collective-permute-start | bytes 196616 | tf_op jit(solution)/shard_map/ppermute | solution.py:466
  36.1 6.5 %collective-permute-start.7 = (bf16[16,2048]{1,0:T(8,128)(2,1)S(1)}, bf16[16,2048]{1,0:T(8,128)(2,1)S(1)}, u32[]{:S(2)}, u32[]{:S(2)}) collective-permute-start(bf16[16,2048]{1,0:T(8,128)(2,1)S(1)} %convert_element_type.81), channel_id=1, source_target_pairs={{8,0},{16,8},{24,16},{32,24},{40,32},{48,40},{56,48},{64,56},{72,6... | collective-permute-start | bytes 196616 | tf_op jit(solution)/shard_map/ppermute | solution.py:470
  37.4 27.8 %copy-start.7 = (bf16[16,2048]{1,0:T(8,128)(2,1)}, bf16[16,2048]{1,0:T(8,128)(2,1)S(1)}, u32[]{:S(2)}) copy-start(bf16[16,2048]{1,0:T(8,128)(2,1)S(1)} %collective-permute-done.2.refs_1_.refs_4_) | copy-start | bytes 196612
  37.4 18.0 %collective-permute-start.4 = (f32[4,4096]{1,0:T(4,128)S(1)}, f32[4,4096]{1,0:T(4,128)S(1)}, u32[]{:S(2)}, u32[]{:S(2)}) collective-permute-start(f32[4,4096]{1,0:T(4,128)S(1)} %get-tuple-element.50), channel_id=1, source_target_pairs={{0,2},{8,10},{16,18},{24,26},{32,34},{40,42},{48,50},{56,58},{64,6... | collective-permute-start | bytes 196616 | tf_op jit(solution)/shard_map/ppermute | solution.py:480
  38.1 17.4 %collective-permute-start.6 = (f32[4,4096]{1,0:T(4,128)S(1)}, f32[4,4096]{1,0:T(4,128)S(1)}, u32[]{:S(2)}, u32[]{:S(2)}) collective-permute-start(f32[4,4096]{1,0:T(4,128)S(1)} %get-tuple-element.51), channel_id=1, source_target_pairs={{0,7},{8,15},{16,23},{24,31},{32,39},{40,47},{48,55},{56,63},{64,7... | collective-permute-start | bytes 196616 | tf_op jit(solution)/shard_map/ppermute | solution.py:480
  38.8 16.7 %collective-permute-start.5 = (f32[4,4096]{1,0:T(4,128)S(1)}, f32[4,4096]{1,0:T(4,128)S(1)}, u32[]{:S(2)}, u32[]{:S(2)}) collective-permute-start(f32[4,4096]{1,0:T(4,128)S(1)} %get-tuple-element.52), channel_id=1, source_target_pairs={{0,6},{8,14},{16,22},{24,30},{32,38},{40,46},{48,54},{56,62},{64,7... | collective-permute-start | bytes 196616 | tf_op jit(solution)/shard_map/ppermute | solution.py:480
  39.4 16.0 %collective-permute-start.3 = (f32[4,4096]{1,0:T(4,128)S(1)}, f32[4,4096]{1,0:T(4,128)S(1)}, u32[]{:S(2)}, u32[]{:S(2)}) collective-permute-start(f32[4,4096]{1,0:T(4,128)S(1)} %get-tuple-element.53), channel_id=1, source_target_pairs={{0,1},{8,9},{16,17},{24,25},{32,33},{40,41},{48,49},{56,57},{64,65... | collective-permute-start | bytes 196616 | tf_op jit(solution)/shard_map/ppermute | solution.py:480
  42.6 22.6 %copy-start.8 = (bf16[16,2048]{1,0:T(8,128)(2,1)}, bf16[16,2048]{1,0:T(8,128)(2,1)S(1)}, u32[]{:S(2)}) copy-start(bf16[16,2048]{1,0:T(8,128)(2,1)S(1)} %collective-permute-done.7.refs_3_.refs_10_) | copy-start | bytes 196612
  48.8 16.4 %copy-start.4 = (f32[16,2048]{1,0:T(8,128)}, f32[16,2048]{1,0:T(8,128)S(1)}, u32[]{:S(2)}) copy-start(f32[16,2048]{1,0:T(8,128)S(1)} %operator.3.refs_8_.v2_ref) | copy-start | bytes 393220
  48.8 14.6 %collective-permute-start.8 = (bf16[16,2048]{1,0:T(8,128)(2,1)S(1)}, bf16[16,2048]{1,0:T(8,128)(2,1)S(1)}, u32[]{:S(2)}, u32[]{:S(2)}) collective-permute-start(bf16[16,2048]{1,0:T(8,128)(2,1)S(1)} %convert_element_type.82), channel_id=1, source_target_pairs={{0,8},{8,16},{16,24},{24,32},{32,40},{40,48},{48,56},{56,64},{64,7... | collective-permute-start | bytes 196616 | tf_op jit(solution)/shard_map/ppermute | solution.py:484
  55.5 2.6 %copy-start.9 = (f32[4,4096]{1,0:T(4,128)}, f32[4,4096]{1,0:T(4,128)S(1)}, u32[]{:S(2)}) copy-start(f32[4,4096]{1,0:T(4,128)S(1)} %add_add_fusion) | copy-start | bytes 196612
  59.9 5.3 %collective-permute-start.9 = (bf16[16,2048]{1,0:T(8,128)(2,1)S(1)}, bf16[16,2048]{1,0:T(8,128)(2,1)S(1)}, u32[]{:S(2)}, u32[]{:S(2)}) collective-permute-start(bf16[16,2048]{1,0:T(8,128)(2,1)S(1)} %convert_element_type.82), channel_id=1, source_target_pairs={{8,0},{16,8},{24,16},{32,24},{40,32},{48,40},{56,48},{64,56},{72,6... | collective-permute-start | bytes 196616 | tf_op jit(solution)/shard_map/ppermute | solution.py:488
  63.4 1.8 copy-start.14
  168.9 5.8 %collective-permute-start.13 = (bf16[16,4096]{1,0:T(8,128)(2,1)}, bf16[16,4096]{1,0:T(8,128)(2,1)S(1)}, u32[]{:S(2)}, u32[]{:S(2)}) collective-permute-start(bf16[16,4096]{1,0:T(8,128)(2,1)} %get-tuple-element.47), channel_id=1, source_target_pairs={{7,0},{15,8},{23,16},{31,24},{39,32},{47,40},{55,48},{63,56},{71,6... | collective-permute-start | bytes 393224 | tf_op jit(solution)/shard_map/ppermute | solution.py:508
  169.6 5.1 %collective-permute-start.12 = (bf16[16,4096]{1,0:T(8,128)(2,1)}, bf16[16,4096]{1,0:T(8,128)(2,1)S(1)}, u32[]{:S(2)}, u32[]{:S(2)}) collective-permute-start(bf16[16,4096]{1,0:T(8,128)(2,1)} %get-tuple-element.47), channel_id=1, source_target_pairs={{6,0},{14,8},{22,16},{30,24},{38,32},{46,40},{54,48},{62,56},{70,6... | collective-permute-start | bytes 393224 | tf_op jit(solution)/shard_map/ppermute | solution.py:508
  170.3 4.5 %collective-permute-start.11 = (bf16[16,4096]{1,0:T(8,128)(2,1)}, bf16[16,4096]{1,0:T(8,128)(2,1)S(1)}, u32[]{:S(2)}, u32[]{:S(2)}) collective-permute-start(bf16[16,4096]{1,0:T(8,128)(2,1)} %get-tuple-element.47), channel_id=1, source_target_pairs={{2,0},{10,8},{18,16},{26,24},{34,32},{42,40},{50,48},{58,56},{66,6... | collective-permute-start | bytes 393224 | tf_op jit(solution)/shard_map/ppermute | solution.py:508
  170.9 4.9 %collective-permute-start.10 = (bf16[16,4096]{1,0:T(8,128)(2,1)}, bf16[16,4096]{1,0:T(8,128)(2,1)S(1)}, u32[]{:S(2)}, u32[]{:S(2)}) collective-permute-start(bf16[16,4096]{1,0:T(8,128)(2,1)} %get-tuple-element.47), channel_id=1, source_target_pairs={{1,0},{9,8},{17,16},{25,24},{33,32},{41,40},{49,48},{57,56},{65,64... | collective-permute-start | bytes 393224 | tf_op jit(solution)/shard_map/ppermute | solution.py:508
  (6 other events, 5.7 us)

commit v5 on v3

--- a/solution.py
+++ b/solution.py
@@ -67,26 +67,15 @@
     )(centres, nodes)
 
 
-def centre_kernel(before_ref, own_ref, after_ref, out_ref):
+def fill_centres(out_ref, before_ref, own_ref, after_ref):
     per = own_ref.shape[1] // BLK
-    origin = own_ref[:, 0:1]
+    origin = own_ref[0:3, 0:1]
     for k, ref in enumerate((before_ref, own_ref, after_ref)):
-        points = (ref[0:3, :] - origin[0:3]) * (1.0 / RADIUS)
+        points = (ref[0:3, :] - origin) * (1.0 / RADIUS)
         a, b, c = split3(augmented(points, False))
         rows = jnp.concatenate([a, a, b, b, a, c], axis=0)
         for t in range(per):
             out_ref[k * per + t] = rows[:, t * BLK : (t + 1) * BLK].astype(bf16)
-
-
-def prepare_centres(before, own, after):
-    per = own.shape[1] // BLK
-    return pl.pallas_call(
-        centre_kernel,
-        in_specs=[whole(pltpu.VMEM)] * 3,
-        out_specs=whole(pltpu.VMEM),
-        out_shape=jax.ShapeDtypeStruct((3 * per, DEPTH, BLK), bf16),
-        name="prepare_centres",
-    )(before, own, after)
 
 
 def pl_reciprocal(x):
@@ -145,37 +134,43 @@
             weight_ref[k * per + t] = jnp.transpose(rows[:, t * BLK : (t + 1) * BLK]).astype(bf16)
 
 
-def operator_kernel(
-    unroll, together, tiles, count_ref, place_ref, member_ref, left_ref, right_ref,
-    before_ref, own_ref, after_ref, out_ref, weight_ref, total,
-):
+def operator_kernel(unroll, together, tiles, first, count_ref, place_ref, member_ref, left_ref, *refs):
+    if first:
+        before_ref, own_ref, after_ref, out_ref, right_ref, weight_ref, total = refs
+        fill_centres(right_ref, before_ref, own_ref, after_ref)
+    else:
+        right_ref, before_ref, own_ref, after_ref, out_ref, weight_ref, total = refs
     fill_weights(weight_ref, ((before_ref,), (own_ref,), (after_ref,)), tiles)
     clear(tiles, total)
     accumulate(
         unroll, together, tiles, count_ref[0], place_ref, member_ref, left_ref, right_ref,
         weight_ref, total,
     )
+    own = modes_of(own_ref)
     for t in range(tiles):
         image = jnp.transpose(total[t])
         sl = slice(t * BLK, (t + 1) * BLK)
-        out_ref[:, sl] = image[0:MODES] + image[MODES : 2 * MODES] + SHIFT * own_ref[:, sl]
+        out_ref[:, sl] = image[0:MODES] + image[MODES : 2 * MODES] + SHIFT * own[:, sl]
 
 
 def apply_operator(unroll, together, lists, left, right, before, own, after):
     tiles = own.shape[1] // BLK
     vmem, smem = whole(pltpu.VMEM), whole(pltpu.SMEM)
+    first = right is None
+    image = jax.ShapeDtypeStruct((MODES, own.shape[1]), f32)
+    factors = jax.ShapeDtypeStruct((3 * tiles, DEPTH, BLK), bf16)
     return pl.pallas_call(
-        functools.partial(operator_kernel, unroll, together, tiles),
-        in_specs=[smem] * 3 + [vmem] * 5,
-        out_specs=vmem,
-        out_shape=jax.ShapeDtypeStruct(own.shape, f32),
+        functools.partial(operator_kernel, unroll, together, tiles, first),
+        in_specs=[smem] * 3 + [vmem] * (4 if first else 5),
+        out_specs=(vmem, vmem) if first else vmem,
+        out_shape=(image, factors) if first else image,
         scratch_shapes=[
             pltpu.VMEM((3 * tiles, BLK, LANES), bf16),
             pltpu.VMEM((tiles + 1, BLK, LANES), f32),
         ],
         compiler_params=pltpu.CompilerParams(vmem_limit_bytes=40 * 2**20),
         name="operator",
-    )(*lists, left, right, before, own, after)
+    )(*lists, left, *(() if first else (right,)), before, own, after)
 
 
 def row_of(columns):
@@ -275,7 +270,7 @@
     per = fields[1][0].shape[1] // BLK
     own, guests = lefts[0].shape[0], lefts[1].shape[0]
     tiles = own + guests + checks
-    vmem, smem, far = whole(pltpu.VMEM), whole(pltpu.SMEM), whole(pl.ANY)
+    vmem, smem, far = whole(pltpu.VMEM), whole(pltpu.SMEM), whole(pltpu.HBM)
     return pl.pallas_call(
         functools.partial(volume_kernel, unroll, together, (own, guests, checks), share),
         in_specs=[smem] * 4 + [vmem] + [far] * 3 + [vmem] * 9,
@@ -293,7 +288,7 @@
             pltpu.SemaphoreType.DMA((3,)),
             pltpu.SemaphoreType.DMA((2,)),
         ],
-        compiler_params=pltpu.CompilerParams(vmem_limit_bytes=58 * 2**20),
+        compiler_params=pltpu.CompilerParams(vmem_limit_bytes=50 * 2**20),
         name="volume",
     )(*lists, turn, right, *lefts, *[f for side in fields for f in side])
 
@@ -335,13 +330,16 @@
     return answer, [a / scale for a in answer]
 
 
-def settle_kernel(total_nodes, sums_ref, v0_ref, v1_ref, v2_ref, guest_ref, weights_ref, coef_ref, out_ref):
+def settle_kernel(total_nodes, sums_ref, v0_ref, v1_ref, v2_ref, far_ref, weights_ref, coef_ref, out_ref, guest_ref, sem):
+    copy = pltpu.make_async_copy(far_ref, guest_ref, sem)
+    copy.start()
     pair = jnp.sum(sums_ref[...], axis=0)
     row = jnp.concatenate([pair[0:1], pair[1:2]], axis=1)
     answer, scaled = coefficients(row, total_nodes)
     weights_ref[...] = answer[0] * v0_ref[...] + answer[1] * v1_ref[...] + answer[2] * v2_ref[...]
     for k, column in enumerate(scaled):
         coef_ref[k] = jnp.broadcast_to(column, (MODES, LANES))
+    copy.wait()
     out_ref[...] = blend(scaled, guest_ref).astype(bf16)
 
 
@@ -357,13 +355,14 @@
     vmem = whole(pltpu.VMEM)
     return pl.pallas_call(
         functools.partial(settle_kernel, total_nodes),
-        in_specs=[vmem] * 5,
+        in_specs=[vmem] * 4 + [whole(pltpu.HBM)],
         out_specs=(vmem,) * 3,
         out_shape=(
             jax.ShapeDtypeStruct(vectors[0].shape, f32),
             jax.ShapeDtypeStruct((KRYLOV, MODES, LANES), f32),
             jax.ShapeDtypeStruct((MODES, guests.shape[1]), bf16),
         ),
+        scratch_shapes=[pltpu.VMEM(guests.shape, f32), pltpu.SemaphoreType.DMA],
         name="settle",
     )(sums, *vectors, guests)
 
@@ -481,13 +480,12 @@
     own_places = place_of(neighbours)
     own_list = work_list(own_places, 3, 8, kinds)
     own_left = prepare_nodes(centres, centres)
-    again, own_left = lax.optimization_barrier((packed, own_left))
+    again, own_left, own_list = lax.optimization_barrier((packed, own_left, own_list))
     after = lax.ppermute(again, "surf", down)
     left = prepare_nodes(centres, volume_nodes)
 
-    right = prepare_centres(before, packed, after)
     v0 = mode_shapes
-    v1 = apply_operator(8, 3, own_list, own_left, right, before, v0, after)
+    v1, right = apply_operator(8, 3, own_list, own_left, None, before, packed, after)
     v1_low = v1.astype(bf16)
     v1_before = lax.ppermute(v1_low, "surf", up)
     v1_after = lax.ppermute(v1_low, "surf", down)
@@ -502,6 +500,12 @@
         piece = parcel[:, k * width : (k + 1) * width]
         got = got + lax.ppermute(piece, "vol", [(0, helper)])
         helping = helping | (turn == helper)
+    v2 = apply_operator(8, 3, own_list, own_left, right, v1_before, v1, v1_after)
+    v2_low = v2.astype(bf16)
+    v2_before = lax.ppermute(v2_low, "surf", up)
+    v2_after = lax.ppermute(v2_low, "surf", down)
+    guest_left = prepare_nodes(centres, got[:3])
+
     guest_ids = got[3].reshape(moved, BLK)[:, :slots].astype(jnp.int32)
     guest_places = jnp.where(helping, place_of(guest_ids), -1)
     kept_here = (turn > 0) | (jnp.arange(tile_dev) < kept)
@@ -509,12 +513,6 @@
     check_places = lax.dynamic_slice_in_dim(own_places, turn * checks, checks, axis=0)
     places = jnp.concatenate([tile_places, guest_places, check_places], axis=0)
     whole_list = work_list(places, 2, 10, kinds)
-    guest_left = prepare_nodes(centres, got[:3])
-
-    v2 = apply_operator(8, 3, own_list, own_left, right, v1_before, v1, v1_after)
-    v2_low = v2.astype(bf16)
-    v2_before = lax.ppermute(v2_low, "surf", up)
-    v2_after = lax.ppermute(v2_low, "surf", down)
     fields = (
         (before, v1_before, v2_before),
         (v0, v1, v2),

time: 183 us -> 175 us (0.956)
  Pallas kernels: 92.6 us -> 87.8 us
  local copies, waits for them, and re-layouts: 9.85 us -> 5.19 us
  waiting for transfers between devices: 0.56 us -> 3.49 us
    unnamed x47 -> x29, local copies, waits for them, and re-layouts: 8.33 us -> 4.27 us
    pallas_call x1, Pallas kernels: 61.7 us -> 58.5 us  [volume_images(): pl.pallas_call(functools.partial(volume_kernel, unroll, together, (own, g...]
    pallas_call x1 -> x0, Pallas kernels: 2.14 us -> none  [prepare_centres(): pl.pallas_call(centre_kernel, in_specs=[whole(pltpu.VMEM)] * 3, out_specs...]
  transfers between devices with their start and end apart: 14 -> 14, of which waited for: 1 -> 2; matrix products, arithmetic and copies ran while one was open for 4% -> 3% of each run, Pallas kernels for 10% -> 11%
where the time goes in v5:
time: 175 us; the launch traced here: 174 us
  Pallas kernels  87.8 us (50%)
  blocking collectives  39.2 us (22%)
  starting transfers between devices  30.4 us (17%)
  local copies, waits for them, and re-layouts  5.19 us (3%)
  other arithmetic  4.22 us (2%)
  waiting for transfers between devices  3.49 us (2%)
  between operations  2.69 us (2%)
    pallas_call x1, Pallas kernels, volume_images(): pl.pallas_call(functools.partial(volume_kernel, unroll, together, (own, g...  58.5 us
    all_to_all x1, blocking collectives, per_device(): sums = lax.all_to_all(sums, ('surf', 'vol'), 0, 0, tiled=True)  39.2 us
    pallas_call x2, Pallas kernels, apply_operator(): pl.pallas_call(functools.partial(operator_kernel, unroll, together, tiles...  12.5 us
    pallas_call x3, Pallas kernels, prepare_nodes(): pl.pallas_call(node_kernel, grid=(tiles // step,), in_specs=[pl.BlockSpec...  7.69 us
    ppermute x1, starting transfers between devices, per_device(): v2_before = lax.ppermute(v2_low, 'surf', up)  7.24 us
    ppermute x1, starting transfers between devices, per_device(): v1_before = lax.ppermute(v1_low, 'surf', up)  5.92 us
    ppermute x4, starting transfers between devices, per_device(): parts = [lax.ppermute(away, 'vol', [(helper, 0)]) for helper in helpers]  5.66 us
    pallas_call x1, Pallas kernels, combine(): pl.pallas_call(combine_kernel, grid=(nodes // width,), in_specs=[pl.Block...  5.05 us
  transfers between devices with their start and end apart: 14, of which 2 were waited for; matrix products, arithmetic and copies ran while one was open for 3% of the time, Pallas kernels for 11%

profile of v5, /device:TPU:1, one launch (start us, length us, event | category | flops | bytes accessed | tf_op | source)
XLA Modules:
  0.0 173.7 jit_solution(17258777671001252995)
XLA Ops:
  0.7 1.0 pad_maximum_fusion.1.refs_1_
  1.7 4.4 %collective-permute-start = (f32[24,2048]{1,0:T(8,128)S(1)}, f32[24,2048]{1,0:T(8,128)S(1)}, u32[]{:S(2)}, u32[]{:S(2)}) collective-permute-start(f32[24,2048]{1,0:T(8,128)S(1)} %pad_maximum_fusion.1.refs_1_), channel_id=1, source_target_pairs={{0,8},{8,16},{16,24},{24,32},{32,40},{40,48},{48,56},{56,64},{64,7... | collective-permute-start | bytes 589832 | tf_op jit(solution)/shard_map/ppermute | solution.py:475
  6.2 0.8 copy.27
  8.2 1.6 prepare_nodes.3.left_ref.refs_2_
  10.9 1.3 collective-permute-start.1
  12.2 4.3 %prepare_nodes.4.refs_0_ = bf16[128,48,256]{2,1,0:T(8,128)(2,1)} custom-call(f32[3,2048]{1,0:T(4,128)} %centres_ref.5, f32[3,32768]{1,0:T(4,128)} %nodes_ref.3), custom_call_target="tpu_custom_call" | custom-call | tf_op jit(solution)/shard_map/prepare_nodes/pallas_call | solution.py:57
  17.0 1.6 collective-permute-done.1.refs_2_.refs_9_
  18.6 6.3 %operator.2 = (f32[16,2048]{1,0:T(8,128)S(1)}, bf16[24,48,256]{2,1,0:T(8,128)(2,1)S(1)}) custom-call(s32[1]{0:T(128)} %bitcast.count_ref, s32[40]{0:T(128)S(1)} %select_reduce_fusion.4.place_ref, s32[120]{0:T(128)S(1)} %reshape.137.member_ref, bf16[8,48,256]{2,1,0:T(8,128)(2,1)S(1)} %copy-done, f32[24,2048]{1,0:T(8,128)S(1)} %collective-permute-done.refs_0_.refs_3_, ...), custom_call_target="tpu_custom_call" | custom-call | tf_op jit(solution)/shard_map/operator/pallas_call | solution.py:162
  24.9 5.9 %collective-permute-start.2 = (bf16[16,2048]{1,0:T(8,128)(2,1)S(1)}, bf16[16,2048]{1,0:T(8,128)(2,1)S(1)}, u32[]{:S(2)}, u32[]{:S(2)}) collective-permute-start(bf16[16,2048]{1,0:T(8,128)(2,1)S(1)} %convert_element_type.81), channel_id=1, source_target_pairs={{0,8},{8,16},{16,24},{24,32},{32,40},{40,48},{48,56},{56,64},{64,7... | collective-permute-start | bytes 196616 | tf_op jit(solution)/shard_map/ppermute | solution.py:490
  30.9 1.3 collective-permute-start.7
  34.2 1.3 collective-permute-start.3
  35.5 1.9 %collective-permute-done.7.refs_3_.refs_10_ = bf16[16,2048]{1,0:T(8,128)(2,1)S(1)} collective-permute-done((bf16[16,2048]{1,0:T(8,128)(2,1)S(1)}, bf16[16,2048]{1,0:T(8,128)(2,1)S(1)}, u32[]{:S(2)}, u32[]{:S(2)}) %collective-permute-start.7) | collective-permute-done | bytes 65568 | tf_op jit(solution)/shard_map/ppermute | solution.py:491
  37.4 6.2 %operator.3.refs_8_.v2_ref = f32[16,2048]{1,0:T(8,128)S(1)} custom-call(s32[1]{0:T(128)} %bitcast.count_ref, s32[40]{0:T(128)S(1)} %select_reduce_fusion.4.place_ref, s32[120]{0:T(128)S(1)} %reshape.137.member_ref, bf16[8,48,256]{2,1,0:T(8,128)(2,1)S(1)} %copy-done, bf16[24,48,256]{2,1,0:T(8,128)(2,1)S(1)} %get-tuple-element.24.refs_0_.right_ref, ...), custom_call_target="tpu_custom_call" | custom-call | tf_op jit(solution)/shard_map/operator/pallas_call | solution.py:162
  43.6 1.3 collective-permute-start.9
  44.9 7.2 %collective-permute-start.8 = (bf16[16,2048]{1,0:T(8,128)(2,1)S(1)}, bf16[16,2048]{1,0:T(8,128)(2,1)S(1)}, u32[]{:S(2)}, u32[]{:S(2)}) collective-permute-start(bf16[16,2048]{1,0:T(8,128)(2,1)S(1)} %convert_element_type.87), channel_id=1, source_target_pairs={{0,8},{8,16},{16,24},{24,32},{32,40},{40,48},{48,56},{56,64},{64,7... | collective-permute-start | bytes 196616 | tf_op jit(solution)/shard_map/ppermute | solution.py:505
  54.8 1.8 %prepare_nodes.5.refs_1_ = bf16[16,48,256]{2,1,0:T(8,128)(2,1)} custom-call(f32[3,2048]{1,0:T(4,128)} %centres_ref.5, f32[3,4096]{1,0:T(4,128)} %bitcast.21), custom_call_target="tpu_custom_call" | custom-call | tf_op jit(solution)/shard_map/prepare_nodes/pallas_call | solution.py:57
  57.7 1.0 copy-done.3
  58.7 58.5 %volume.1 = (f32[48,32768]{1,0:T(8,128)}, f32[48,4096]{1,0:T(8,128)S(1)}, f32[256,2,128]{2,1,0:T(2,128)S(1)}) custom-call(s32[1]{0:T(128)} %bitcast.4.count_ref, s32[670]{0:T(1024)S(1)} %select_reduce_fusion.1.place_ref, s32[1340]{0:T(1024)S(1)} %reshape.139.member_ref, s32[1]{0:T(128)} %bitcast.6.turn_ref, ...), custom_call_target="tpu_custom_call" | custom-call | tf_op jit(solution)/shard_map/volume/pallas_call | solution.py:274
  117.2 0.9 copy-done.5
  118.0 39.2 %all_to_all.5.sums_ref = f32[256,2,128]{2,1,0:T(2,128)} all-to-all(f32[256,2,128]{2,1,0:T(2,128)S(1)} %get-tuple-element.26), channel_id=1, replica_groups=mesh['surf'=32,'vol'=8] {'surf','vol'}, dimensions={0} | all-to-all | bytes 524288 | tf_op jit(solution)/shard_map/all_to_all | solution.py:525
  157.3 3.0 %settle.1 = (f32[16,2048]{1,0:T(8,128)}, f32[3,16,128]{2,1,0:T(8,128)}, bf16[16,4096]{1,0:T(8,128)(2,1)}) custom-call(f32[256,2,128]{2,1,0:T(2,128)} %all_to_all.5.sums_ref, f32[16,2048]{1,0:T(8,128)} %v0_ref.1, f32[16,2048]{1,0:T(8,128)} %copy-done.1, f32[16,2048]{1,0:T(8,128)} %copy-done.2, f32[48,4096]{1,0:T(8,128)} %copy-done.5), custom_call_target="tpu_custom_call" | custom-call | tf_op jit(solution)/shard_map/settle/pallas_call | solution.py:356
  162.3 3.7 %collective-permute-start.10 = (bf16[16,4096]{1,0:T(8,128)(2,1)}, bf16[16,4096]{1,0:T(8,128)(2,1)S(1)}, u32[]{:S(2)}, u32[]{:S(2)}) collective-permute-start(bf16[16,4096]{1,0:T(8,128)(2,1)} %get-tuple-element.31), channel_id=1, source_target_pairs={{1,0},{9,8},{17,16},{25,24},{33,32},{41,40},{49,48},{57,56},{65,64... | collective-permute-start | bytes 393224 | tf_op jit(solution)/shard_map/ppermute | solution.py:527
  166.0 5.1 %combine.1.refs_0_ = f32[16,32768]{1,0:T(8,128)} custom-call(f32[3,16,128]{2,1,0:T(8,128)} %get-tuple-element.29.coef_ref, f32[48,32768]{1,0:T(8,128)} %get-tuple-element.30.image_ref), custom_call_target="tpu_custom_call" | custom-call | tf_op jit(solution)/shard_map/combine/pallas_call | solution.py:377
  172.4 1.1 insert.1
  (94 shorter events, 10.5 us)
Async XLA Ops:
  0.6 16.2 %slice-start = ((f32[3,32768]{1,0:T(4,128)}), f32[3,16384]{1,0:T(4,128)S(1)}, s32[]{:S(2)}) async-start(f32[3,32768]{1,0:T(4,128)} %nodes_ref.3), calls=%async_computation.1 | async-start | bytes 524288 | tf_op jit(solution)/shard_map/slice | solution.py:494
  0.6 15.9 %copy-start.11 = (s32[128,9]{0,1:T(8,128)S(1)}, s32[128,9]{0,1:T(8,128)}, u32[]{:S(2)}) copy-start(s32[128,9]{0,1:T(8,128)} %param.9) | copy-start | bytes 13828
  1.7 16.9 %collective-permute-start = (f32[24,2048]{1,0:T(8,128)S(1)}, f32[24,2048]{1,0:T(8,128)S(1)}, u32[]{:S(2)}, u32[]{:S(2)}) collective-permute-start(f32[24,2048]{1,0:T(8,128)S(1)} %pad_maximum_fusion.1.refs_1_), channel_id=1, source_target_pairs={{0,8},{8,16},{16,24},{24,32},{32,40},{40,48},{48,56},{56,64},{64,7... | collective-permute-start | bytes 589832 | tf_op jit(solution)/shard_map/ppermute | solution.py:475
  9.9 8.7 %copy-start = (bf16[8,48,256]{2,1,0:T(8,128)(2,1)S(1)}, bf16[8,48,256]{2,1,0:T(8,128)(2,1)}, u32[]{:S(2)}) copy-start(bf16[8,48,256]{2,1,0:T(8,128)(2,1)} %prepare_nodes.3.left_ref.refs_2_) | copy-start | bytes 589828
  10.9 7.7 %collective-permute-start.1 = (f32[24,2048]{1,0:T(8,128)S(1)}, f32[24,2048]{1,0:T(8,128)S(1)}, u32[]{:S(2)}, u32[]{:S(2)}) collective-permute-start(f32[24,2048]{1,0:T(8,128)S(1)} %pad_maximum_fusion.1.refs_1_), channel_id=1, source_target_pairs={{8,0},{16,8},{24,16},{32,24},{40,32},{48,40},{56,48},{64,56},{72,6... | collective-permute-start | bytes 589832 | tf_op jit(solution)/shard_map/ppermute | solution.py:484
  16.8 40.9 %copy-start.4 = (f32[16,2048]{1,0:T(8,128)S(1)}, f32[16,2048]{1,0:T(8,128)}, u32[]{:S(2)}) copy-start(f32[16,2048]{1,0:T(8,128)} %v0_ref.1) | copy-start | bytes 393220
  24.9 92.3 %copy-start.1 = (f32[16,2048]{1,0:T(8,128)}, f32[16,2048]{1,0:T(8,128)S(1)}, u32[]{:S(2)}) copy-start(f32[16,2048]{1,0:T(8,128)S(1)} %get-tuple-element.22.refs_2_.refs_7_.v1_ref) | copy-start | bytes 393220
  24.9 7.2 %collective-permute-start.2 = (bf16[16,2048]{1,0:T(8,128)(2,1)S(1)}, bf16[16,2048]{1,0:T(8,128)(2,1)S(1)}, u32[]{:S(2)}, u32[]{:S(2)}) collective-permute-start(bf16[16,2048]{1,0:T(8,128)(2,1)S(1)} %convert_element_type.81), channel_id=1, source_target_pairs={{0,8},{8,16},{16,24},{24,32},{32,40},{40,48},{48,56},{56,64},{64,7... | collective-permute-start | bytes 196616 | tf_op jit(solution)/shard_map/ppermute | solution.py:490
  30.9 6.5 %collective-permute-start.7 = (bf16[16,2048]{1,0:T(8,128)(2,1)S(1)}, bf16[16,2048]{1,0:T(8,128)(2,1)S(1)}, u32[]{:S(2)}, u32[]{:S(2)}) collective-permute-start(bf16[16,2048]{1,0:T(8,128)(2,1)S(1)} %convert_element_type.81), channel_id=1, source_target_pairs={{8,0},{16,8},{24,16},{32,24},{40,32},{48,40},{56,48},{64,56},{72,6... | collective-permute-start | bytes 196616 | tf_op jit(solution)/shard_map/ppermute | solution.py:491
  32.2 12.7 %collective-permute-start.4 = (f32[4,4096]{1,0:T(4,128)S(1)}, f32[4,4096]{1,0:T(4,128)S(1)}, u32[]{:S(2)}, u32[]{:S(2)}) collective-permute-start(f32[4,4096]{1,0:T(4,128)S(1)} %get-tuple-element.34), channel_id=1, source_target_pairs={{0,2},{8,10},{16,18},{24,26},{32,34},{40,42},{48,50},{56,58},{64,6... | collective-permute-start | bytes 196616 | tf_op jit(solution)/shard_map/ppermute | solution.py:501
  32.9 19.3 %collective-permute-start.6 = (f32[4,4096]{1,0:T(4,128)S(1)}, f32[4,4096]{1,0:T(4,128)S(1)}, u32[]{:S(2)}, u32[]{:S(2)}) collective-permute-start(f32[4,4096]{1,0:T(4,128)S(1)} %get-tuple-element.35), channel_id=1, source_target_pairs={{0,7},{8,15},{16,23},{24,31},{32,39},{40,47},{48,55},{56,63},{64,7... | collective-permute-start | bytes 196616 | tf_op jit(solution)/shard_map/ppermute | solution.py:501
  33.5 18.6 %collective-permute-start.5 = (f32[4,4096]{1,0:T(4,128)S(1)}, f32[4,4096]{1,0:T(4,128)S(1)}, u32[]{:S(2)}, u32[]{:S(2)}) collective-permute-start(f32[4,4096]{1,0:T(4,128)S(1)} %get-tuple-element.36), channel_id=1, source_target_pairs={{0,6},{8,14},{16,22},{24,30},{32,38},{40,46},{48,54},{56,62},{64,7... | collective-permute-start | bytes 196616 | tf_op jit(solution)/shard_map/ppermute | solution.py:501
  34.2 17.9 %collective-permute-start.3 = (f32[4,4096]{1,0:T(4,128)S(1)}, f32[4,4096]{1,0:T(4,128)S(1)}, u32[]{:S(2)}, u32[]{:S(2)}) collective-permute-start(f32[4,4096]{1,0:T(4,128)S(1)} %get-tuple-element.37), channel_id=1, source_target_pairs={{0,1},{8,9},{16,17},{24,25},{32,33},{40,41},{48,49},{56,57},{64,65... | collective-permute-start | bytes 196616 | tf_op jit(solution)/shard_map/ppermute | solution.py:501
  43.5 73.6 %copy-start.2 = (f32[16,2048]{1,0:T(8,128)}, f32[16,2048]{1,0:T(8,128)S(1)}, u32[]{:S(2)}) copy-start(f32[16,2048]{1,0:T(8,128)S(1)} %operator.3.refs_8_.v2_ref) | copy-start | bytes 393220
  43.6 14.1 %collective-permute-start.9 = (bf16[16,2048]{1,0:T(8,128)(2,1)S(1)}, bf16[16,2048]{1,0:T(8,128)(2,1)S(1)}, u32[]{:S(2)}, u32[]{:S(2)}) collective-permute-start(bf16[16,2048]{1,0:T(8,128)(2,1)S(1)} %convert_element_type.87), channel_id=1, source_target_pairs={{8,0},{16,8},{24,16},{32,24},{40,32},{48,40},{56,48},{64,56},{72,6... | collective-permute-start | bytes 196616 | tf_op jit(solution)/shard_map/ppermute | solution.py:506
  44.9 12.8 %collective-permute-start.8 = (bf16[16,2048]{1,0:T(8,128)(2,1)S(1)}, bf16[16,2048]{1,0:T(8,128)(2,1)S(1)}, u32[]{:S(2)}, u32[]{:S(2)}) collective-permute-start(bf16[16,2048]{1,0:T(8,128)(2,1)S(1)} %convert_element_type.87), channel_id=1, source_target_pairs={{0,8},{8,16},{16,24},{24,32},{32,40},{40,48},{48,56},{56,64},{64,7... | collective-permute-start | bytes 196616 | tf_op jit(solution)/shard_map/ppermute | solution.py:505
  52.2 2.6 %copy-start.6 = (f32[4,4096]{1,0:T(4,128)}, f32[4,4096]{1,0:T(4,128)S(1)}, u32[]{:S(2)}) copy-start(f32[4,4096]{1,0:T(4,128)S(1)} %add_add_fusion) | copy-start | bytes 196612
  57.7 1.0 copy-start.3
  117.2 0.9 copy-start.5
  160.3 10.8 %collective-permute-start.13 = (bf16[16,4096]{1,0:T(8,128)(2,1)}, bf16[16,4096]{1,0:T(8,128)(2,1)S(1)}, u32[]{:S(2)}, u32[]{:S(2)}) collective-permute-start(bf16[16,4096]{1,0:T(8,128)(2,1)} %get-tuple-element.31), channel_id=1, source_target_pairs={{7,0},{15,8},{23,16},{31,24},{39,32},{47,40},{55,48},{63,56},{71,6... | collective-permute-start | bytes 393224 | tf_op jit(solution)/shard_map/ppermute | solution.py:527
  160.9 10.1 %collective-permute-start.12 = (bf16[16,4096]{1,0:T(8,128)(2,1)}, bf16[16,4096]{1,0:T(8,128)(2,1)S(1)}, u32[]{:S(2)}, u32[]{:S(2)}) collective-permute-start(bf16[16,4096]{1,0:T(8,128)(2,1)} %get-tuple-element.31), channel_id=1, source_target_pairs={{6,0},{14,8},{22,16},{30,24},{38,32},{46,40},{54,48},{62,56},{70,6... | collective-permute-start | bytes 393224 | tf_op jit(solution)/shard_map/ppermute | solution.py:527
  161.6 9.4 %collective-permute-start.11 = (bf16[16,4096]{1,0:T(8,128)(2,1)}, bf16[16,4096]{1,0:T(8,128)(2,1)S(1)}, u32[]{:S(2)}, u32[]{:S(2)}) collective-permute-start(bf16[16,4096]{1,0:T(8,128)(2,1)} %get-tuple-element.31), channel_id=1, source_target_pairs={{2,0},{10,8},{18,16},{26,24},{34,32},{42,40},{50,48},{58,56},{66,6... | collective-permute-start | bytes 393224 | tf_op jit(solution)/shard_map/ppermute | solution.py:527
  162.3 8.8 %collective-permute-start.10 = (bf16[16,4096]{1,0:T(8,128)(2,1)}, bf16[16,4096]{1,0:T(8,128)(2,1)S(1)}, u32[]{:S(2)}, u32[]{:S(2)}) collective-permute-start(bf16[16,4096]{1,0:T(8,128)(2,1)} %get-tuple-element.31), channel_id=1, source_target_pairs={{1,0},{9,8},{17,16},{25,24},{33,32},{41,40},{49,48},{57,56},{65,64... | collective-permute-start | bytes 393224 | tf_op jit(solution)/shard_map/ppermute | solution.py:527
  171.0 0.7 copy-start.9
  (3 other events, 2.0 us)

commit v6 on v5

--- a/solution.py
+++ b/solution.py
@@ -53,7 +53,7 @@
 
 def prepare_nodes(centres, nodes):
     tiles = nodes.shape[1] // BLK
-    step = 32 if tiles % 32 == 0 else tiles
+    step = 64 if tiles % 64 == 0 else tiles
     return pl.pallas_call(
         node_kernel,
         grid=(tiles // step,),
@@ -63,6 +63,7 @@
         ],
         out_specs=pl.BlockSpec((step, DEPTH, BLK), lambda i: (i, 0, 0)),
         out_shape=jax.ShapeDtypeStruct((tiles, DEPTH, BLK), bf16),
+        compiler_params=pltpu.CompilerParams(vmem_limit_bytes=32 * 2**20),
         name="prepare_nodes",
     )(centres, nodes)
 
@@ -373,7 +374,7 @@
 
 def combine(coef, images):
     nodes = images.shape[1]
-    width = 8192 if nodes % 8192 == 0 else nodes
+    width = 16384 if nodes % 16384 == 0 else nodes
     return pl.pallas_call(
         combine_kernel,
         grid=(nodes // width,),
@@ -383,6 +384,7 @@
         ],
         out_specs=pl.BlockSpec((MODES, width), lambda i: (0, i)),
         out_shape=jax.ShapeDtypeStruct((MODES, nodes), f32),
+        compiler_params=pltpu.CompilerParams(vmem_limit_bytes=24 * 2**20),
         name="combine",
     )(coef, images)
 
@@ -512,7 +514,7 @@
     tile_places = jnp.where(kept_here[:, None], place_of(supports), -1)
     check_places = lax.dynamic_slice_in_dim(own_places, turn * checks, checks, axis=0)
     places = jnp.concatenate([tile_places, guest_places, check_places], axis=0)
-    whole_list = work_list(places, 2, 10, kinds)
+    whole_list = work_list(places, 2, 16, kinds)
     fields = (
         (before, v1_before, v2_before),
         (v0, v1, v2),
@@ -520,7 +522,7 @@
     )
     lefts = (left, guest_left, own_left)
     images, guests, sums = volume_images(
-        10, 2, whole_list, turns, right, lefts, checks, fields, devices, share
+        16, 2, whole_list, turns, right, lefts, checks, fields, devices, share
     )
     sums = lax.all_to_all(sums, ("surf", "vol"), 0, 0, tiled=True)
     weights, coef, away = settle(sums, (v0, v1, v2), guests, total_nodes)

time: 175 us -> 171 us (0.977)
  Pallas kernels: 87.8 us -> 79.1 us
  local copies, waits for them, and re-layouts: 5.19 us -> 11.9 us
  blocking collectives: 39.2 us -> 36.8 us
    unnamed x29 -> x37, local copies, waits for them, and re-layouts: 4.27 us -> 11 us
    pallas_call x3, Pallas kernels: 7.69 us -> 1.45 us  [prepare_nodes(): pl.pallas_call(node_kernel, grid=(tiles // step,), in_specs=[pl.BlockSpec...]
    pallas_call x1, Pallas kernels: 5.05 us -> 2.29 us  [combine(): pl.pallas_call(combine_kernel, grid=(nodes // width,), in_specs=[pl.Block...]
    all_to_all x1, blocking collectives: 39.2 us -> 36.8 us  [per_device(): sums = lax.all_to_all(sums, ('surf', 'vol'), 0, 0, tiled=True)]
  transfers between devices with their start and end apart: 14 -> 14, of which waited for: 2 -> 2; matrix products, arithmetic and copies ran while one was open for 3% -> 3% of each run, Pallas kernels for 11% -> 6%
where the time goes in v6:
time: 171 us; the launch traced here: 169 us
  Pallas kernels  79.1 us (46%)
  blocking collectives  36.8 us (22%)
  starting transfers between devices  30.4 us (18%)
  local copies, waits for them, and re-layouts  11.9 us (7%)
  other arithmetic  4.22 us (2%)
  waiting for transfers between devices  3.11 us (2%)
  between operations  2.67 us (2%)
    pallas_call x1, Pallas kernels, volume_images(): pl.pallas_call(functools.partial(volume_kernel, unroll, together, (own, g...  58.8 us
    all_to_all x1, blocking collectives, per_device(): sums = lax.all_to_all(sums, ('surf', 'vol'), 0, 0, tiled=True)  36.8 us
    pallas_call x2, Pallas kernels, apply_operator(): pl.pallas_call(functools.partial(operator_kernel, unroll, together, tiles...  12.5 us
    unnamed x37, local copies, waits for them, and re-layouts  11 us
    ppermute x1, starting transfers between devices, per_device(): v2_before = lax.ppermute(v2_low, 'surf', up)  7.25 us
    ppermute x1, starting transfers between devices, per_device(): v1_before = lax.ppermute(v1_low, 'surf', up)  5.92 us
    ppermute x4, starting transfers between devices, per_device(): parts = [lax.ppermute(away, 'vol', [(helper, 0)]) for helper in helpers]  5.66 us
    ppermute x1, starting transfers between devices, per_device(): before = lax.ppermute(packed, 'surf', up)  4.38 us
  transfers between devices with their start and end apart: 14, of which 2 were waited for; matrix products, arithmetic and copies ran while one was open for 3% of the time, Pallas kernels for 6%

profile of v6, /device:TPU:1, one launch (start us, length us, event | category | flops | bytes accessed | tf_op | source)
XLA Modules:
  0.0 169.0 jit_solution(1526024942086498254)
XLA Ops:
  0.7 1.0 pad_maximum_fusion.1.refs_1_
  1.7 4.4 %collective-permute-start = (f32[24,2048]{1,0:T(8,128)S(1)}, f32[24,2048]{1,0:T(8,128)S(1)}, u32[]{:S(2)}, u32[]{:S(2)}) collective-permute-start(f32[24,2048]{1,0:T(8,128)S(1)} %pad_maximum_fusion.1.refs_1_), channel_id=1, source_target_pairs={{0,8},{8,16},{16,24},{24,32},{32,40},{40,48},{48,56},{56,64},{64,7... | collective-permute-start | bytes 589832 | tf_op jit(solution)/shard_map/ppermute | solution.py:477
  6.2 0.8 copy.27
  10.1 1.3 collective-permute-start.1
  11.4 1.0 copy-done.4
  13.2 1.1 prepare_nodes.4.refs_0_
  14.3 1.7 copy-done
  16.6 1.2 collective-permute-done.1.refs_2_.refs_9_
  17.8 6.3 %operator.2 = (f32[16,2048]{1,0:T(8,128)S(1)}, bf16[24,48,256]{2,1,0:T(8,128)(2,1)S(1)}) custom-call(s32[1]{0:T(128)} %bitcast.count_ref, s32[40]{0:T(128)S(1)} %select_reduce_fusion.4.place_ref, s32[120]{0:T(128)S(1)} %reshape.137.member_ref, bf16[8,48,256]{2,1,0:T(8,128)(2,1)S(1)} %prepare_nodes.3.left_ref.refs_2_, ...), custom_call_target="tpu_custom_call" | custom-call | tf_op jit(solution)/shard_map/operator/pallas_call | solution.py:163
  24.1 5.9 %collective-permute-start.2 = (bf16[16,2048]{1,0:T(8,128)(2,1)S(1)}, bf16[16,2048]{1,0:T(8,128)(2,1)S(1)}, u32[]{:S(2)}, u32[]{:S(2)}) collective-permute-start(bf16[16,2048]{1,0:T(8,128)(2,1)S(1)} %convert_element_type.81), channel_id=1, source_target_pairs={{0,8},{8,16},{16,24},{24,32},{32,40},{40,48},{48,56},{56,64},{64,7... | collective-permute-start | bytes 196616 | tf_op jit(solution)/shard_map/ppermute | solution.py:492
  30.1 1.3 collective-permute-start.7
  33.4 1.3 collective-permute-start.3
  34.7 1.9 %collective-permute-done.7.refs_3_.refs_10_ = bf16[16,2048]{1,0:T(8,128)(2,1)S(1)} collective-permute-done((bf16[16,2048]{1,0:T(8,128)(2,1)S(1)}, bf16[16,2048]{1,0:T(8,128)(2,1)S(1)}, u32[]{:S(2)}, u32[]{:S(2)}) %collective-permute-start.7) | collective-permute-done | bytes 65568 | tf_op jit(solution)/shard_map/ppermute | solution.py:493
  36.6 6.2 %operator.3.refs_8_.v2_ref = f32[16,2048]{1,0:T(8,128)S(1)} custom-call(s32[1]{0:T(128)} %bitcast.count_ref, s32[40]{0:T(128)S(1)} %select_reduce_fusion.4.place_ref, s32[120]{0:T(128)S(1)} %reshape.137.member_ref, bf16[8,48,256]{2,1,0:T(8,128)(2,1)S(1)} %prepare_nodes.3.left_ref.refs_2_, bf16[24,48,256]{2,1,0:T(8,128)(2,1)S(1)} %get-tuple-element.24.refs_0_.right_ref, ...), custom_call_target="tpu_custom_call" | custom-call | tf_op jit(solution)/shard_map/operator/pallas_call | solution.py:163
  42.8 1.3 collective-permute-start.9
  44.1 7.3 %collective-permute-start.8 = (bf16[16,2048]{1,0:T(8,128)(2,1)S(1)}, bf16[16,2048]{1,0:T(8,128)(2,1)S(1)}, u32[]{:S(2)}, u32[]{:S(2)}) collective-permute-start(bf16[16,2048]{1,0:T(8,128)(2,1)S(1)} %convert_element_type.87), channel_id=1, source_target_pairs={{0,8},{8,16},{16,24},{24,32},{32,40},{40,48},{48,56},{56,64},{64,7... | collective-permute-start | bytes 196616 | tf_op jit(solution)/shard_map/ppermute | solution.py:507
  55.3 58.8 %volume.1 = (f32[48,32768]{1,0:T(8,128)}, f32[48,4096]{1,0:T(8,128)S(1)}, f32[256,2,128]{2,1,0:T(2,128)S(1)}) custom-call(s32[1]{0:T(128)} %bitcast.4.count_ref, s32[672]{0:T(1024)S(1)} %select_reduce_fusion.1.place_ref, s32[1344]{0:T(1024)S(1)} %reshape.139.member_ref, s32[1]{0:T(128)} %bitcast.6.turn_ref, ...), custom_call_target="tpu_custom_call" | custom-call | tf_op jit(solution)/shard_map/volume/pallas_call | solution.py:275
  114.2 0.9 copy-done.9
  115.0 36.8 %all_to_all.5.sums_ref = f32[256,2,128]{2,1,0:T(2,128)} all-to-all(f32[256,2,128]{2,1,0:T(2,128)S(1)} %get-tuple-element.26), channel_id=1, replica_groups=mesh['surf'=32,'vol'=8] {'surf','vol'}, dimensions={0} | all-to-all | bytes 524288 | tf_op jit(solution)/shard_map/all_to_all | solution.py:527
  151.8 3.0 %settle.1 = (f32[16,2048]{1,0:T(8,128)}, f32[3,16,128]{2,1,0:T(8,128)}, bf16[16,4096]{1,0:T(8,128)(2,1)}) custom-call(f32[256,2,128]{2,1,0:T(2,128)} %all_to_all.5.sums_ref, f32[16,2048]{1,0:T(8,128)} %v0_ref.1, f32[16,2048]{1,0:T(8,128)} %copy-done.2, f32[16,2048]{1,0:T(8,128)} %copy-done.3, f32[48,4096]{1,0:T(8,128)} %copy-done.9), custom_call_target="tpu_custom_call" | custom-call | tf_op jit(solution)/shard_map/settle/pallas_call | solution.py:357
  156.8 3.7 %collective-permute-start.10 = (bf16[16,4096]{1,0:T(8,128)(2,1)}, bf16[16,4096]{1,0:T(8,128)(2,1)S(1)}, u32[]{:S(2)}, u32[]{:S(2)}) collective-permute-start(bf16[16,4096]{1,0:T(8,128)(2,1)} %get-tuple-element.31), channel_id=1, source_target_pairs={{1,0},{9,8},{17,16},{25,24},{33,32},{41,40},{49,48},{57,56},{65,64... | collective-permute-start | bytes 393224 | tf_op jit(solution)/shard_map/ppermute | solution.py:529
  160.5 2.8 %copy-done.1 = f32[48,32768]{1,0:T(8,128)S(1)} copy-done((f32[48,32768]{1,0:T(8,128)S(1)}, f32[48,32768]{1,0:T(8,128)}, u32[]{:S(2)}) %copy-start.1) | copy-done | bytes 6291480
  164.0 2.3 %combine.1.refs_0_ = f32[16,32768]{1,0:T(8,128)} custom-call(f32[3,16,128]{2,1,0:T(8,128)S(1)} %copy-done.10, f32[48,32768]{1,0:T(8,128)S(1)} %copy-done.1), custom_call_target="tpu_custom_call" | custom-call | tf_op jit(solution)/shard_map/combine/pallas_call | solution.py:378
  167.7 1.1 insert.1
  (102 shorter events, 13.1 us)
Async XLA Ops:
  0.6 15.8 %slice-start = ((f32[3,32768]{1,0:T(4,128)}), f32[3,16384]{1,0:T(4,128)S(1)}, s32[]{:S(2)}) async-start(f32[3,32768]{1,0:T(4,128)} %nodes_ref.3), calls=%async_computation.1 | async-start | bytes 524288 | tf_op jit(solution)/shard_map/slice | solution.py:496
  0.6 15.5 %copy-start.15 = (s32[128,9]{0,1:T(8,128)S(1)}, s32[128,9]{0,1:T(8,128)}, u32[]{:S(2)}) copy-start(s32[128,9]{0,1:T(8,128)} %param.9) | copy-start | bytes 13828
  1.7 16.1 %collective-permute-start = (f32[24,2048]{1,0:T(8,128)S(1)}, f32[24,2048]{1,0:T(8,128)S(1)}, u32[]{:S(2)}, u32[]{:S(2)}) collective-permute-start(f32[24,2048]{1,0:T(8,128)S(1)} %pad_maximum_fusion.1.refs_1_), channel_id=1, source_target_pairs={{0,8},{8,16},{16,24},{24,32},{32,40},{40,48},{48,56},{56,64},{64,7... | collective-permute-start | bytes 589832 | tf_op jit(solution)/shard_map/ppermute | solution.py:477
  10.1 7.7 %collective-permute-start.1 = (f32[24,2048]{1,0:T(8,128)S(1)}, f32[24,2048]{1,0:T(8,128)S(1)}, u32[]{:S(2)}, u32[]{:S(2)}) collective-permute-start(f32[24,2048]{1,0:T(8,128)S(1)} %pad_maximum_fusion.1.refs_1_), channel_id=1, source_target_pairs={{8,0},{16,8},{24,16},{32,24},{40,32},{48,40},{56,48},{64,56},{72,6... | collective-permute-start | bytes 589832 | tf_op jit(solution)/shard_map/ppermute | solution.py:486
  11.4 1.0 copy-start.4
  14.3 1.7 %copy-start = (bf16[128,48,256]{2,1,0:T(8,128)(2,1)}, bf16[128,48,256]{2,1,0:T(8,128)(2,1)S(1)}, u32[]{:S(2)}) copy-start(bf16[128,48,256]{2,1,0:T(8,128)(2,1)S(1)} %prepare_nodes.4.refs_0_) | copy-start | bytes 9437188
  16.0 37.9 %copy-start.8 = (f32[3,2048]{1,0:T(4,128)S(1)}, f32[3,2048]{1,0:T(4,128)}, u32[]{:S(2)}) copy-start(f32[3,2048]{1,0:T(4,128)} %centres_ref.5) | copy-start | bytes 73732
  16.4 38.9 %copy-start.5 = (f32[16,2048]{1,0:T(8,128)S(1)}, f32[16,2048]{1,0:T(8,128)}, u32[]{:S(2)}) copy-start(f32[16,2048]{1,0:T(8,128)} %v0_ref.1) | copy-start | bytes 393220
  24.1 90.0 %copy-start.2 = (f32[16,2048]{1,0:T(8,128)}, f32[16,2048]{1,0:T(8,128)S(1)}, u32[]{:S(2)}) copy-start(f32[16,2048]{1,0:T(8,128)S(1)} %get-tuple-element.22.refs_2_.refs_7_.v1_ref) | copy-start | bytes 393220
  24.1 7.2 %collective-permute-start.2 = (bf16[16,2048]{1,0:T(8,128)(2,1)S(1)}, bf16[16,2048]{1,0:T(8,128)(2,1)S(1)}, u32[]{:S(2)}, u32[]{:S(2)}) collective-permute-start(bf16[16,2048]{1,0:T(8,128)(2,1)S(1)} %convert_element_type.81), channel_id=1, source_target_pairs={{0,8},{8,16},{16,24},{24,32},{32,40},{40,48},{48,56},{56,64},{64,7... | collective-permute-start | bytes 196616 | tf_op jit(solution)/shard_map/ppermute | solution.py:492
  30.1 6.5 %collective-permute-start.7 = (bf16[16,2048]{1,0:T(8,128)(2,1)S(1)}, bf16[16,2048]{1,0:T(8,128)(2,1)S(1)}, u32[]{:S(2)}, u32[]{:S(2)}) collective-permute-start(bf16[16,2048]{1,0:T(8,128)(2,1)S(1)} %convert_element_type.81), channel_id=1, source_target_pairs={{8,0},{16,8},{24,16},{32,24},{40,32},{48,40},{56,48},{64,56},{72,6... | collective-permute-start | bytes 196616 | tf_op jit(solution)/shard_map/ppermute | solution.py:493
  31.4 12.7 %collective-permute-start.4 = (f32[4,4096]{1,0:T(4,128)S(1)}, f32[4,4096]{1,0:T(4,128)S(1)}, u32[]{:S(2)}, u32[]{:S(2)}) collective-permute-start(f32[4,4096]{1,0:T(4,128)S(1)} %get-tuple-element.34), channel_id=1, source_target_pairs={{0,2},{8,10},{16,18},{24,26},{32,34},{40,42},{48,50},{56,58},{64,6... | collective-permute-start | bytes 196616 | tf_op jit(solution)/shard_map/ppermute | solution.py:503
  32.1 19.3 %collective-permute-start.6 = (f32[4,4096]{1,0:T(4,128)S(1)}, f32[4,4096]{1,0:T(4,128)S(1)}, u32[]{:S(2)}, u32[]{:S(2)}) collective-permute-start(f32[4,4096]{1,0:T(4,128)S(1)} %get-tuple-element.35), channel_id=1, source_target_pairs={{0,7},{8,15},{16,23},{24,31},{32,39},{40,47},{48,55},{56,63},{64,7... | collective-permute-start | bytes 196616 | tf_op jit(solution)/shard_map/ppermute | solution.py:503
  32.8 18.6 %collective-permute-start.5 = (f32[4,4096]{1,0:T(4,128)S(1)}, f32[4,4096]{1,0:T(4,128)S(1)}, u32[]{:S(2)}, u32[]{:S(2)}) collective-permute-start(f32[4,4096]{1,0:T(4,128)S(1)} %get-tuple-element.36), channel_id=1, source_target_pairs={{0,6},{8,14},{16,22},{24,30},{32,38},{40,46},{48,54},{56,62},{64,7... | collective-permute-start | bytes 196616 | tf_op jit(solution)/shard_map/ppermute | solution.py:503
  33.4 17.9 %collective-permute-start.3 = (f32[4,4096]{1,0:T(4,128)S(1)}, f32[4,4096]{1,0:T(4,128)S(1)}, u32[]{:S(2)}, u32[]{:S(2)}) collective-permute-start(f32[4,4096]{1,0:T(4,128)S(1)} %get-tuple-element.37), channel_id=1, source_target_pairs={{0,1},{8,9},{16,17},{24,25},{32,33},{40,41},{48,49},{56,57},{64,65... | collective-permute-start | bytes 196616 | tf_op jit(solution)/shard_map/ppermute | solution.py:503
  42.7 71.4 %copy-start.3 = (f32[16,2048]{1,0:T(8,128)}, f32[16,2048]{1,0:T(8,128)S(1)}, u32[]{:S(2)}) copy-start(f32[16,2048]{1,0:T(8,128)S(1)} %operator.3.refs_8_.v2_ref) | copy-start | bytes 393220
  42.8 12.5 %collective-permute-start.9 = (bf16[16,2048]{1,0:T(8,128)(2,1)S(1)}, bf16[16,2048]{1,0:T(8,128)(2,1)S(1)}, u32[]{:S(2)}, u32[]{:S(2)}) collective-permute-start(bf16[16,2048]{1,0:T(8,128)(2,1)S(1)} %convert_element_type.87), channel_id=1, source_target_pairs={{8,0},{16,8},{24,16},{32,24},{40,32},{48,40},{56,48},{64,56},{72,6... | collective-permute-start | bytes 196616 | tf_op jit(solution)/shard_map/ppermute | solution.py:508
  44.1 11.2 %collective-permute-start.8 = (bf16[16,2048]{1,0:T(8,128)(2,1)S(1)}, bf16[16,2048]{1,0:T(8,128)(2,1)S(1)}, u32[]{:S(2)}, u32[]{:S(2)}) collective-permute-start(bf16[16,2048]{1,0:T(8,128)(2,1)S(1)} %convert_element_type.87), channel_id=1, source_target_pairs={{0,8},{8,16},{16,24},{24,32},{32,40},{40,48},{48,56},{56,64},{64,7... | collective-permute-start | bytes 196616 | tf_op jit(solution)/shard_map/ppermute | solution.py:507
  114.2 0.9 copy-start.9
  154.8 11.5 %collective-permute-start.13 = (bf16[16,4096]{1,0:T(8,128)(2,1)}, bf16[16,4096]{1,0:T(8,128)(2,1)S(1)}, u32[]{:S(2)}, u32[]{:S(2)}) collective-permute-start(bf16[16,4096]{1,0:T(8,128)(2,1)} %get-tuple-element.31), channel_id=1, source_target_pairs={{7,0},{15,8},{23,16},{31,24},{39,32},{47,40},{55,48},{63,56},{71,6... | collective-permute-start | bytes 393224 | tf_op jit(solution)/shard_map/ppermute | solution.py:529
  155.4 10.8 %collective-permute-start.12 = (bf16[16,4096]{1,0:T(8,128)(2,1)}, bf16[16,4096]{1,0:T(8,128)(2,1)S(1)}, u32[]{:S(2)}, u32[]{:S(2)}) collective-permute-start(bf16[16,4096]{1,0:T(8,128)(2,1)} %get-tuple-element.31), channel_id=1, source_target_pairs={{6,0},{14,8},{22,16},{30,24},{38,32},{46,40},{54,48},{62,56},{70,6... | collective-permute-start | bytes 393224 | tf_op jit(solution)/shard_map/ppermute | solution.py:529
  156.1 10.2 %collective-permute-start.11 = (bf16[16,4096]{1,0:T(8,128)(2,1)}, bf16[16,4096]{1,0:T(8,128)(2,1)S(1)}, u32[]{:S(2)}, u32[]{:S(2)}) collective-permute-start(bf16[16,4096]{1,0:T(8,128)(2,1)} %get-tuple-element.31), channel_id=1, source_target_pairs={{2,0},{10,8},{18,16},{26,24},{34,32},{42,40},{50,48},{58,56},{66,6... | collective-permute-start | bytes 393224 | tf_op jit(solution)/shard_map/ppermute | solution.py:529
  156.8 9.5 %collective-permute-start.10 = (bf16[16,4096]{1,0:T(8,128)(2,1)}, bf16[16,4096]{1,0:T(8,128)(2,1)S(1)}, u32[]{:S(2)}, u32[]{:S(2)}) collective-permute-start(bf16[16,4096]{1,0:T(8,128)(2,1)} %get-tuple-element.31), channel_id=1, source_target_pairs={{1,0},{9,8},{17,16},{25,24},{33,32},{41,40},{49,48},{57,56},{65,64... | collective-permute-start | bytes 393224 | tf_op jit(solution)/shard_map/ppermute | solution.py:529
  160.5 2.8 %copy-start.1 = (f32[48,32768]{1,0:T(8,128)S(1)}, f32[48,32768]{1,0:T(8,128)}, u32[]{:S(2)}) copy-start(f32[48,32768]{1,0:T(8,128)} %get-tuple-element.30.image_ref) | copy-start | bytes 18874372
  (7 other events, 5.0 us)
